TPU v7x, 256 devices: a whole 4x4x8 slice. The times are simulated.
256 devices in a mesh: dp: 2 (over core), tensor: 8 (over z), context: 16 (over y, x).
Axes of the slice: x: 4, y: 4, z: 8, core: 2. Of those that a mesh axis runs over, the one named last changes fastest.
Arguments:
- x_raw: bfloat16 [8192, 8192], P(('dp', 'context'), 'tensor'), parts along dimension 0, may hold values from -6 to 6
- b_raw: bfloat16 [8192, 1024], P(('dp', 'context'), 'tensor'), parts along dimension 0, may hold values from -6 to 6
- c_raw: bfloat16 [8192, 1024], P(('dp', 'context'), 'tensor'), parts along dimension 0, may hold values from -6 to 6
- dt_raw: bfloat16 [128, 8192], P('tensor', ('dp', 'context')), parts along dimension 1, may hold values from -3.5 to 12
- dt_bias: float32 [128], P('tensor'), may hold values from -8 to -7
- a_log: float32 [128], P('tensor'), may hold values from -4.5 to 4.5
- skip_gain: float32 [128], P('tensor'), may hold values from 0.5 to 1.5
- conv_x: float32 [4, 8192], P(None, 'tensor'), may hold values from -2 to 2
- conv_b: float32 [4, 1024], P(None, 'tensor'), may hold values from -2 to 2
- conv_c: float32 [4, 1024], P(None, 'tensor'), may hold values from -2 to 2
- grad_y: bfloat16 [8192, 8192], P(('dp', 'context'), 'tensor'), parts along dimension 0, may hold values from -6 to 6
Outputs:
- y_out: float32 [8192, 8192], P(('dp', 'context'), 'tensor'), parts along dimension 0
- grad_x: float32 [8192, 8192], P(('dp', 'context'), 'tensor'), parts along dimension 0
- grad_b: float32 [8192, 1024], P(('dp', 'context'), 'tensor'), parts along dimension 0
- grad_c: float32 [8192, 1024], P(('dp', 'context'), 'tensor'), parts along dimension 0
- grad_dt: float32 [128, 8192], P('tensor', ('dp', 'context')), parts along dimension 1
There are 2 independent parts, one for each index of `dp`. A program takes and returns all parts, laid end to end along the dimension named above; an argument that names none is the same for every part. Nothing has to cross between parts.
All inputs are finite; a program needn't handle non-finite values.
Results may differ from a plain program's by a relative error of at most 0.0003.
Values may be sent and summed in bfloat16 or wider, within the bound.
No kernel may reach another device: no remote copies, remote signals or barrier semaphores. Data moves between devices by JAX's collectives and lax.ppermute only.
A program may use at most 64 MiB of HBM per device.

v0:
```python
import jax
import jax.numpy as jnp
from jax import lax
from jax.sharding import PartitionSpec as P

STATE = 128
SPAN = 256


precise = lax.Precision.HIGHEST


def from_behind(block, axis, distance):
    devices = range(lax.axis_size(axis))
    route = [(i - distance, i) for i in devices if i - distance in devices]
    return lax.ppermute(block, axis, route)


def prefix(value, axis, combine, identity, reverse):
    count, here = (lax.axis_size(axis), lax.axis_index(axis))
    everything = jax.tree.map(lambda part: lax.all_gather(part, axis), value)
    start = jax.tree.map(
        lambda part, zero: jnp.broadcast_to(jnp.asarray(zero, part.dtype), part.shape),
        value,
        identity,
    )

    def lap(k, before):
        at = count - 1 - k if reverse else k
        reached = at > here if reverse else at < here
        new = combine(before, jax.tree.map(lambda part: part[at], everything))
        return jax.tree.map(lambda a, b: jnp.where(reached, a, b), new, before)

    return lax.fori_loop(0, count, lap, start)


def conv_silu(padded, taps):
    length = padded.shape[0] - taps.shape[0] + 1
    total = padded[0:length] * taps[0]
    for offset in range(1, taps.shape[0]):
        total = total + padded[offset : offset + length] * taps[offset]
    return jax.nn.silu(total)


def span_step(running, inputs):
    x_block, b_block, c_block, a_block, dt_block = inputs
    block_size = a_block.shape[1]
    head_count = x_block.shape[1]
    head_size = x_block.shape[2]
    group_count = b_block.shape[1]
    per_group = head_count // group_count
    state_size = b_block.shape[2]
    cumulative = jnp.cumsum(a_block, axis=1)
    position = jnp.arange(block_size)
    causal = position[:, None] >= position[None, :]
    exponent = jnp.where(causal[None], cumulative[:, :, None] - cumulative[:, None, :], 0.0)
    decay = jnp.where(causal[None], jnp.exp(exponent), 0.0)
    scores = jnp.einsum("ign,jgn->gij", c_block, b_block, precision=precise)
    mixing = (
        scores[:, None]
        * decay.reshape(group_count, per_group, block_size, block_size)
        * dt_block.reshape(group_count, per_group, 1, block_size)
    )
    x_group = x_block.reshape(block_size, group_count, per_group, head_size)
    inside = jnp.einsum("gkij,jgkp->igkp", mixing, x_group, precision=precise).reshape(
        block_size, head_count, head_size
    )
    state_group = running.reshape(group_count, per_group, head_size, state_size)
    entering = jnp.einsum("ign,gkpn->igkp", c_block, state_group, precision=precise).reshape(
        block_size, head_count, head_size
    )
    entering = entering * jnp.exp(cumulative).T[:, :, None]
    to_end = jnp.exp(cumulative[:, -1:] - cumulative) * dt_block
    written = jnp.einsum(
        "jgkp,gkj,jgn->gkpn",
        x_group,
        to_end.reshape(group_count, per_group, block_size),
        b_block,
        precision=precise,
    )
    written = written.reshape(head_count, head_size, state_size)
    return (jnp.exp(cumulative[:, -1])[:, None, None] * running + written, inside + entering)


def spanned(x_heads, b_conv, c_conv, log_decay, step_size, running):
    length = x_heads.shape[0]
    blocks = length // SPAN
    head_count = x_heads.shape[1]
    group_count = b_conv.shape[1] // STATE
    x_blocks = x_heads.reshape(blocks, SPAN, head_count, x_heads.shape[2])
    b_blocks = b_conv.reshape(blocks, SPAN, group_count, STATE)
    c_blocks = c_conv.reshape(blocks, SPAN, group_count, STATE)
    a_blocks = log_decay.reshape(head_count, blocks, SPAN).transpose(1, 0, 2)
    dt_blocks = step_size.reshape(head_count, blocks, SPAN).transpose(1, 0, 2)
    final_state, outputs = lax.scan(
        span_step, running, (x_blocks, b_blocks, c_blocks, a_blocks, dt_blocks)
    )
    return (outputs.reshape(length, head_count, x_heads.shape[2]), final_state)


def combine(earlier, later):
    return (earlier[0] + later[0], jnp.exp(later[0])[:, None, None] * earlier[1] + later[1])


def carry_term(c_conv, cumulative, entering_state):
    rows = c_conv.shape[0]
    head_count = entering_state.shape[0]
    head_size = entering_state.shape[1]
    group_count = c_conv.shape[1] // STATE
    per_group = head_count // group_count
    product = jnp.einsum(
        "tgn,gkpn->tgkp",
        c_conv.reshape(rows, group_count, STATE),
        entering_state.reshape(group_count, per_group, head_size, STATE),
        precision=precise,
    )
    product = product.reshape(rows, head_count, head_size)
    return product * jnp.exp(cumulative).T[:, :, None]


def on_device(
    x_raw, b_raw, c_raw, dt_raw, dt_bias, a_log, skip_gain, conv_x, conv_b, conv_c, grad_y
):
    row_count = x_raw.shape[0]
    feature_width = x_raw.shape[1]
    heads_here = dt_raw.shape[0]
    head_size = feature_width // heads_here
    proj_width = b_raw.shape[1]
    rim_rows = conv_x.shape[0] - 1
    first_kept = row_count - rim_rows
    edge_rows = jnp.concatenate(
        [x_raw[first_kept:], b_raw[first_kept:], c_raw[first_kept:]], axis=1
    )
    before = from_behind(edge_rows, "context", 1)
    ext_x = jnp.concatenate([before[:, :feature_width], x_raw], axis=0).astype(jnp.float32)
    ext_b = jnp.concatenate(
        [before[:, feature_width : feature_width + proj_width], b_raw], axis=0
    ).astype(jnp.float32)
    ext_c = jnp.concatenate([before[:, feature_width + proj_width :], c_raw], axis=0).astype(
        jnp.float32
    )

    def local_pass(x_float, b_float, c_float, dt_float):
        x_conv = conv_silu(x_float, conv_x)
        b_conv = conv_silu(b_float, conv_b)
        c_conv = conv_silu(c_float, conv_c)
        step_size = jax.nn.softplus(dt_float + dt_bias[:, None])
        log_decay = -jnp.exp(a_log)[:, None] * step_size
        x_heads = x_conv.reshape(row_count, heads_here, head_size)
        start_state = jnp.zeros((heads_here, head_size, STATE), jnp.float32)
        y_heads, final_state = spanned(x_heads, b_conv, c_conv, log_decay, step_size, start_state)
        y_heads = y_heads + skip_gain[None, :, None] * x_heads
        return (
            y_heads.reshape(row_count, feature_width),
            final_state,
            c_conv,
            jnp.cumsum(log_decay, axis=1),
        )

    primal, pullback = jax.vjp(local_pass, ext_x, ext_b, ext_c, dt_raw.astype(jnp.float32))
    y_local, shard_state, c_conv, cumulative = primal
    shard_decay = cumulative[:, -1]
    zero_state = jnp.zeros_like(shard_state)
    identity = (jnp.zeros_like(shard_decay), zero_state)
    entering = prefix((shard_decay, shard_state), "context", combine, identity, False)[1]
    carried, carry_pull = jax.vjp(carry_term, c_conv, cumulative, entering)
    y_out = y_local + carried.reshape(row_count, feature_width)
    upstream = grad_y.astype(jnp.float32)
    d_conv, d_cumulative, leaving = carry_pull(upstream.reshape(row_count, heads_here, head_size))
    later = prefix((shard_decay, leaving), "context", combine, identity, True)[1]
    decay_grad = jnp.exp(shard_decay) * jnp.sum(later * entering, axis=(1, 2))
    d_cumulative = d_cumulative.at[:, -1].add(decay_grad)
    grad_xe, grad_be, grad_ce, grad_dt = pullback((upstream, later, d_conv, d_cumulative))
    edge_grads = jnp.concatenate(
        [grad_xe[:rim_rows], grad_be[:rim_rows], grad_ce[:rim_rows]], axis=1
    )
    from_next = from_behind(edge_grads, "context", -1)

    def settle(extended, received):
        return jnp.concatenate(
            [extended[rim_rows:row_count], extended[row_count:] + received], axis=0
        )

    grad_x = settle(grad_xe, from_next[:, :feature_width])
    grad_b = settle(grad_be, from_next[:, feature_width : feature_width + proj_width])
    grad_c = settle(grad_ce, from_next[:, feature_width + proj_width :])
    return (y_out, grad_x, grad_b, grad_c, grad_dt)


def solution(mesh):
    return jax.shard_map(
        on_device,
        mesh=mesh,
        in_specs=(
            P(("dp", "context"), "tensor"),
            P(("dp", "context"), "tensor"),
            P(("dp", "context"), "tensor"),
            P("tensor", ("dp", "context")),
            P("tensor"),
            P("tensor"),
            P("tensor"),
            P(None, "tensor"),
            P(None, "tensor"),
            P(None, "tensor"),
            P(("dp", "context"), "tensor"),
        ),
        out_specs=(
            P(("dp", "context"), "tensor"),
            P(("dp", "context"), "tensor"),
            P(("dp", "context"), "tensor"),
            P(("dp", "context"), "tensor"),
            P("tensor", ("dp", "context")),
        ),
        check_vma=False,
    )
```

profile of v0, /device:TPU:38, one launch (start us, length us, event | category | flops | bytes accessed | tf_op | source)
XLA Modules:
  0.0 298.6 jit_solution(7090270863106617675)
XLA Ops:
  9.6 3.4 %collective-permute-start = (bf16[3,1280]{0,1:T(8,128)(2,1)S(1)}, bf16[3,1280]{0,1:T(8,128)(2,1)S(1)}, u32[]{:S(2)}, u32[]{:S(2)}) collective-permute-start(bf16[3,1280]{0,1:T(8,128)(2,1)S(1)} %copy.142), channel_id=1, source_target_pairs={{0,1},{1,2},{2,3},{3,4},{4,5},{5,6},{6,7},{7,8},{8,9},{9,10},{10,1... | collective-permute-start | bytes 23048 | tf_op jit(solution)/shard_map/ppermute | solution.py:16
  19.5 1.5 collective-permute-done
  21.3 1.8 fusion.45
  26.3 32.9 %all-reduce.14 = f32[256]{0:T(256)S(1)} all-reduce(f32[256]{0:T(256)S(1)} %dynamic-update-slice.3), channel_id=2, replica_groups=mesh['dp'=2,'tensor'=8,'context'=16] {'context'}, use_global_device_ids=true, to_apply=%add.14 | all-reduce | flops 256 | bytes 2048
  60.6 41.3 %all-gather.8.cloned.1.call-done = f32[256,64,128]{2,1,0:T(8,128)} async-done(((f32[16,64,128]{2,1,0:T(8,128)}), f32[256,64,128]{2,1,0:T(8,128)}) %all-gather.8.cloned.1.call-update) | async-done | bytes 8388624 | tf_op jit(solution)/shard_map/all_gather | solution.py:21
  101.9 30.2 %while.26 = (s32[]{:T(128)}, f32[16,64,128]{2,1,0:T(8,128)S(1)}, s32[]{:T(128)}, f32[16,16]{1,0:T(8,128)}, f32[16,16,64,128]{3,2,1,0:T(8,128)}, /*index=5*/s32[]{:T(128)}, s32[]{:T(128)}, s32[]{:T(128)}, s32[]{:T(128)}) while((s32[]{:T(128)}, f32[16,64,128]{2,1,0:T(8,128)S(1)}, s32[]{:T(128)}, f32[16,16]{1,0:T(8,128)}, ...), condition=%wide.region_5.6_spmd.clone, body=%wide.region_4.5_spmd.clone.sunk | while | flops 524296 | bytes 1573223 | solution.py:34
  132.2 2.5 multiply_reduce_fusion.1
  136.0 1.8 convolution_add_fusion
  138.6 1.4 convolution_bitcast_fusion.2
  141.5 6.8 %fusion.11 = (f32[16,256]{1,0:T(8,128)}, f32[16,256]{1,0:T(8,128)}, f32[16,256]{1,0:T(8,128)}, f32[256,256]{1,0:T(8,128)S(1)}) fusion(f32[16,256]{1,0:T(8,128)S(1)} %get-tuple-element.715, f32[16,256]{1,0:T(8,128)S(1)} %copy_bitcast_fusion, f32[256,256]{1,0:T(8,128)S(1)} %fusion.99, pred[256,256]{1,0:T(8,128)(4,1)S(1)} %iota_compare_fusion, ...), kind=kOutput, calls=%fused_computation.18 | convolution fusion | flops 820957184 | bytes 2244608 | tf_op jit(solution)/shard_map/transpose(jvp())/while/body/eval_jaxpr/gkij,jgkp->igkp/dot_general | solution.py:65
  152.0 1.5 copy.160
  153.5 7.4 %fusion.8 = f32[16,64,256]{2,1,0:T(8,128)} fusion(f32[256,16,64]{0,2,1:T(8,128)} %bitcast.263, f32[16,256]{1,0:T(8,128)} %copy-done.32, f32[16,256]{1,0:T(8,128)} %copy-done.22, f32[256,256]{1,0:T(8,128)} %copy-done.46, pred[256,256]{1,0:T(8,128)(4,1)} %copy-done.20), kind=kOutput, calls=%fused_computation.16 | convolution fusion | flops 810549248 | bytes 2457600 | tf_op jit(solution)/shard_map/jvp()/while/body/eval_jaxpr/gkij,jgkp->igkp/dot_general | solution.py:65
  161.0 3.9 %fusion.27 = f32[256,1,16,64]{0,3,2,1:T(8,128)} fusion(bf16[16,64,256]{2,1,0:T(8,128)(2,1)S(1)} %bitcast.266, f32[16,256]{1,0:T(8,128)S(1)} %copy-done.33, f32[16,256]{1,0:T(8,128)S(1)} %copy-done.23, f32[256,256]{1,0:T(8,128)S(1)} %copy-done.47, pred[256,256]{1,0:T(8,128)(4,1)S(1)} %copy-done.21, f32[16,256,64]{1,2,0:T(8,128)S(1)} %copy-done.12, ...), kind=kOutput, calls=%fused_computation.37 | convolution fusion | flops 811073536 | bytes 2998272 | tf_op jit(solution)/shard_map/transpose(jvp())/while/body/eval_jaxpr/gkij,jgkp->igkp/dot_general | solution.py:65
  164.9 48.6 %all-gather.6.cloned.1.call-done = f32[256,64,128]{2,1,0:T(8,128)} async-done(((f32[16,64,128]{2,1,0:T(8,128)}), f32[256,64,128]{2,1,0:T(8,128)}) %all-gather.6.cloned.1.call-update) | async-done | bytes 8388624 | tf_op jit(solution)/shard_map/all_gather | solution.py:21
  213.4 38.3 %while.25 = (s32[]{:T(128)}, f32[16,64,128]{2,1,0:T(8,128)S(1)}, s32[]{:T(128)}, f32[16,16]{1,0:T(8,128)}, f32[16,16,64,128]{3,2,1,0:T(8,128)}, /*index=5*/s32[]{:T(128)}, s32[]{:T(128)}) while((s32[]{:T(128)}, f32[16,64,128]{2,1,0:T(8,128)S(1)}, s32[]{:T(128)}, f32[16,16]{1,0:T(8,128)}, f32[16,16,64,128]{3,2,1,0:T(8,128)}, ...), condition=%wide.region_3.4_spmd.clone, body=%wide.region_2.3_spmd.clone.sunk | while | flops 524292 | bytes 1573161 | solution.py:34
  252.5 2.5 convolution_bitcast_fusion.3
  254.9 1.4 copy.165
  257.6 3.7 %fusion.42 = (f32[256,16]{0,1:T(8,128)S(1)}, f32[256,16]{0,1:T(8,128)}, f32[16,64,256]{2,1,0:T(8,128)}) fusion(f32[16,64,256]{2,1,0:T(8,128)S(1)} %fusion.59, f32[16,64,128]{2,1,0:T(8,128)S(1)} %get-tuple-element.596, f32[256,128]{0,1:T(8,128)S(1)} %fusion.68, bf16[256,1024]{0,1:T(8,128)(2,1)} %copy-done.6), kind=kOutput, calls=%fused_computation.63 | convolution fusion | flops 404086784 | bytes 3309568 | tf_op jit(solution)/shard_map/jvp(tgn,gkpn->tgkp)/dot_general | solution.py:111
  263.0 2.7 reduce-window.44
  267.3 2.5 reduce-window.46
  270.5 3.6 %broadcast_multiply_fusion = (f32[256,1024]{0,1:T(8,128)S(1)}, f32[256,1024]{0,1:T(8,128)S(1)}, f32[256,1024]{0,1:T(8,128)}) fusion(f32[1024]{0:T(1024)} %bitcast.270, f32[256,1024]{0,1:T(8,128)S(1)} %copy-done.5, f32[256,1,16,64]{0,3,2,1:T(8,128)} %fusion.27, bf16[256,1024]{0,1:T(8,128)(2,1)S(1)} %copy-done.8, f32[1024]{0:T(1024)} %mul.671, ...), kind=kLoop, calls=%fused_computation.86 | loop fusion | flops 5242880 | bytes 8937472 | tf_op jit(solution)/shard_map/transpose(jvp())/mul | solution.py:41
  276.8 1.5 broadcast_multiply_fusion.8
  279.4 2.7 collective-permute-start.1
  282.1 1.5 fusion.83
  (251 shorter events, 105.5 us)
Async XLA Ops:
  7.2 17.3 %copy-start.44 = (u32[256]{0:T(256)S(1)}, u32[256]{0:T(256)}, u32[]{:S(2)}) copy-start(u32[256]{0:T(256)} %constant.275) | copy-start | bytes 3076
  7.2 52.7 %copy-start.42 = (f32[4,128]{1,0:T(4,128)S(1)}, f32[4,128]{1,0:T(4,128)}, u32[]{:S(2)}) copy-start(f32[4,128]{1,0:T(4,128)} %param.25) | copy-start | bytes 6148
  7.2 52.7 %copy-start.34 = (f32[4,1024]{1,0:T(4,128)S(1)}, f32[4,1024]{1,0:T(4,128)}, u32[]{:S(2)}) copy-start(f32[4,1024]{1,0:T(4,128)} %param.24) | copy-start | bytes 49156
  7.2 94.7 %all-gather.8.cloned.1.call-start = ((), (), s32[]{:S(2)}) async-start(), calls=%async_computation.1 | async-start | bytes 8912896 | tf_op jit(solution)/shard_map/all_gather | solution.py:21
  9.6 11.3 %collective-permute-start = (bf16[3,1280]{0,1:T(8,128)(2,1)S(1)}, bf16[3,1280]{0,1:T(8,128)(2,1)S(1)}, u32[]{:S(2)}, u32[]{:S(2)}) collective-permute-start(bf16[3,1280]{0,1:T(8,128)(2,1)S(1)} %copy.142), channel_id=1, source_target_pairs={{0,1},{1,2},{2,3},{3,4},{4,5},{5,6},{6,7},{7,8},{8,9},{9,10},{10,1... | collective-permute-start | bytes 23048 | tf_op jit(solution)/shard_map/ppermute | solution.py:16
  13.7 46.2 %copy-start.37 = (f32[16]{0:T(128)}, f32[16]{0:T(128)S(1)}, u32[]{:S(2)}) copy-start(f32[16]{0:T(128)S(1)} %exponential_negate_fusion) | copy-start | bytes 196
  15.3 119.4 %copy-start.24 = (f32[16,2]{0,1:T(2,128)}, f32[16,2]{0,1:T(2,128)S(1)}, u32[]{:S(2)}) copy-start(f32[16,2]{0,1:T(2,128)S(1)} %slice.214) | copy-start | bytes 388
  15.4 123.2 %copy-start.13 = (f32[256,16]{0,1:T(8,128)}, f32[256,16]{0,1:T(8,128)S(1)}, u32[]{:S(2)}) copy-start(f32[256,16]{0,1:T(8,128)S(1)} %exponential_bitcast_fusion.2) | copy-start | bytes 49156
  16.2 43.7 %copy-start.38 = (f32[128]{0:T(128)}, f32[128]{0:T(128)S(1)}, u32[]{:S(2)}) copy-start(f32[128]{0:T(128)S(1)} %get-tuple-element.720) | copy-start | bytes 1540
  16.2 43.7 %copy-start.39 = (f32[128]{0:T(128)}, f32[128]{0:T(128)S(1)}, u32[]{:S(2)}) copy-start(f32[128]{0:T(128)S(1)} %get-tuple-element.721) | copy-start | bytes 1540
  16.2 43.7 %copy-start.40 = (f32[128]{0:T(128)}, f32[128]{0:T(128)S(1)}, u32[]{:S(2)}) copy-start(f32[128]{0:T(128)S(1)} %get-tuple-element.722) | copy-start | bytes 1540
  16.2 43.7 %copy-start.41 = (f32[128]{0:T(128)}, f32[128]{0:T(128)S(1)}, u32[]{:S(2)}) copy-start(f32[128]{0:T(128)S(1)} %get-tuple-element.723) | copy-start | bytes 1540
  23.2 190.3 %all-gather.6.cloned.1.call-start = ((), (), s32[]{:S(2)}) async-start(), calls=%async_computation | async-start | bytes 8912896 | tf_op jit(solution)/shard_map/all_gather | solution.py:21
  25.8 115.7 %copy-start.22 = (f32[16,256]{1,0:T(8,128)}, f32[16,256]{1,0:T(8,128)S(1)}, u32[]{:S(2)}) copy-start(f32[16,256]{1,0:T(8,128)S(1)} %copy_bitcast_fusion) | copy-start | bytes 49156
  26.0 108.7 %copy-start.36 = (f32[16]{0:T(128)}, f32[16]{0:T(128)S(1)}, u32[]{:S(2)}) copy-start(f32[16]{0:T(128)S(1)} %slice_reduce_fusion.3) | copy-start | bytes 196
  59.9 72.2 %copy-start.25 = (f32[1,1024]{1,0:T(1,128)}, f32[1,1024]{1,0:T(1,128)S(1)}, u32[]{:S(2)}) copy-start(f32[1,1024]{1,0:T(1,128)S(1)} %get-tuple-element.713) | copy-start | bytes 12292
  59.9 72.2 %copy-start.26 = (f32[1,1024]{1,0:T(1,128)}, f32[1,1024]{1,0:T(1,128)S(1)}, u32[]{:S(2)}) copy-start(f32[1,1024]{1,0:T(1,128)S(1)} %get-tuple-element.711) | copy-start | bytes 12292
  59.9 72.2 %copy-start.28 = (f32[1,1024]{1,0:T(1,128)}, f32[1,1024]{1,0:T(1,128)S(1)}, u32[]{:S(2)}) copy-start(f32[1,1024]{1,0:T(1,128)S(1)} %get-tuple-element.712) | copy-start | bytes 12292
  60.0 72.2 %copy-start.30 = (f32[1,1024]{1,0:T(1,128)}, f32[1,1024]{1,0:T(1,128)S(1)}, u32[]{:S(2)}) copy-start(f32[1,1024]{1,0:T(1,128)S(1)} %get-tuple-element.714) | copy-start | bytes 12292
  135.4 12.8 %copy-start.32 = (f32[16,256]{1,0:T(8,128)}, f32[16,256]{1,0:T(8,128)S(1)}, u32[]{:S(2)}) copy-start(f32[16,256]{1,0:T(8,128)S(1)} %get-tuple-element.715) | copy-start | bytes 49156
  135.4 13.2 %copy-start.15 = (f32[16,256]{1,0:T(8,128)}, f32[16,256]{1,0:T(8,128)S(1)}, u32[]{:S(2)}) copy-start(f32[16,256]{1,0:T(8,128)S(1)} %get-tuple-element.706) | copy-start | bytes 49156
  252.5 18.0 %copy-start.8 = (bf16[256,1024]{0,1:T(8,128)(2,1)S(1)}, bf16[256,1024]{0,1:T(8,128)(2,1)}, u32[]{:S(2)}) copy-start(bf16[256,1024]{0,1:T(8,128)(2,1)} %copy-done.6) | copy-start | bytes 1572868
  254.9 15.6 %copy-start.5 = (f32[256,1024]{0,1:T(8,128)S(1)}, f32[256,1024]{0,1:T(8,128)}, u32[]{:S(2)}) copy-start(f32[256,1024]{0,1:T(8,128)} %copy-done.4) | copy-start | bytes 3145732
  279.4 7.8 %collective-permute-start.1 = (f32[3,1280]{1,0:T(4,128)S(1)}, f32[3,1280]{1,0:T(4,128)S(1)}, u32[]{:S(2)}, u32[]{:S(2)}) collective-permute-start(f32[3,1280]{1,0:T(4,128)S(1)} %pad_maximum_fusion.3), channel_id=1, source_target_pairs={{1,0},{2,1},{3,2},{4,3},{5,4},{6,5},{7,6},{8,7},{9,8},{10,9},{11,1... | collective-permute-start | bytes 46088 | tf_op jit(solution)/shard_map/ppermute | solution.py:16
  (28 other events, 145.1 us)
Sparse Core Ops, SparseCore 0:
  23.3 78.5 all-gather.7
  137.9 75.4 all-gather.5
where the time goes:
time: 303 us; the launch traced here: 299 us
  waiting for transfers between devices  92.1 us (30%)
  other arithmetic  59.7 us (20%)
  local copies, waits for them, and re-layouts  55.5 us (18%)
  matrix products  36.1 us (12%)
  blocking collectives  32.9 us (11%)
  between operations  15.5 us (5%)
  starting transfers between devices  6.22 us (2%)
    all_gather x2, waiting for transfers between devices, prefix(): everything = jax.tree.map(lambda part: lax.all_gather(part, axis), value)  89.8 us
    select_n x32, other arithmetic, lap(): return jax.tree.map(lambda a, b: jnp.where(reached, a, b), new, before)  37.5 us
    unnamed x1, blocking collectives  32.9 us
    exp x32, local copies, waits for them, and re-layouts, combine(): jnp.exp(later[0])[:, None, None] * earlier[1] + later[1]  30.3 us
    dot_general x3, matrix products, span_step(): jnp.einsum('gkij,jgkp->igkp', mixing, x_group, precision=precise)  18.1 us
    unnamed x107, local copies, waits for them, and re-layouts  9.78 us
    dot_general x3, matrix products, carry_term(): jnp.einsum('tgn,gkpn->tgkp', c_conv.reshape(rows, group_count, STATE), en...  7.97 us
    another operation x8, other arithmetic  7.63 us
  transfers between devices with their start and end apart: 4, of which 4 were waited for; matrix products, arithmetic and copies ran while one was open for 14% of the time, Pallas kernels for 0%

commit v1 on v0

v1 whole, which is shorter than its diff:
```python
import functools

import jax
import jax.numpy as jnp
from jax import lax
from jax.experimental import pallas as pl
from jax.experimental.pallas import tpu as pltpu
from jax.sharding import PartitionSpec as P

f32 = jnp.float32
bf16 = jnp.bfloat16

TOKENS = 256
SUB = 128
HEADS = 16
HEAD_DIM = 64
STATE = 128
WIDTH = HEADS * HEAD_DIM
PAIRS = HEADS // 2
RIM = 3
RANKS = 16
CHUNK = 144
NEG = -1e30
CODE_SPAN = 200.0

NN = ((1,), (0,))
NT = ((1,), (1,))
TN = ((0,), (0,))


def dot(a, b, dims=NN):
    return lax.dot_general(a, b, (dims, ((), ())), preferred_element_type=f32)


def split2(v):
    hi = v.astype(bf16)
    return hi, (v - hi.astype(f32)).astype(bf16)


def split3(v):
    hi = v.astype(bf16)
    rest = v - hi.astype(f32)
    mid = rest.astype(bf16)
    return hi, mid, (rest - mid.astype(f32)).astype(bf16)


def dot3(a, b, dims=NN):
    return dot(a[0], b[0], dims) + dot(a[1], b[0], dims) + dot(a[0], b[1], dims)


def iota(shape, axis):
    return lax.broadcasted_iota(jnp.int32, shape, axis)


def onehot(mask):
    return jnp.where(mask, 1.0, 0.0).astype(bf16)


def to_column(row):
    n = row.shape[1]
    eye = iota((n, n), 0) == iota((n, n), 1)
    return jnp.sum(jnp.where(eye, row, 0.0), axis=1, keepdims=True)


def low_half(shape):
    return iota(shape, 1) < HEAD_DIM


def swap_halves(v):
    return pltpu.roll(v, HEAD_DIM, 1)


def encode(v):
    top = jnp.max(jnp.abs(v), axis=0, keepdims=True)
    scale = (jnp.maximum(top, 1e-30) * 1.01).astype(bf16).astype(f32)
    unit = jnp.abs(v) * (CODE_SPAN / scale)
    size = jnp.exp2(unit - CODE_SPAN / 2)
    return jnp.where(v < 0, -size, size).astype(bf16), scale


def decode(code, scale):
    v = code.astype(f32)
    unit = jnp.log2(jnp.abs(v)) + CODE_SPAN / 2
    size = unit * (scale * (1.0 / CODE_SPAN))
    return jnp.where(v < 0, -size, size)


def split_heads(pair):
    top, bottom = pair[:HEAD_DIM], pair[HEAD_DIM:]
    low = low_half(top.shape)
    return (
        jnp.where(low, top, swap_halves(bottom)),
        jnp.where(low, swap_halves(top), bottom),
    )


def join_heads(first, second):
    low = low_half(first.shape)
    return (
        jnp.where(low, first, swap_halves(second)),
        jnp.where(low, swap_halves(first), second),
    )


def transpose_rows(arrays):
    rows = sum(a.shape[0] for a in arrays)
    pad = jnp.zeros((128 - rows, TOKENS), f32)
    return split3(jnp.concatenate(list(arrays) + [pad], axis=0).T)


def spread(parts, which, first_head, lanes_per_head, lanes):
    shape = (128, lanes)
    hot = onehot(iota(shape, 0) == which * HEADS + first_head + iota(shape, 1) // lanes_per_head)
    return dot(parts[0], hot) + dot(parts[1], hot) + dot(parts[2], hot)


def decay_terms(cum, step):
    first = iota(cum.shape, 1) < SUB
    end0 = cum[:, SUB - 1 : SUB]
    end1 = cum[:, TOKENS - 1 : TOKENS]
    inner = jnp.exp(cum)
    outer = jnp.exp(jnp.where(first, end0, end1) - cum) * step
    from_start = jnp.where(first, inner, inner * jnp.exp(end0))
    to_end = jnp.where(first, outer * jnp.exp(end1), outer)
    return inner, outer, from_start, to_end, end0 + end1


def enter_kernel(
    x_raw, b_raw, c_raw, before, dt_raw, dt_bias, a_log, conv_x, conv_b, conv_c, grad_y,
    pay, x_out, slope_out, bc_out, slope_bc_out, cum_out, step_out,
    rows_scr,
):
    pre = dt_raw[...].astype(f32) + to_column(dt_bias[...])
    step = jnp.maximum(pre, 0.0) + jnp.log1p(jnp.exp(-jnp.abs(pre)))
    log_decay = -jnp.exp(to_column(a_log[...])) * step
    r, c = iota((TOKENS, TOKENS), 0), iota((TOKENS, TOKENS), 1)
    upto = onehot((r <= c) & (r // SUB == c // SUB))
    parts = split3(log_decay)
    cum = dot(parts[2], upto) + dot(parts[1], upto) + dot(parts[0], upto)
    cum_out[...] = cum
    step_out[...] = step
    _, _, from_start, to_end, total = decay_terms(cum, step)
    columns = transpose_rows([from_start, to_end])

    def conv(raw, halo, taps, lanes):
        rows_scr[8 - RIM : 8, lanes] = halo.astype(f32)
        rows_scr[8:, lanes] = raw.astype(f32)
        v = taps[0:1] * rows_scr[8 - RIM : 8 - RIM + TOKENS, lanes]
        for k in range(1, RIM + 1):
            v += taps[k : k + 1] * rows_scr[8 - RIM + k : 8 - RIM + k + TOKENS, lanes]
        gate = 1.0 / (1.0 + jnp.exp(-v))
        return v * gate, gate * (1.0 + v * (1.0 - gate))

    b, slope_b = conv(b_raw[...], before[:, WIDTH : WIDTH + STATE], conv_b[...], pl.ds(0, 128))
    c, slope_c = conv(c_raw[...], before[:, WIDTH + STATE :], conv_c[...], pl.ds(0, 128))
    bc_out[:, :STATE] = b
    bc_out[:, STATE:] = c
    slope_bc_out[:, :STATE] = slope_b
    slope_bc_out[:, STATE:] = slope_c
    bt = split2(b.T)
    ct = split2(c.T)
    for pair in range(PAIRS):
        lanes = pl.ds(pair * 128, 128)
        x, slope = conv(x_raw[:, lanes], before[:, pair * 128 : pair * 128 + 128], conv_x[:, lanes], lanes)
        x_out[:, lanes] = x
        slope_out[:, lanes] = slope
        xw = x * spread(columns, 1, 2 * pair, HEAD_DIM, 128)
        ge = grad_y[:, lanes].astype(f32) * spread(columns, 0, 2 * pair, HEAD_DIM, 128)
        s_heads = split_heads(dot3(bt, split2(xw)))
        g_heads = split_heads(dot3(ct, split2(ge)))
        for k in range(2):
            head = 2 * pair + k
            s_code, s_scale = encode(s_heads[k])
            g_code, g_scale = encode(g_heads[k])
            pay[head, 0:64, :] = s_code
            pay[head, 64:128, :] = g_code
            d = split3(jnp.broadcast_to(total[head : head + 1], (1, 128)))
            at = iota((16, 128), 0)
            aux = jnp.where(at == 0, s_scale, g_scale)
            for n, part in enumerate(d):
                aux = jnp.where(at == 2 + n, part.astype(f32), aux)
            pay[head, 128:144, :] = aux.astype(bf16)


def scan_kernel(got, back):
    def aux_row(k, n):
        return got[k, 128:144, :].astype(f32)[n : n + 1]

    decay = [jnp.exp(aux_row(k, 2) + aux_row(k, 3) + aux_row(k, 4)) for k in range(RANKS)]
    scales = [[None, None] for _ in range(RANKS)]
    run = jnp.zeros((HEAD_DIM, 128), f32)
    for k in range(RANKS):
        code, scales[k][0] = encode(run)
        back[k, 0:64, :] = code
        if k < RANKS - 1:
            run = decay[k] * run + decode(got[k, 0:64, :], aux_row(k, 0))
    run = jnp.zeros((HEAD_DIM, 128), f32)
    for k in reversed(range(RANKS)):
        code, scales[k][1] = encode(run)
        back[k, 64:128, :] = code
        if k > 0:
            run = decay[k] * run + decode(got[k, 64:128, :], aux_row(k, 1))
    at = iota((16, 128), 0)
    for k in range(RANKS):
        back[k, 128:144, :] = jnp.where(at == 0, scales[k][0], scales[k][1]).astype(bf16)


def block_kernel(
    x_in, grad_y, bc_in, cum_in, step_in, skip,
    y_out, dx_out, dbc_out, sums_out,
    ds_scr, diag_scr, cols_scr, sc_scr, row_scr,
):
    cum, step = cum_in[...], step_in[...]
    shifted = cum - jnp.log(step)
    for head in range(HEADS):
        row_scr[head] = jnp.broadcast_to(cum[head : head + 1], (8, TOKENS))
        row_scr[HEADS + head] = jnp.broadcast_to(shifted[head : head + 1], (8, TOKENS))
    inner, outer, _, _, _ = decay_terms(cum, step)
    for n, part in enumerate(transpose_rows([cum, shifted, inner, outer, step])):
        cols_scr[n] = part
    b, c = bc_in[:, :STATE], bc_in[:, STATE:]
    r, l = iota((SUB, SUB), 0), iota((SUB, SUB), 1)
    b2, c2 = split2(b), split2(c)

    def rows(parts, s):
        return tuple(p[s * SUB : s * SUB + SUB] for p in parts)

    for s in range(2):
        sc_scr[s] = jnp.where(r > l, dot3(rows(c2, s), rows(b2, s), NT), 0.0)
        sc_scr[2 + s] = jnp.where(l > r, dot3(rows(b2, s), rows(c2, s), NT), 0.0)
    sc_scr[4] = dot3(rows(c2, 1), rows(b2, 0), NT)
    sc_scr[5] = dot3(rows(b2, 0), rows(c2, 1), NT)
    ds_scr[...] = jnp.zeros_like(ds_scr)
    sums_out[...] = jnp.zeros_like(sums_out)
    diag = jnp.broadcast_to(jnp.sum(b * c, axis=1, keepdims=True), (TOKENS, 128))
    diag_scr[0] = diag
    diag_scr[1] = jnp.zeros((TOKENS, 128), f32)
    low = low_half((SUB, 128))

    def pair_step(pair, carry):
        lanes = pl.ds(pl.multiple_of(pair * 128, 128), 128)
        cols = (cols_scr[0], cols_scr[1], cols_scr[2])
        x = x_in[:, lanes]
        g = grad_y[:, lanes]
        gf = g.astype(f32)
        xh, xl = split2(x)
        cum_cols = spread(cols, 0, 2 * pair, 128, 256)
        shifted_cols = spread(cols, 1, 2 * pair, 128, 256)
        inner_x = spread(cols, 2, 2 * pair, HEAD_DIM, 128)
        outer_x = spread(cols, 3, 2 * pair, HEAD_DIM, 128)
        step_x = spread(cols, 4, 2 * pair, HEAD_DIM, 128)
        ys, dxs = [], []
        for s in range(2):
            at = slice(s * SUB, s * SUB + SUB)
            xh_s, xl_s, g_s = xh[at], xl[at], g[at]
            xh2 = jnp.concatenate([xh_s, xh_s], axis=0)
            g2 = jnp.concatenate([g_s, g_s], axis=0)
            xhl = jnp.concatenate([xh_s, xl_s], axis=1)
            y_k, dx_k = [], []
            for k in range(2):
                head = 2 * pair + k
                row_cum = row_scr[head][0:1, at]
                row_shift = row_scr[HEADS + head][0:1, at]
                col_cum = cum_cols[at, k * 128 : k * 128 + 128]
                col_shift = shifted_cols[at, k * 128 : k * 128 + 128]
                decay = jnp.exp(jnp.where(r > l, col_cum - row_shift, NEG))
                decay_t = jnp.exp(jnp.where(l > r, row_cum - col_shift, NEG))
                mh, ml = split2(sc_scr[s] * decay)
                th, tl = split2(sc_scr[2 + s] * decay_t)
                y_k.append(dot(jnp.concatenate([mh, ml], axis=1), xh2) + dot(mh, xl_s))
                dx_k.append(dot(jnp.concatenate([th, tl], axis=1), g2))
                g_k = jnp.where(low if k == 0 else ~low, g_s.astype(f32), 0.0).astype(bf16)
                dm = dot(jnp.concatenate([g_k, g_k], axis=1), xhl, NT)
                ds_scr[s] += dm * decay
            ys.append(jnp.where(low, y_k[0], y_k[1]))
            dxs.append(jnp.where(low, dx_k[0], dx_k[1]))
        xw = split2(x[:SUB] * outer_x[:SUB])
        ge = split2(gf[SUB:] * inner_x[SUB:])
        ys[1] += inner_x[SUB:] * dot3(split2(sc_scr[4]), xw)
        dxs[0] += outer_x[:SUB] * dot3(split2(sc_scr[5]), ge)
        ds_scr[2] += dot3(ge, xw, NT)
        y = jnp.concatenate(ys, axis=0)
        dx = jnp.concatenate(dxs, axis=0)
        xg = x * gf
        xdx = x * dx
        hot = onehot(iota((HEADS, 128), 0) == 2 * pair + iota((HEADS, 128), 1) // HEAD_DIM)

        def head_sums(v):
            hi, mid, lo = split3(v)
            return dot(hot, hi, NT) + dot(hot, mid, NT) + dot(hot, lo, NT)

        sums_out[0] += head_sums(gf * y - xdx)
        sums_out[1] += head_sums(xdx)
        sums_out[2] += head_sums(xg)
        diag_scr[1] += step_x * xg
        low2 = low_half((TOKENS, 128))
        direct = jnp.where(low2, skip[0, 2 * pair], skip[0, 2 * pair + 1]) + diag_scr[0] * step_x
        y_out[:, lanes] = y + direct * x
        dx_out[:, lanes] = dx + direct * gf
        return carry

    lax.fori_loop(0, PAIRS, pair_step, 0)
    d_diag = jnp.sum(diag_scr[1], axis=1, keepdims=True)
    db = d_diag * c
    dc = d_diag * b
    for s in range(2):
        d2 = split2(jnp.where(r > l, ds_scr[s], 0.0))
        t2 = split2(jnp.where(r > l, ds_scr[s], 0.0).T)
        at = slice(s * SUB, s * SUB + SUB)
        dc_s = dc[at] + dot3(d2, rows(b2, s))
        db_s = db[at] + dot3(t2, rows(c2, s))
        if s == 0:
            db_s += dot3(split2(ds_scr[2].T), rows(c2, 1))
        else:
            dc_s += dot3(split2(ds_scr[2]), rows(b2, 0))
        dbc_out[at, :STATE] = db_s
        dbc_out[at, STATE:] = dc_s
    ones = onehot(iota((16, 128), 0) >= 0)
    bc = split3(b * c)
    diag_row = dot(ones, bc[0], NT) + dot(ones, bc[1], NT) + dot(ones, bc[2], NT)
    sums_out[1] = sums_out[1] / step + diag_row * sums_out[2]


def leave_kernel(
    back, x_in, grad_y, bc_in, slope_in, slope_bc_in, cum_in, step_in, y_in, dx_in, dbc_in, sums_in,
    dt_raw, dt_bias, a_log,
    y_out, dpre_out, dpre_bc_out, dt_out,
    e_scr, f_scr,
):
    cum, step = cum_in[...], step_in[...]
    _, _, from_start, to_end, total = decay_terms(cum, step)
    columns = transpose_rows([from_start, to_end])
    b2, c2 = split2(bc_in[:, :STATE]), split2(bc_in[:, STATE:])
    db = dbc_in[:, :STATE]
    dc = dbc_in[:, STATE:]
    carried = jnp.zeros((HEADS, TOKENS), f32)
    later = jnp.zeros((HEADS, TOKENS), f32)
    both = jnp.zeros((HEADS, 8), f32)
    for pair in range(PAIRS):
        lanes = pl.ds(pair * 128, 128)
        codes = []
        for k in range(2):
            head = 2 * pair + k
            aux = back[head, 128:144, :].astype(f32)
            codes.append((decode(back[head, 0:64, :], aux[0:1]), decode(back[head, 64:128, :], aux[1:2])))
        e = jnp.concatenate(join_heads(codes[0][0], codes[1][0]), axis=0)
        f = jnp.concatenate(join_heads(codes[0][1], codes[1][1]), axis=0)
        e2, f2 = split2(e), split2(f)
        start_x = spread(columns, 0, 2 * pair, HEAD_DIM, 128)
        end_x = spread(columns, 1, 2 * pair, HEAD_DIM, 128)
        ge = grad_y[:, lanes].astype(f32) * start_x
        xw = x_in[:, lanes] * end_x
        ce = dot3(c2, e2)
        bf = dot3(b2, f2)
        y_out[:, lanes] = y_in[:, lanes] + start_x * ce
        dpre_out[:, lanes] = (dx_in[:, lanes] + end_x * bf) * slope_in[:, lanes]
        dc += dot3(split2(ge), e2, NT)
        db += dot3(split2(xw), f2, NT)
        hot = onehot(iota((HEADS, 128), 0) == 2 * pair + iota((HEADS, 128), 1) // HEAD_DIM)

        def head_sums(v):
            hi, mid, lo = split3(v)
            return dot(hot, hi, NT) + dot(hot, mid, NT) + dot(hot, lo, NT)

        carried += head_sums(ge * ce)
        later += head_sums(xw * bf)
        both += head_sums(jnp.broadcast_to(jnp.sum(e * f, axis=0, keepdims=True), (8, 128)))
    dpre_bc_out[:, :STATE] = db * slope_bc_in[:, :STATE]
    dpre_bc_out[:, STATE:] = dc * slope_bc_in[:, STATE:]
    r, c = iota((TOKENS, TOKENS), 0), iota((TOKENS, TOKENS), 1)
    suffix = onehot(r >= c)
    prefix = onehot(r < c)

    def summed(v, tri):
        hi, mid, lo = split3(v)
        return dot(lo, tri) + dot(mid, tri) + dot(hi, tri)

    d_decay = summed(sums_in[0] + carried, suffix) + summed(later, prefix) + jnp.exp(total) * both[:, 0:1]
    d_step = sums_in[1] + later / step - jnp.exp(to_column(a_log[...])) * d_decay
    pre = dt_raw[...].astype(f32) + to_column(dt_bias[...])
    dt_out[...] = d_step / (1.0 + jnp.exp(-pre))


def settle_kernel(dpre, dpre_bc, after, conv_x, conv_b, conv_c, gx, gb, gc, rows_scr):
    def unconv(d, halo, taps, lanes):
        rows_scr[0:TOKENS, lanes] = d
        rows_scr[TOKENS : TOKENS + RIM, lanes] = halo
        v = taps[RIM : RIM + 1] * d
        for k in range(RIM):
            v += taps[k : k + 1] * rows_scr[RIM - k : RIM - k + TOKENS, lanes]
        return v

    for pair in range(PAIRS):
        lanes = pl.ds(pair * 128, 128)
        gx[:, lanes] = unconv(dpre[:, lanes], after[:, pair * 128 : pair * 128 + 128], conv_x[:, lanes], lanes)
    gb[...] = unconv(dpre_bc[:, :STATE], after[:, WIDTH : WIDTH + STATE], conv_b[...], pl.ds(0, 128))
    gc[...] = unconv(dpre_bc[:, STATE:], after[:, WIDTH + STATE :], conv_c[...], pl.ds(0, 128))


VMEM = pl.BlockSpec(memory_space=pltpu.VMEM)
SMEM = pl.BlockSpec(memory_space=pltpu.SMEM)
PARAMS = pltpu.CompilerParams(vmem_limit_bytes=48 * 1024 * 1024)


def call(kernel, outs, ins, scratch=(), flops=0, specs=None):
    shapes = [jax.ShapeDtypeStruct(s, d) for s, d in outs]
    moved = sum(a.size * a.dtype.itemsize for a in ins) + sum(
        s.size * s.dtype.itemsize for s in shapes
    )
    return pl.pallas_call(
        kernel,
        out_shape=shapes,
        in_specs=specs or [VMEM] * len(ins),
        out_specs=[VMEM] * len(outs),
        scratch_shapes=list(scratch),
        compiler_params=PARAMS,
        cost_estimate=pl.CostEstimate(flops=flops, bytes_accessed=moved, transcendentals=0),
    )(*ins)


def on_device(
    x_raw, b_raw, c_raw, dt_raw, dt_bias, a_log, skip_gain, conv_x, conv_b, conv_c, grad_y
):
    wide, slim, bc = (TOKENS, WIDTH), (HEADS, TOKENS), (TOKENS, 2 * STATE)
    dt_bias, a_log, skip_gain = (v.reshape(1, HEADS) for v in (dt_bias, a_log, skip_gain))
    edge = jnp.concatenate([v[TOKENS - RIM :] for v in (x_raw, b_raw, c_raw)], axis=1)
    before = lax.ppermute(edge, "context", [(i, i + 1) for i in range(RANKS - 1)])
    pay, x, slope, bcs, slope_bc, cum, step = call(
        enter_kernel,
        [((HEADS, CHUNK, 128), bf16), (wide, f32), (wide, f32), (bc, f32), (bc, f32), (slim, f32), (slim, f32)],
        [x_raw, b_raw, c_raw, before, dt_raw, dt_bias, a_log, conv_x, conv_b, conv_c, grad_y],
        [pltpu.VMEM((TOKENS + 8, WIDTH), f32)],
        flops=2_000_000_000,
    )
    got = lax.all_to_all(pay, "context", 0, 0, tiled=True)
    y_part, dx_part, dbc_part, sums = call(
        block_kernel,
        [(wide, f32), (wide, f32), (bc, f32), ((3,) + slim, f32)],
        [x, grad_y, bcs, cum, step, skip_gain],
        [
            pltpu.VMEM((3, SUB, SUB), f32),
            pltpu.VMEM((2, TOKENS, 128), f32),
            pltpu.VMEM((3, TOKENS, 128), bf16),
            pltpu.VMEM((6, SUB, SUB), f32),
            pltpu.VMEM((2 * HEADS, 8, TOKENS), f32),
        ],
        flops=8_000_000_000,
        specs=[VMEM] * 5 + [SMEM],
    )
    (answer,) = call(scan_kernel, [((RANKS, CHUNK, 128), bf16)], [got])
    back = lax.all_to_all(answer, "context", 0, 0, tiled=True)
    y_out, dpre, dpre_bc, grad_dt = call(
        leave_kernel,
        [(wide, f32), (wide, f32), (bc, f32), (slim, f32)],
        [back, x, grad_y, bcs, slope, slope_bc, cum, step, y_part, dx_part, dbc_part, sums, dt_raw, dt_bias, a_log],
        [pltpu.VMEM((8, 128), f32), pltpu.VMEM((8, 128), f32)],
        flops=2_000_000_000,
    )
    rim = jnp.concatenate([dpre[:RIM], dpre_bc[:RIM]], axis=1)
    after = lax.ppermute(rim, "context", [(i, i - 1) for i in range(1, RANKS)])
    grad_x, grad_b, grad_c = call(
        settle_kernel,
        [(wide, f32), ((TOKENS, STATE), f32), ((TOKENS, STATE), f32)],
        [dpre, dpre_bc, after, conv_x, conv_b, conv_c],
        [pltpu.VMEM((TOKENS + 8, WIDTH), f32)],
        flops=2_000_000,
    )
    return (y_out, grad_x, grad_b, grad_c, grad_dt)


def solution(mesh):
    tokens = P(("dp", "context"), "tensor")
    heads = P("tensor", ("dp", "context"))
    one, taps = P("tensor"), P(None, "tensor")
    return jax.shard_map(
        on_device,
        mesh=mesh,
        in_specs=(tokens, tokens, tokens, heads, one, one, one, taps, taps, taps, tokens),
        out_specs=(tokens, tokens, tokens, tokens, heads),
        check_vma=False,
    )
```

time: 303 us -> 75.8 us (0.25); the launches traced: 299 us -> 75 us
  waiting for transfers between devices: 92.1 us -> 7.18 us
  other arithmetic: 59.7 us -> 0.02 us
  local copies, waits for them, and re-layouts: 55.5 us -> 13.2 us
  matrix products: 36.1 us -> 0 us
  Pallas kernels: 0 us -> 25.8 us
  blocking collectives: 32.9 us -> 16.4 us
  between operations: 15.5 us -> 0.75 us
  starting transfers between devices: 6.22 us -> 11.7 us
    all_gather x2 -> x0, waiting for transfers between devices: 89.8 us -> none  [prefix(): everything = jax.tree.map(lambda part: lax.all_gather(part, axis), value)]
    select_n x32 -> x0, other arithmetic: 37.5 us -> none  [lap(): return jax.tree.map(lambda a, b: jnp.where(reached, a, b), new, before)]
    dot_general x14 -> x0, matrix products: 36.1 us -> none  [the longest x3 18.1 us: span_step(): jnp.einsum('gkij,jgkp->igkp', mixing, x_group, precision=precise)]
    unnamed x1 -> x0, blocking collectives: 32.9 us -> none
    exp x32 -> x0, local copies, waits for them, and re-layouts: 30.3 us -> none  [combine(): jnp.exp(later[0])[:, None, None] * earlier[1] + later[1]]
    pallas_call x0 -> x5, Pallas kernels: none -> 25.8 us  [call(): pl.pallas_call(kernel, out_shape=shapes, in_specs=specs or [VMEM] * len(i...]
    all_to_all x0 -> x1, blocking collectives: none -> 16.4 us  [on_device(): got = lax.all_to_all(pay, 'context', 0, 0, tiled=True)]
    another operation x9 -> x0, other arithmetic: 7.7 us -> none
  transfers between devices with their start and end apart: 4 -> 3, of which waited for: 4 -> 2; matrix products, arithmetic and copies ran while one was open for 14% -> 0% of each run, Pallas kernels for 0% -> 15%
where the time goes in v1:
time: 75.8 us; the launch traced here: 75 us
  Pallas kernels  25.8 us (34%)
  blocking collectives  16.4 us (22%)
  local copies, waits for them, and re-layouts  13.2 us (17%)
  starting transfers between devices  11.7 us (15%)
  waiting for transfers between devices  7.18 us (9%)
    pallas_call x5, Pallas kernels, call(): pl.pallas_call(kernel, out_shape=shapes, in_specs=specs or [VMEM] * len(i...  25.8 us
    all_to_all x1, blocking collectives, on_device(): got = lax.all_to_all(pay, 'context', 0, 0, tiled=True)  16.4 us
    unnamed x40, local copies, waits for them, and re-layouts  11.1 us
    all_to_all x1, starting transfers between devices, on_device(): back = lax.all_to_all(answer, 'context', 0, 0, tiled=True)  5.58 us
    ppermute x1, waiting for transfers between devices, on_device(): after = lax.ppermute(rim, 'context', [(i, i - 1) for i in range(1, RANKS)])  5.02 us
    ppermute x1, starting transfers between devices, on_device(): lax.ppermute(edge, 'context', [(i, i + 1) for i in range(RANKS - 1)])  3.4 us
    ppermute x1, starting transfers between devices, on_device(): after = lax.ppermute(rim, 'context', [(i, i - 1) for i in range(1, RANKS)])  2.76 us
    ppermute x1, waiting for transfers between devices, on_device(): lax.ppermute(edge, 'context', [(i, i + 1) for i in range(RANKS - 1)])  2.16 us
  transfers between devices with their start and end apart: 3, of which 2 were waited for; matrix products, arithmetic and copies ran while one was open for 0% of the time, Pallas kernels for 15%

profile of v1, /device:TPU:38, one launch (start us, length us, event | category | flops | bytes accessed | tf_op | source)
XLA Modules:
  0.0 75.0 jit_solution(7426152118769147228)
XLA Ops:
  0.6 0.7 slice.16
  1.3 0.7 slice.17
  2.0 0.7 slice.15
  2.8 3.4 %collective-permute-start = (bf16[3,1280]{1,0:T(4,128)(2,1)S(1)}, bf16[3,1280]{1,0:T(4,128)(2,1)S(1)}, u32[]{:S(2)}, u32[]{:S(2)}) collective-permute-start(bf16[3,1280]{1,0:T(4,128)(2,1)S(1)} %pad_maximum_fusion.1), channel_id=1, source_target_pairs={{0,1},{1,2},{2,3},{3,4},{4,5},{5,6},{6,7},{7,8},{8,9},{9,10},{10,1... | collective-permute-start | bytes 23048 | tf_op jit(solution)/shard_map/ppermute | solution.py:427
  6.2 2.2 %collective-permute-done.before = bf16[3,1280]{1,0:T(4,128)(2,1)S(1)} collective-permute-done((bf16[3,1280]{1,0:T(4,128)(2,1)S(1)}, bf16[3,1280]{1,0:T(4,128)(2,1)S(1)}, u32[]{:S(2)}, u32[]{:S(2)}) %collective-permute-start) | collective-permute-done | bytes 7712 | tf_op jit(solution)/shard_map/ppermute | solution.py:427
  9.0 1.0 %copy-done.3 = bf16[256,1024]{1,0:T(8,128)(2,1)S(1)} copy-done((bf16[256,1024]{1,0:T(8,128)(2,1)S(1)}, bf16[256,1024]{1,0:T(8,128)(2,1)}, u32[]{:S(2)}) %copy-start.3) | copy-done | bytes 524312
  10.1 0.8 %copy-done.4 = bf16[256,128]{1,0:T(8,128)(2,1)S(1)} copy-done((bf16[256,128]{1,0:T(8,128)(2,1)S(1)}, bf16[256,128]{1,0:T(8,128)(2,1)}, u32[]{:S(2)}) %copy-start.4) | copy-done | bytes 65560
  10.9 0.8 %copy-done.5 = bf16[256,128]{1,0:T(8,128)(2,1)S(1)} copy-done((bf16[256,128]{1,0:T(8,128)(2,1)S(1)}, bf16[256,128]{1,0:T(8,128)(2,1)}, u32[]{:S(2)}) %copy-start.5) | copy-done | bytes 65560
  11.8 1.0 %copy-done.6 = bf16[256,1024]{1,0:T(8,128)(2,1)S(1)} copy-done((bf16[256,1024]{1,0:T(8,128)(2,1)S(1)}, bf16[256,1024]{1,0:T(8,128)(2,1)}, u32[]{:S(2)}) %copy-start.6) | copy-done | bytes 524312
  12.8 4.8 %shard_map.146 = (bf16[16,144,128]{2,1,0:T(8,128)(2,1)S(1)}, f32[256,1024]{1,0:T(8,128)S(1)}, f32[256,1024]{1,0:T(8,128)S(1)}, f32[256,256]{1,0:T(8,128)S(1)}, f...) custom-call(bf16[256,1024]{1,0:T(8,128)(2,1)S(1)} %copy-done.3, ...), custom_call_target="tpu_custom_call" | custom-call | flops 2000000000 | bytes 4460160 | tf_op jit(solution)/shard_map/pallas_call | solution.py:410
  17.6 16.4 %all_to_all.10.got = bf16[16,144,128]{2,1,0:T(8,128)(2,1)S(1)} all-to-all(bf16[16,144,128]{2,1,0:T(8,128)(2,1)S(1)} %get-tuple-element.23), channel_id=1, replica_groups=mesh['dp'=2,'tensor'=8,'context'=16] {'context'}, dimensions={0} | all-to-all | bytes 1179648 | tf_op jit(solution)/shard_map/all_to_all | solution.py:435
  34.0 1.5 %shard_map.147 = bf16[16,144,128]{2,1,0:T(8,128)(2,1)} custom-call(bf16[16,144,128]{2,1,0:T(8,128)(2,1)S(1)} %all_to_all.10.got), custom_call_target="tpu_custom_call" | custom-call | bytes 1179648 | tf_op jit(solution)/shard_map/pallas_call | solution.py:410
  35.5 5.6 %all-to-all-start.1 = ((bf16[16,144,128]{2,1,0:T(8,128)(2,1)}), bf16[16,144,128]{2,1,0:T(8,128)(2,1)S(1)}, u32[]{:S(2)}, u32[]{:S(2)}) async-start(bf16[16,144,128]{2,1,0:T(8,128)(2,1)} %shard_map.147), calls=%async_computation.1 | async-start | bytes 1179648 | tf_op jit(solution)/shard_map/all_to_all | solution.py:451
  41.8 11.0 %shard_map.148 = (f32[256,1024]{1,0:T(8,128)S(1)}, f32[256,1024]{1,0:T(8,128)S(1)}, f32[256,256]{1,0:T(8,128)S(1)}, f32[3,16,256]{2,1,0:T(8,128)S(1)}) custom-call(f32[256,1024]{1,0:T(8,128)S(1)} %get-tuple-element.24.x_in, bf16[256,1024]{1,0:T(8,128)(2,1)S(1)} %copy-done.7, f32[256,256]{1,0:T(8,128)S(1)} %get-tuple-element.25.bc_in, ...), custom_call_target="tpu_custom_call" | custom-call | flops 8000000000 | bytes 4276288 | tf_op jit(solution)/shard_map/pallas_call | solution.py:410
  52.8 1.0 %copy-done.12 = f32[256,1024]{1,0:T(8,128)} copy-done((f32[256,1024]{1,0:T(8,128)}, f32[256,1024]{1,0:T(8,128)S(1)}, u32[]{:S(2)}) %copy-start.12) | copy-done | bytes 1048600
  53.7 1.0 %copy-done.13 = f32[256,1024]{1,0:T(8,128)} copy-done((f32[256,1024]{1,0:T(8,128)}, f32[256,1024]{1,0:T(8,128)S(1)}, u32[]{:S(2)}) %copy-start.13) | copy-done | bytes 1048600
  54.8 0.7 copy-done.16
  56.1 0.9 %copy-done.15 = f32[256,256]{1,0:T(8,128)S(1)} copy-done((f32[256,256]{1,0:T(8,128)S(1)}, f32[256,256]{1,0:T(8,128)}, u32[]{:S(2)}) %copy-start.15) | copy-done | bytes 262168
  57.0 0.9 %copy-done.17 = f32[256,256]{1,0:T(8,128)S(1)} copy-done((f32[256,256]{1,0:T(8,128)S(1)}, f32[256,256]{1,0:T(8,128)}, u32[]{:S(2)}) %copy-start.17) | copy-done | bytes 262168
  58.0 0.8 %copy-done.19 = f32[3,16,256]{2,1,0:T(8,128)S(1)} copy-done((f32[3,16,256]{2,1,0:T(8,128)S(1)}, f32[3,16,256]{2,1,0:T(8,128)}, u32[]{:S(2)}) %copy-start.19) | copy-done | bytes 49176
  58.8 6.6 %shard_map.149 = (f32[256,1024]{1,0:T(8,128)}, f32[256,1024]{1,0:T(8,128)S(1)}, f32[256,256]{1,0:T(8,128)S(1)}, f32[16,256]{1,0:T(8,128)}) custom-call(bf16[16,144,128]{2,1,0:T(8,128)(2,1)S(1)} %all-to-all-done.1.back, f32[256,1024]{1,0:T(8,128)S(1)} %get-tuple-element.24.x_in, bf16[256,1024]{1,0:T(8,128)(2,1)S(1)} %copy-done.7, ...), custom_call_target="tpu_custom_call" | custom-call | flops 2000000000 | bytes 8560768 | tf_op jit(solution)/shard_map/pallas_call | solution.py:410
  65.4 2.8 %collective-permute-start.1 = (f32[3,1280]{1,0:T(4,128)S(1)}, f32[3,1280]{1,0:T(4,128)S(1)}, u32[]{:S(2)}, u32[]{:S(2)}) collective-permute-start(f32[3,1280]{1,0:T(4,128)S(1)} %pad_maximum_fusion), channel_id=1, source_target_pairs={{1,0},{2,1},{3,2},{4,3},{5,4},{6,5},{7,6},{8,7},{9,8},{10,9},{11,1... | collective-permute-start | bytes 46088 | tf_op jit(solution)/shard_map/ppermute | solution.py:460
  68.2 5.0 %collective-permute-done.1.after = f32[3,1280]{1,0:T(4,128)S(1)} collective-permute-done((f32[3,1280]{1,0:T(4,128)S(1)}, f32[3,1280]{1,0:T(4,128)S(1)}, u32[]{:S(2)}, u32[]{:S(2)}) %collective-permute-start.1) | collective-permute-done | bytes 15392 | tf_op jit(solution)/shard_map/ppermute | solution.py:460
  73.2 1.8 %shard_map.150 = (f32[256,1024]{1,0:T(8,128)}, f32[256,128]{1,0:T(8,128)}, f32[256,128]{1,0:T(8,128)}) custom-call(f32[256,1024]{1,0:T(8,128)S(1)} %get-tuple-element.35.dpre, f32[256,256]{1,0:T(8,128)S(1)} %get-tuple-element.36.dpre_bc, f32[3,1280]{1,0:T(4,128)S(1)} %collective-permute-done.1.after, f32[4,1024]{1,0:T(4,128)S(1)} %copy-done, ...), custom_call_target="tpu_custom_call" | custom-call | flops 2000000 | bytes 2657280 | tf_op jit(solution)/shard_map/pallas_call | solution.py:410
  (35 shorter events, 2.0 us)
Async XLA Ops:
  2.0 6.4 %copy-start = (f32[4,1024]{1,0:T(4,128)S(1)}, f32[4,1024]{1,0:T(4,128)}, u32[]{:S(2)}) copy-start(f32[4,1024]{1,0:T(4,128)} %conv_x.3) | copy-start | bytes 49156
  2.7 5.6 %copy-start.2 = (f32[4,128]{1,0:T(4,128)S(1)}, f32[4,128]{1,0:T(4,128)}, u32[]{:S(2)}) copy-start(f32[4,128]{1,0:T(4,128)} %conv_c.3) | copy-start | bytes 6148
  2.8 5.6 %copy-start.8 = (bf16[16,256]{1,0:T(8,128)(2,1)S(1)}, bf16[16,256]{1,0:T(8,128)(2,1)}, u32[]{:S(2)}) copy-start(bf16[16,256]{1,0:T(8,128)(2,1)} %dt_raw.3) | copy-start | bytes 24580
  2.8 5.6 %copy-start.1 = (f32[4,128]{1,0:T(4,128)S(1)}, f32[4,128]{1,0:T(4,128)}, u32[]{:S(2)}) copy-start(f32[4,128]{1,0:T(4,128)} %conv_b.3) | copy-start | bytes 6148
  2.8 5.6 %collective-permute-start = (bf16[3,1280]{1,0:T(4,128)(2,1)S(1)}, bf16[3,1280]{1,0:T(4,128)(2,1)S(1)}, u32[]{:S(2)}, u32[]{:S(2)}) collective-permute-start(bf16[3,1280]{1,0:T(4,128)(2,1)S(1)} %pad_maximum_fusion.1), channel_id=1, source_target_pairs={{0,1},{1,2},{2,3},{3,4},{4,5},{5,6},{6,7},{7,8},{8,9},{9,10},{10,1... | collective-permute-start | bytes 23048 | tf_op jit(solution)/shard_map/ppermute | solution.py:427
  8.4 0.7 copy-start.10
  8.4 0.7 copy-start.11
  9.0 1.0 %copy-start.3 = (bf16[256,1024]{1,0:T(8,128)(2,1)S(1)}, bf16[256,1024]{1,0:T(8,128)(2,1)}, u32[]{:S(2)}) copy-start(bf16[256,1024]{1,0:T(8,128)(2,1)} %x_raw.1) | copy-start | bytes 1572868
  10.1 0.8 %copy-start.4 = (bf16[256,128]{1,0:T(8,128)(2,1)S(1)}, bf16[256,128]{1,0:T(8,128)(2,1)}, u32[]{:S(2)}) copy-start(bf16[256,128]{1,0:T(8,128)(2,1)} %b_raw.1) | copy-start | bytes 196612
  10.9 0.8 %copy-start.5 = (bf16[256,128]{1,0:T(8,128)(2,1)S(1)}, bf16[256,128]{1,0:T(8,128)(2,1)}, u32[]{:S(2)}) copy-start(bf16[256,128]{1,0:T(8,128)(2,1)} %c_raw.1) | copy-start | bytes 196612
  11.8 1.0 %copy-start.6 = (bf16[256,1024]{1,0:T(8,128)(2,1)S(1)}, bf16[256,1024]{1,0:T(8,128)(2,1)}, u32[]{:S(2)}) copy-start(bf16[256,1024]{1,0:T(8,128)(2,1)} %grad_y.5) | copy-start | bytes 1572868
  17.6 16.4 %copy-start.14 = (f32[256,256]{1,0:T(8,128)}, f32[256,256]{1,0:T(8,128)S(1)}, u32[]{:S(2)}) copy-start(f32[256,256]{1,0:T(8,128)S(1)} %get-tuple-element.27.slope_bc_in) | copy-start | bytes 786436
  35.5 5.6 %copy-start.7 = (bf16[256,1024]{1,0:T(8,128)(2,1)S(1)}, bf16[256,1024]{1,0:T(8,128)(2,1)}, u32[]{:S(2)}) copy-start(bf16[256,1024]{1,0:T(8,128)(2,1)} %grad_y.5) | copy-start | bytes 1572868
  35.5 20.5 %all-to-all-start.1 = ((bf16[16,144,128]{2,1,0:T(8,128)(2,1)}), bf16[16,144,128]{2,1,0:T(8,128)(2,1)S(1)}, u32[]{:S(2)}, u32[]{:S(2)}) async-start(bf16[16,144,128]{2,1,0:T(8,128)(2,1)} %shard_map.147), calls=%async_computation.1 | async-start | bytes 1179648 | tf_op jit(solution)/shard_map/all_to_all | solution.py:451
  41.1 0.7 copy-start.9
  52.8 1.0 %copy-start.12 = (f32[256,1024]{1,0:T(8,128)}, f32[256,1024]{1,0:T(8,128)S(1)}, u32[]{:S(2)}) copy-start(f32[256,1024]{1,0:T(8,128)S(1)} %get-tuple-element.30.y_in) | copy-start | bytes 3145732
  53.7 1.0 %copy-start.13 = (f32[256,1024]{1,0:T(8,128)}, f32[256,1024]{1,0:T(8,128)S(1)}, u32[]{:S(2)}) copy-start(f32[256,1024]{1,0:T(8,128)S(1)} %get-tuple-element.31.dx_in) | copy-start | bytes 3145732
  54.7 0.7 copy-start.16
  55.4 0.6 copy-start.18
  56.1 1.0 %copy-start.15 = (f32[256,256]{1,0:T(8,128)S(1)}, f32[256,256]{1,0:T(8,128)}, u32[]{:S(2)}) copy-start(f32[256,256]{1,0:T(8,128)} %copy-done.14) | copy-start | bytes 786436
  57.0 0.9 %copy-start.17 = (f32[256,256]{1,0:T(8,128)S(1)}, f32[256,256]{1,0:T(8,128)}, u32[]{:S(2)}) copy-start(f32[256,256]{1,0:T(8,128)} %copy-done.16) | copy-start | bytes 786436
  58.0 0.8 %copy-start.19 = (f32[3,16,256]{2,1,0:T(8,128)S(1)}, f32[3,16,256]{2,1,0:T(8,128)}, u32[]{:S(2)}) copy-start(f32[3,16,256]{2,1,0:T(8,128)} %copy-done.18) | copy-start | bytes 147460
  65.4 7.8 %collective-permute-start.1 = (f32[3,1280]{1,0:T(4,128)S(1)}, f32[3,1280]{1,0:T(4,128)S(1)}, u32[]{:S(2)}, u32[]{:S(2)}) collective-permute-start(f32[3,1280]{1,0:T(4,128)S(1)} %pad_maximum_fusion), channel_id=1, source_target_pairs={{1,0},{2,1},{3,2},{4,3},{5,4},{6,5},{7,6},{8,7},{9,8},{10,9},{11,1... | collective-permute-start | bytes 46088 | tf_op jit(solution)/shard_map/ppermute | solution.py:460

commit v2 on v1

v2 whole, which is shorter than its diff:
```python
import functools

import jax
import jax.numpy as jnp
from jax import lax
from jax.experimental import pallas as pl
from jax.experimental.pallas import tpu as pltpu
from jax.sharding import PartitionSpec as P

f32 = jnp.float32
bf16 = jnp.bfloat16

TOKENS = 256
SUB = 128
HEADS = 16
HEAD_DIM = 64
STATE = 128
WIDTH = HEADS * HEAD_DIM
PAIRS = HEADS // 2
RIM = 3
RANKS = 16
SIDE = 4
QUARTER = HEADS // SIDE
ROWMSG = 80
CHUNK = 144
ALL = WIDTH + 2 * STATE
PART = 256
PARTS = WIDTH // PART
NEG = -1e30
CODE_SPAN = 248.0

NN = ((1,), (0,))
NT = ((1,), (1,))
TN = ((0,), (0,))


def dot(a, b, dims=NN):
    return lax.dot_general(a, b, (dims, ((), ())), preferred_element_type=f32)


def split2(v):
    hi = v.astype(bf16)
    return hi, (v - hi.astype(f32)).astype(bf16)


def split3(v):
    hi = v.astype(bf16)
    rest = v - hi.astype(f32)
    mid = rest.astype(bf16)
    return hi, mid, (rest - mid.astype(f32)).astype(bf16)


def dot3(a, b, dims=NN):
    return dot(a[0], b[0], dims) + dot(a[1], b[0], dims) + dot(a[0], b[1], dims)


def iota(shape, axis):
    return lax.broadcasted_iota(jnp.int32, shape, axis)


def onehot(mask):
    return jnp.where(mask, 1.0, 0.0).astype(bf16)


def to_column(row):
    n = row.shape[1]
    eye = iota((n, n), 0) == iota((n, n), 1)
    return jnp.sum(jnp.where(eye, row, 0.0), axis=1, keepdims=True)


def low_half(shape):
    return iota(shape, 1) < HEAD_DIM


def swap_halves(v):
    return pltpu.roll(v, HEAD_DIM, 1)


def encode(v):
    top = jnp.max(jnp.abs(v), axis=0, keepdims=True)
    scale = (jnp.maximum(top, 1e-30) * 1.01).astype(bf16).astype(f32)
    unit = jnp.abs(v) * (CODE_SPAN / scale)
    size = jnp.exp2(unit - CODE_SPAN / 2)
    return jnp.where(v < 0, -size, size).astype(bf16), scale


def decode(code, scale):
    v = code.astype(f32)
    unit = jnp.log2(jnp.abs(v)) + CODE_SPAN / 2
    size = unit * (scale * (1.0 / CODE_SPAN))
    return jnp.where(v < 0, -size, size)


def split_heads(pair):
    top, bottom = pair[:HEAD_DIM], pair[HEAD_DIM:]
    low = low_half(top.shape)
    return (
        jnp.where(low, top, swap_halves(bottom)),
        jnp.where(low, swap_halves(top), bottom),
    )


def join_heads(first, second):
    low = low_half(first.shape)
    return (
        jnp.where(low, first, swap_halves(second)),
        jnp.where(low, swap_halves(first), second),
    )


def stack_columns(arrays):
    stacked = jnp.concatenate(list(arrays), axis=0)
    parts = [p.astype(f32) for p in split3(stacked)]
    rows = 3 * stacked.shape[0]
    full = 128 if rows <= 128 else 256
    parts.append(jnp.zeros((full - rows, TOKENS), f32))
    return jnp.concatenate(parts, axis=0).T.astype(bf16)


def spread_matrix(count, full, which, first_head, lanes_per_head, lanes):
    r, l = iota((full, lanes), 0), iota((full, lanes), 1)
    rows = r - (r // (count * HEADS)) * (count * HEADS)
    return onehot((r < 3 * count * HEADS) & (rows - l // lanes_per_head == which * HEADS + first_head))


def sum_matrix(rows, offset):
    r, l = iota((rows, 128), 0), iota((rows, 128), 1)
    return onehot(r // HEAD_DIM + offset == l)


def decay_terms(cum, step):
    first = iota(cum.shape, 1) < SUB
    end0 = cum[:, SUB - 1 : SUB]
    end1 = cum[:, TOKENS - 1 : TOKENS]
    inner = jnp.exp(cum)
    outer = jnp.exp(jnp.where(first, end0, end1) - cum) * step
    from_start = jnp.where(first, inner, inner * jnp.exp(end0))
    to_end = jnp.where(first, outer * jnp.exp(end1), outer)
    return inner, outer, from_start, to_end, end0 + end1


def begin(moves, sems):
    copies = [pltpu.make_async_copy(a, b, sems.at[n]) for n, (a, b) in enumerate(moves)]
    for copy in copies:
        copy.start()
    return copies


def wait(copies):
    for copy in copies:
        copy.wait()


def part(n):
    return pl.ds(n * PART, PART)


def silu_of(v):
    return v / (1.0 + jnp.exp(-v))


def slope_of(v):
    gate = 1.0 / (1.0 + jnp.exp(-v))
    return v * gate, gate * (1.0 + v * (1.0 - gate))


def conv_rows(rows_scr, taps, lanes):
    v = taps[0:1] * rows_scr[8 - RIM : 8 - RIM + TOKENS, lanes]
    for k in range(1, RIM + 1):
        v += taps[k : k + 1] * rows_scr[8 - RIM + k : 8 - RIM + k + TOKENS, lanes]
    return v


B_LANES = pl.ds(WIDTH, STATE)
C_LANES = pl.ds(WIDTH + STATE, STATE)


def edge_kernel(x_raw, b_raw, c_raw, edge, scr, sems):
    rows = pl.ds(TOKENS - 16, 16)
    wait(
        begin(
            [
                (x_raw.at[rows, :], scr.at[:, pl.ds(0, WIDTH)]),
                (b_raw.at[rows, :], scr.at[:, B_LANES]),
                (c_raw.at[rows, :], scr.at[:, C_LANES]),
            ],
            sems,
        )
    )
    edge[...] = scr[...].astype(f32)[16 - RIM :].astype(bf16)


def first_kernel(
    xs, gs, bs, cs, dts, bias, rate, taps_x, taps_b, taps_c,
    sg, pre16, end16, ge16, taps_out, total_out, cum_out, step_out, columns_out,
    rows_scr,
):
    pre = dts[...].astype(f32) + to_column(bias[...])
    step = jnp.maximum(pre, 0.0) + jnp.log1p(jnp.exp(-jnp.abs(pre)))
    log_decay = -jnp.exp(to_column(rate[...])) * step
    r, c = iota((TOKENS, TOKENS), 0), iota((TOKENS, TOKENS), 1)
    upto = onehot((r <= c) & (r // SUB == c // SUB))
    parts = split3(log_decay)
    cum = dot(parts[2], upto) + dot(parts[1], upto) + dot(parts[0], upto)
    cum_out[...] = cum
    step_out[...] = step
    _, _, from_start, to_end, total = decay_terms(cum, step)
    for head in range(HEADS):
        total_out[head] = jnp.broadcast_to(total[head : head + 1], (8, 128))
    columns = stack_columns([from_start, to_end])
    columns_out[...] = columns
    taps_out[:, 0:WIDTH] = taps_x[...]
    taps_out[:, WIDTH : WIDTH + STATE] = taps_b[...]
    taps_out[:, WIDTH + STATE :] = taps_c[...]
    rows_scr[0:8, :] = jnp.zeros((8, ALL), f32)
    known = iota((TOKENS, 128), 0) >= 16
    turned = []
    for raw, taps, lanes in ((bs, taps_b, B_LANES), (cs, taps_c, C_LANES)):
        rows_scr[8:, lanes] = raw[...].astype(f32)
        v = conv_rows(rows_scr, taps[...], lanes)
        pre16[:, lanes] = v[:16]
        turned.append(split2(jnp.where(known, silu_of(v), 0.0).T))
    bt, ct = turned
    for n in range(PARTS):
        lanes = part(n)
        heads = n * PART // HEAD_DIM
        start_x = dot(columns, spread_matrix(2, 128, 0, heads, HEAD_DIM, PART))
        end_x = dot(columns, spread_matrix(2, 128, 1, heads, HEAD_DIM, PART))
        rows_scr[8:, lanes] = xs[:, lanes].astype(f32)
        v = conv_rows(rows_scr, taps_x[:, lanes], lanes)
        pre16[:, lanes] = v[:16]
        end16[:, lanes] = end_x[:16]
        xw = silu_of(v) * end_x
        ge = gs[:, lanes].astype(f32) * start_x
        ge16[:, lanes] = ge[:16]
        sg[0, :, lanes] = dot3(bt, split2(xw))
        sg[1, :, lanes] = dot3(ct, split2(ge))


def quarter(q):
    return pl.ds(pl.multiple_of(q * PART, PART), PART)


def place():
    here = lax.axis_index("context")
    return lax.rem(here, SIDE), lax.div(here, SIDE)


def write_aux(scales, total):
    at = iota((16, 128), 0)
    aux = jnp.where(at == 0, scales[0], scales[-1])
    for m, piece in enumerate(split3(total)):
        aux = jnp.where(at == 2 + m, piece.astype(f32), aux)
    return aux.astype(bf16)


def send_kernel(before, sg, pre16, end16, ge16, taps, total, *refs):
    pays, (xw_scr, ge_scr) = refs[:SIDE], refs[SIDE:]
    halo = before[...].astype(f32)
    v = pre16[...]
    at = iota((16, ALL), 0)
    for row in range(RIM):
        more = taps[0:1] * halo[row : row + 1]
        for k in range(1, RIM - row):
            more += taps[k : k + 1] * halo[row + k : row + k + 1]
        v += jnp.where(at == row, more, 0.0)
    act = silu_of(v)
    xw_scr[...] = act[:, :WIDTH] * end16[...]
    ge_scr[...] = ge16[...]
    b = split2(act[:, WIDTH : WIDTH + STATE])
    c = split2(act[:, WIDTH + STATE :])
    x, _ = place()
    for shift, pay in enumerate(pays):
        q = lax.rem(x + shift, SIDE)
        lanes = quarter(q)
        s = sg[0, :, lanes] + dot3(b, split2(xw_scr[:, lanes]), TN)
        g = sg[1, :, lanes] + dot3(c, split2(ge_scr[:, lanes]), TN)
        for half in range(PART // 128):
            s_heads = split_heads(s[:, half * 128 : half * 128 + 128])
            g_heads = split_heads(g[:, half * 128 : half * 128 + 128])
            for k in range(2):
                slot = 2 * half + k
                s_code, s_scale = encode(s_heads[k])
                g_code, g_scale = encode(g_heads[k])
                pay[slot, 0:64, :] = s_code
                pay[slot, 64:128, :] = g_code
                pay[slot, 128:144, :] = write_aux((s_scale, g_scale), total[q * QUARTER + slot][0:1])


def row_kernel(*refs):
    pays, tick, refs = refs[:SIDE], refs[SIDE], refs[SIDE + 1 :]
    (*sends, s_out, g_out, d_out) = refs
    x, y = place()
    for shift, pay in enumerate(pays):
        source = lax.rem(x - shift + SIDE, SIDE)
        for k in range(QUARTER):
            aux = pay[k, 128:144, :].astype(f32)
            s_out[source, k] = decode(pay[k, 0:64, :], aux[0:1])
            g_out[source, k] = decode(pay[k, 64:128, :], aux[1:2])
            d_out[source, k] = jnp.broadcast_to(aux[2:3] + aux[3:4] + aux[4:5], (8, 128))
    for k in range(QUARTER):
        s_run, g_run = s_out[0, k], g_out[SIDE - 1, k]
        for n in range(1, SIDE):
            s_run = jnp.exp(d_out[n, k][0:1]) * s_run + s_out[n, k]
            m = SIDE - 1 - n
            g_run = jnp.exp(d_out[m, k][0:1]) * g_run + g_out[m, k]
        total = sum(d_out[n, k][0:1] for n in range(SIDE))
        for shift, message in enumerate(sends, 1):
            code, scale = encode(jnp.where(y + shift < SIDE, s_run, g_run))
            message[k, 0:64, :] = code
            message[k, 64:80, :] = write_aux((scale,), total)


def column_kernel(*refs):
    rows, (s_in, g_in, d_in, tick), refs = refs[: SIDE - 1], refs[SIDE - 1 : SIDE + 3], refs[SIDE + 3 :]
    backs, (row_scr, decay_scr, code_scr) = refs[:SIDE], refs[SIDE:]
    x, y = place()
    row_scr[...] = jnp.zeros_like(row_scr)
    decay_scr[...] = jnp.zeros_like(decay_scr)
    for shift, row in enumerate(rows, 1):
        source = lax.rem(y - shift + SIDE, SIDE)
        for k in range(QUARTER):
            aux = row[k, 64:80, :].astype(f32)
            row_scr[source, k] = decode(row[k, 0:64, :], aux[0:1])
            decay_scr[source, k] = jnp.broadcast_to(jnp.exp(aux[2:3] + aux[3:4] + aux[4:5]), (8, 128))
    for k in range(QUARTER):
        e_run = jnp.zeros((HEAD_DIM, 128), f32)
        f_run = jnp.zeros((HEAD_DIM, 128), f32)
        for n in range(SIDE):
            e_run = jnp.where(n < y, decay_scr[n, k][0:1] * e_run + row_scr[n, k], e_run)
            m = SIDE - 1 - n
            f_run = jnp.where(m > y, decay_scr[m, k][0:1] * f_run + row_scr[m, k], f_run)
        scales = [[None, None] for _ in range(SIDE)]
        for n in range(SIDE):
            m = SIDE - 1 - n
            code_scr[n, k, 0:64, :], scales[n][0] = encode(e_run)
            code_scr[m, k, 64:128, :], scales[m][1] = encode(f_run)
            e_run = jnp.exp(d_in[n, k][0:1]) * e_run + s_in[n, k]
            f_run = jnp.exp(d_in[m, k][0:1]) * f_run + g_in[m, k]
        at = iota((16, 128), 0)
        for n in range(SIDE):
            code_scr[n, k, 128:144, :] = jnp.where(at == 0, scales[n][0], scales[n][1]).astype(bf16)
    for shift, back in enumerate(backs):
        back[...] = code_scr[lax.rem(x + shift, SIDE)]


def block_kernel(
    first_pair, xs, gs, bs, cs, before, taps, cums, steps, after_this, skip,
    ys, dxs, slopes, xws, ges, bcs, slopes_bc, dbcs, sums,
    rows_scr, ds_scr, off_scr, diag_scr, cols_scr, pick_scr, sc_scr, row_scr, acc_scr,
):
    cum, step = cums[...], steps[...]
    shifted = cum - jnp.log(step)
    for head in range(HEADS):
        row_scr[head] = jnp.broadcast_to(cum[head : head + 1], (8, TOKENS))
        row_scr[HEADS + head] = jnp.broadcast_to(shifted[head : head + 1], (8, TOKENS))
    inner, outer, from_start, to_end, _ = decay_terms(cum, step)
    stacked = []
    for n, v in enumerate((cum, shifted, inner, outer, step, from_start, to_end)):
        stacked += [p.astype(f32) for p in split3(v)[: 3 if n < 2 else 2]]
    cols_scr[...] = jnp.concatenate(stacked, axis=0).T
    r, l = iota((256, 256), 0), iota((256, 256), 1)
    same = r % 2 == l // 128
    pick_scr[:, 0:256] = onehot((r < 48) & same)
    pick_scr[:, 256:512] = onehot((r >= 48) & (r < 96) & same)
    r, l = iota((256, 128), 0), iota((256, 128), 1)
    same = r % 2 == l // HEAD_DIM
    for n in range(5):
        pick_scr[:, 512 + 128 * n : 640 + 128 * n] = onehot(((r - 96) // 32 == n) & (r >= 96) & same)
    pair_of = (iota((TOKENS, 256), 1) % HEADS) // 2
    column = iota((256, 128), 1) - (iota((256, 128), 0) // HEAD_DIM) % 2
    rows_scr[8 - RIM : 8, :] = before[...].astype(f32)
    for n, (raw, lanes) in enumerate(((bs, B_LANES), (cs, C_LANES))):
        rows_scr[8:, lanes] = raw[...].astype(f32)
        act, slope = slope_of(conv_rows(rows_scr, taps[:, lanes], lanes))
        bcs[:, n * STATE : n * STATE + STATE] = act
        slopes_bc[:, n * STATE : n * STATE + STATE] = slope
    b, c = bcs[:, :STATE], bcs[:, STATE:]
    r, l = iota((SUB, SUB), 0), iota((SUB, SUB), 1)
    b2, c2 = split2(b), split2(c)

    def rows(parts, s):
        return tuple(p[s * SUB : s * SUB + SUB] for p in parts)

    for s in range(2):
        sc_scr[s] = jnp.where(r > l, dot3(rows(c2, s), rows(b2, s), NT), 0.0)
        sc_scr[2 + s] = jnp.where(l > r, dot3(rows(b2, s), rows(c2, s), NT), 0.0)
    off_scr[0] = jnp.concatenate(split2(dot3(rows(c2, 1), rows(b2, 0), NT)), axis=1)
    off_scr[1] = jnp.concatenate(split2(dot3(rows(b2, 0), rows(c2, 1), NT)), axis=1)
    ds_scr[...] = jnp.zeros_like(ds_scr)
    acc_scr[...] = jnp.zeros_like(acc_scr)
    diag = jnp.broadcast_to(jnp.sum(b * c, axis=1, keepdims=True), (TOKENS, 128))
    diag_scr[0] = diag
    diag_scr[1] = jnp.zeros((TOKENS, 128), f32)
    low = low_half((SUB, 128))
    zero = jnp.zeros((SUB, 128), bf16)

    def twice(hi, lo):
        return jnp.concatenate([jnp.concatenate([hi, lo], axis=1), jnp.concatenate([hi, zero], axis=1)], axis=0)

    def fold(v):
        return v[:, :128] + v[:, 128:]

    def pair_step(pair):
        lanes = pl.ds(pair * 128, 128)
        local = pl.ds((pair - first_pair) * 128, 128)
        head = 2 * pair
        rows_scr[8:, lanes] = xs[:, lanes].astype(f32)
        x, slope = slope_of(conv_rows(rows_scr, taps[:, lanes], lanes))
        slopes[:, local] = slope
        g = gs[:, lanes]
        gf = g.astype(f32)
        xh, xl = split2(x)
        cols = jnp.where(pair_of == pair, cols_scr[...], 0.0).astype(bf16)
        cum_cols = dot(cols, pick_scr[:, 0:256])
        shifted_cols = dot(cols, pick_scr[:, 256:512])
        inner_x, outer_x = (dot(cols, pick_scr[:, a : a + 128]) for a in (512, 640))
        step_x, start_x, end_x = (dot(cols, pick_scr[:, a : a + 128]) for a in (768, 896, 1024))
        for n, piece in enumerate(split2(x * end_x)):
            xws[n, :, local] = piece
        for n, piece in enumerate(split2(gf * start_x)):
            ges[n, :, local] = piece
        y_parts, dx_parts = [], []
        for s in range(2):
            at = slice(s * SUB, s * SUB + SUB)
            xh_s, xl_s, g_s = xh[at], xl[at], g[at]
            ms, ts, decays = [], [], []
            for k in range(2):
                row_cum = row_scr[head + k][0:1, at]
                row_shift = row_scr[HEADS + head + k][0:1, at]
                col_cum = cum_cols[at, k * 128 : k * 128 + 128]
                col_shift = shifted_cols[at, k * 128 : k * 128 + 128]
                decay = jnp.exp(jnp.where(r > l, col_cum - row_shift, NEG))
                decay_t = jnp.exp(jnp.where(l > r, row_cum - col_shift, NEG))
                decays.append(decay)
                ms.append(jnp.concatenate(split2(sc_scr[s] * decay), axis=1))
                ts.append(jnp.concatenate(split2(sc_scr[2 + s] * decay_t), axis=1))
            y2 = fold(dot(jnp.concatenate(ms, axis=0), twice(xh_s, xl_s)))
            dx2 = dot(jnp.concatenate(ts, axis=0), jnp.concatenate([g_s, g_s], axis=0))
            gf_s = g_s.astype(f32)
            g0 = jnp.where(low, gf_s, 0.0).astype(bf16)
            g1 = jnp.where(low, 0.0, gf_s).astype(bf16)
            g01 = jnp.concatenate([g0, g1], axis=0)
            dm = dot(jnp.concatenate([g01, g01], axis=1), jnp.concatenate([xh_s, xl_s], axis=1), NT)
            ds_scr[s] += dm[:SUB] * decays[0] + dm[SUB:] * decays[1]
            y_parts.append(jnp.where(low, y2[:SUB], y2[SUB:]))
            dx_parts.append(jnp.where(low, dx2[:SUB], dx2[SUB:]))
        xwh, xwl = split2(x[:SUB] * outer_x[:SUB])
        geh, gel = split2(gf[SUB:] * inner_x[SUB:])
        y_parts[1] += inner_x[SUB:] * fold(dot(off_scr[0], twice(xwh, xwl)))
        dx_parts[0] += outer_x[:SUB] * fold(dot(off_scr[1], twice(geh, gel)))
        ds_scr[2] += dot(jnp.concatenate([geh, gel], axis=1), jnp.concatenate([xwh, xwh], axis=1), NT) + dot(geh, xwl, NT)
        y = jnp.concatenate(y_parts, axis=0)
        dx = jnp.concatenate(dx_parts, axis=0)
        xg = x * gf
        xdx = x * dx
        total = acc_scr[...]
        for n, v in enumerate((gf * y - xdx, xdx, xg)):
            hot = onehot(column == n * HEADS + head)
            total += dot(jnp.concatenate(split2(v), axis=1), hot)
        acc_scr[...] = total
        diag_scr[1] += step_x * xg
        direct = jnp.where(low_half((TOKENS, 128)), skip[0, head], skip[0, head + 1]) + diag_scr[0] * step_x
        ys[:, local] = y + direct * x
        dxs[:, local] = dx + direct * gf

    for pair in range(first_pair, first_pair + PAIRS // 2):
        pair_step(pair)
    d_diag = jnp.sum(diag_scr[1], axis=1, keepdims=True)
    db = d_diag * c
    dc = d_diag * b
    for s in range(2):
        ds = jnp.where(r > l, ds_scr[s], 0.0)
        d2 = split2(ds)
        t2 = split2(ds.T)
        at = slice(s * SUB, s * SUB + SUB)
        dc_s = dc[at] + dot3(d2, rows(b2, s))
        db_s = db[at] + dot3(t2, rows(c2, s))
        if s == 0:
            db_s += dot3(split2(ds_scr[2].T), rows(c2, 1))
        else:
            dc_s += dot3(split2(ds_scr[2]), rows(b2, 0))
        dbcs[at, :STATE] = db_s
        dbcs[at, STATE:] = dc_s
    turned = acc_scr[...].T
    sums[0] = turned[0:HEADS]
    sums[1] = turned[HEADS : 2 * HEADS] / step + diag_scr[0].T[0:1] * turned[2 * HEADS : 3 * HEADS]


def wide_product(a2, cat, lanes):
    return dot(jnp.concatenate([a2[0], a2[0]], axis=1), cat[:, lanes]) + dot(a2[1], cat[:STATE, lanes])


def both_halves(n):
    per = PARTS // 2
    return n // per, pl.ds((n % per) * PART, PART)


def rim_kernel(*refs):
    backs, refs = refs[:SIDE], refs[SIDE:]
    bc, dx0, dx1, slope0, slope1, slope_bc, dbc0, dbc1, xw0, xw1, ge0, ge1, end16, e_cat, f_cat, rim = refs
    x, _ = place()
    for shift, back in enumerate(backs):
        q = lax.rem(x - shift + SIDE, SIDE)
        blocks = [[], []]
        for half in range(PART // 128):
            codes = []
            for k in range(2):
                slot = 2 * half + k
                aux = back[slot, 128:144, :].astype(f32)
                codes.append((decode(back[slot, 0:64, :], aux[0:1]), decode(back[slot, 64:128, :], aux[1:2])))
            for n in range(2):
                blocks[n].append(jnp.concatenate(join_heads(codes[0][n], codes[1][n]), axis=0))
        for n, cat in enumerate((e_cat, f_cat)):
            hi, lo = split2(jnp.concatenate(blocks[n], axis=1))
            cat[:STATE, quarter(q)] = hi
            cat[STATE:, quarter(q)] = lo
    b2 = split2(bc[0:16, :STATE])
    for n in range(PARTS):
        side, lanes = both_halves(n)
        dx, slope = ((dx0, slope0), (dx1, slope1))[side]
        d = (dx[0:16, lanes] + end16[:, part(n)] * wide_product(b2, f_cat, part(n))) * slope[0:16, lanes]
        rim[:, n * PART : n * PART + PART] = d[:RIM]
    for n, (v, cat) in enumerate((((xw0, xw1), f_cat), ((ge0, ge1), e_cat))):
        hi, lo = (jnp.concatenate([v[0][m, 0:16, :], v[1][m, 0:16, :]], axis=1) for m in range(2))
        both = dot(hi, cat[...], NT)
        d = both[:, :STATE] + both[:, STATE:] + dot(lo, cat[:STATE], NT)
        cut = slice(n * STATE, n * STATE + STATE)
        d = (dbc0[0:16, cut] + dbc1[0:16, cut] + d) * slope_bc[0:16, cut]
        rim[:, WIDTH + n * STATE : WIDTH + n * STATE + STATE] = d[:RIM]


def main_kernel(
    e_cat, f_cat, columns, bc, y0, y1, dx0, dx1, slope0, slope1, ge0, ge1, xw0, xw1, dbc0, dbc1, slope_bc,
    sums0, sums1, cums, steps, dts, bias, rate,
    y_out, dpre, dpre_bc, dt_out,
    ys, gdt, out_sems,
):
    b2, c2 = split2(bc[:, :STATE]), split2(bc[:, STATE:])
    grads = [[jnp.zeros((TOKENS, PART), f32), jnp.zeros((TOKENS, STATE), f32)] for _ in range(2)]
    total = jnp.zeros((TOKENS, 128), f32)
    both = jnp.zeros((8, 128), f32)
    out = []
    for n in range(PARTS):
        lanes = part(n)
        heads = n * PART // HEAD_DIM
        side, own = both_halves(n)
        y_in, dx, slope, ge, xw = ((y0, dx0, slope0, ge0, xw0), (y1, dx1, slope1, ge1, xw1))[side]
        start_x = dot(columns[...], spread_matrix(2, 128, 0, heads, HEAD_DIM, PART))
        end_x = dot(columns[...], spread_matrix(2, 128, 1, heads, HEAD_DIM, PART))
        ce = wide_product(c2, e_cat, lanes)
        bf = wide_product(b2, f_cat, lanes)
        ys[:, lanes] = y_in[:, own] + start_x * ce
        copy = pltpu.make_async_copy(ys.at[:, lanes], y_out.at[:, lanes], out_sems.at[n])
        copy.start()
        out.append(copy)
        dpre[:, lanes] = (dx[:, own] + end_x * bf) * slope[:, own]
        for grad, v, cat in zip(grads, (xw, ge), (f_cat, e_cat)):
            grad[0] += dot(v[0, :, own], cat[:, lanes], NT)
            grad[1] += dot(v[1, :, own], cat[:STATE, lanes], NT)
        for v, product, offset in ((xw, bf, 0), (ge, ce, HEADS)):
            hi, lo = split2((v[0, :, own].astype(f32) + v[1, :, own].astype(f32)) * product)
            hot = sum_matrix(PART, offset + heads)
            total += dot(hi, hot) + dot(lo, hot)
        e = e_cat[:STATE, lanes].astype(f32) + e_cat[STATE:, lanes].astype(f32)
        f = f_cat[:STATE, lanes].astype(f32) + f_cat[STATE:, lanes].astype(f32)
        hi, lo = split2(jnp.broadcast_to(jnp.sum(e * f, axis=0, keepdims=True), (8, PART)))
        hot = sum_matrix(PART, heads)
        both += dot(hi, hot) + dot(lo, hot)
    for n, grad in enumerate(grads):
        cut = slice(n * STATE, n * STATE + STATE)
        d = dbc0[:, cut] + dbc1[:, cut] + grad[0][:, :STATE] + grad[0][:, STATE:] + grad[1]
        dpre_bc[:, cut] = d * slope_bc[:, cut]
    turned = total.T
    later, kept = turned[0:HEADS], turned[HEADS : 2 * HEADS]
    r, c = iota((TOKENS, TOKENS), 0), iota((TOKENS, TOKENS), 1)
    suffix = onehot(r >= c)
    prefix = onehot(r < c)

    def summed(v, tri):
        hi, mid, lo = split3(v)
        return dot(lo, tri) + dot(mid, tri) + dot(hi, tri)

    cum, step = cums[...], steps[...]
    ends = jnp.exp(cum[:, SUB - 1 : SUB] + cum[:, TOKENS - 1 : TOKENS])
    local = sums0[0] + sums1[0]
    direct = sums0[1] + sums1[1]
    d_decay = summed(local + kept, suffix) + summed(later, prefix) + ends * to_column(both[0:1, 0:HEADS])
    d_step = direct + later / step - jnp.exp(to_column(rate[...])) * d_decay
    pre = dts[...].astype(f32) + to_column(bias[...])
    gdt[...] = d_step / (1.0 + jnp.exp(-pre))
    out.append(pltpu.make_async_copy(gdt, dt_out, out_sems.at[PARTS]))
    out[-1].start()
    wait(out)


def settle_kernel(dpre, dpre_bc, after, taps, gx_out, gb_out, gc_out, rows_scr, gx, gb, gc, out_sems):
    out = []

    def send(src, dst):
        copy = pltpu.make_async_copy(src, dst, out_sems.at[len(out)])
        copy.start()
        out.append(copy)

    rows_scr[TOKENS : TOKENS + RIM, :] = after[...]

    def unconv(d, lanes):
        rows_scr[0:TOKENS, lanes] = d
        v = taps[RIM : RIM + 1, lanes] * d
        for k in range(RIM):
            v += taps[k : k + 1, lanes] * rows_scr[RIM - k : RIM - k + TOKENS, lanes]
        return v

    for n in range(PARTS):
        lanes = part(n)
        gx[:, lanes] = unconv(dpre[:, lanes], lanes)
        send(gx.at[:, lanes], gx_out.at[:, lanes])
    gb[...] = unconv(dpre_bc[:, :STATE], B_LANES)
    send(gb, gb_out)
    gc[...] = unconv(dpre_bc[:, STATE:], C_LANES)
    send(gc, gc_out)
    wait(out)


VMEM = pl.BlockSpec(memory_space=pltpu.VMEM)
SMEM = pl.BlockSpec(memory_space=pltpu.SMEM)
HBM = pl.BlockSpec(memory_space=pltpu.HBM)


def call(kernel, ins, outs, scratch=(), sems=(), flops=0, mib=20):
    shapes = [jax.ShapeDtypeStruct(s, d) for s, d, _ in outs]
    moved = sum(a.size * a.dtype.itemsize for a, _ in ins) + sum(s.size * s.dtype.itemsize for s in shapes)
    return pl.pallas_call(
        kernel,
        out_shape=shapes,
        in_specs=[w for _, w in ins],
        out_specs=[w for _, _, w in outs],
        scratch_shapes=[pltpu.VMEM(s, d) for s, d in scratch] + [pltpu.SemaphoreType.DMA((n,)) for n in sems],
        compiler_params=pltpu.CompilerParams(vmem_limit_bytes=mib * 1024 * 1024),
        cost_estimate=pl.CostEstimate(flops=flops, bytes_accessed=moved, transcendentals=0),
    )(*[a for a, _ in ins])


def along_row(block, shift):
    return lax.ppermute(
        block, "context", [(SIDE * y + x, SIDE * y + (x + shift) % SIDE) for y in range(SIDE) for x in range(SIDE)]
    )


def along_column(block, shift):
    return lax.ppermute(
        block, "context", [(SIDE * y + x, SIDE * ((y + shift) % SIDE) + x) for y in range(SIDE) for x in range(SIDE)]
    )


def on_device(
    x_raw, b_raw, c_raw, dt_raw, dt_bias, a_log, skip_gain, conv_x, conv_b, conv_c, grad_y
):
    wide, slim, bc, narrow = (TOKENS, WIDTH), (HEADS, TOKENS), (TOKENS, 2 * STATE), (TOKENS, STATE)
    rim16, row = (16, WIDTH), (1, HEADS)
    dt_bias, a_log, skip_gain = (v.reshape(row) for v in (dt_bias, a_log, skip_gain))

    def near(*arrays):
        return [(a, VMEM) for a in arrays]

    (edge,) = call(
        edge_kernel, [(a, HBM) for a in (x_raw, b_raw, c_raw)], [((RIM, ALL), bf16, VMEM)], [((16, ALL), bf16)], [3],
        mib=60,
    )
    before = lax.ppermute(edge, "context", [(i, i + 1) for i in range(RANKS - 1)])
    sg, pre16, end16, ge16, taps, total, cum, step, columns = call(
        first_kernel,
        near(x_raw, grad_y, b_raw, c_raw, dt_raw, dt_bias, a_log, conv_x, conv_b, conv_c),
        [((2, STATE, WIDTH), f32, VMEM), ((16, ALL), f32, VMEM), (rim16, f32, VMEM), (rim16, f32, VMEM),
         ((4, ALL), f32, VMEM), ((HEADS, 8, 128), f32, VMEM), (slim, f32, VMEM), (slim, f32, VMEM),
         ((TOKENS, 128), bf16, VMEM)],
        [((TOKENS + 8, ALL), f32)],
        flops=2_000_000_000,
    )
    message = ((QUARTER, CHUNK, 128), bf16, VMEM)
    pays = call(
        send_kernel, near(before, sg, pre16, end16, ge16, taps, total), [message] * SIDE, [(rim16, f32), (rim16, f32)]
    )

    def block(first_pair, after_this):
        half = (TOKENS, WIDTH // 2)
        return call(
            functools.partial(block_kernel, first_pair),
            near(x_raw, grad_y, b_raw, c_raw, before, taps, cum, step, after_this) + [(skip_gain, SMEM)],
            [(half, f32, VMEM)] * 3 + [((2,) + half, bf16, VMEM)] * 2 + [(bc, f32, VMEM)] * 3
            + [((2,) + slim, f32, VMEM)],
            [((TOKENS + 8, ALL), f32), ((3, SUB, SUB), f32), ((2, SUB, 2 * SUB), bf16), ((2, TOKENS, 128), f32),
             ((TOKENS, 256), f32), ((256, 1152), bf16), ((4, SUB, SUB), f32), ((2 * HEADS, 8, TOKENS), f32),
             ((TOKENS, 128), f32)],
            flops=4_000_000_000,
        )

    got = [pays[0]] + [along_row(pays[shift], shift) for shift in (1, 2, 3)]
    y0, dx0, slope0, xw0, ge0, bcs, slope_bc, dbc0, sums0 = block(0, pays[0])
    *sends, s_all, g_all, d_all = call(
        row_kernel,
        near(*got, sums0),
        [((QUARTER, ROWMSG, 128), bf16, VMEM)] * (SIDE - 1)
        + [((SIDE, QUARTER, HEAD_DIM, 128), f32, VMEM)] * 2 + [((SIDE, QUARTER, 8, 128), f32, VMEM)],
    )
    rows = [along_column(sends[shift - 1], shift) for shift in (1, 2, 3)]
    y1, dx1, slope1, xw1, ge1, _, _, dbc1, sums1 = block(PAIRS // 2, d_all)
    answers = call(
        column_kernel,
        near(*rows, s_all, g_all, d_all, sums1),
        [message] * SIDE,
        [((SIDE, QUARTER, HEAD_DIM, 128), f32), ((SIDE, QUARTER, 8, 128), f32), ((SIDE, QUARTER, CHUNK, 128), bf16)],
    )
    backs = [answers[0]] + [along_row(answers[shift], shift) for shift in (1, 2, 3)]
    cat = ((2 * STATE, WIDTH), bf16)
    e_cat, f_cat, rim = call(
        rim_kernel,
        near(*backs, bcs, dx0, dx1, slope0, slope1, slope_bc, dbc0, dbc1, xw0, xw1, ge0, ge1, end16),
        [(*cat, VMEM), (*cat, VMEM), ((RIM, ALL), f32, VMEM)],
    )
    after = lax.ppermute(rim, "context", [(i, i - 1) for i in range(1, RANKS)])
    y_out, dpre, dpre_bc, grad_dt = call(
        main_kernel,
        near(e_cat, f_cat, columns, bcs, y0, y1, dx0, dx1, slope0, slope1, ge0, ge1, xw0, xw1, dbc0, dbc1, slope_bc,
             sums0, sums1, cum, step, dt_raw, dt_bias, a_log),
        [(wide, f32, HBM), (wide, f32, VMEM), (bc, f32, VMEM), (slim, f32, HBM)],
        [(wide, f32), (slim, f32)],
        [PARTS + 1],
        flops=2_000_000_000,
    )
    grad_x, grad_b, grad_c = call(
        settle_kernel,
        near(dpre, dpre_bc, after, taps),
        [(wide, f32, HBM), (narrow, f32, HBM), (narrow, f32, HBM)],
        [((TOKENS + 8, ALL), f32), (wide, f32), (narrow, f32), (narrow, f32)],
        [PARTS + 2],
    )
    return (y_out, grad_x, grad_b, grad_c, grad_dt)


def solution(mesh):
    tokens = P(("dp", "context"), "tensor")
    heads = P("tensor", ("dp", "context"))
    one, taps = P("tensor"), P(None, "tensor")
    return jax.shard_map(
        on_device,
        mesh=mesh,
        in_specs=(tokens, tokens, tokens, heads, one, one, one, taps, taps, taps, tokens),
        out_specs=(tokens, tokens, tokens, tokens, heads),
        check_vma=False,
    )
```

time: 75.8 us -> 57.1 us (0.75)
  blocking collectives: 16.4 us -> 0 us
  local copies, waits for them, and re-layouts: 13.2 us -> 3.04 us
  starting transfers between devices: 11.7 us -> 17.9 us
  waiting for transfers between devices: 7.18 us -> 9.79 us
  Pallas kernels: 25.8 us -> 24.4 us
    all_to_all x1 -> x0, blocking collectives: 16.4 us -> none  [on_device(): got = lax.all_to_all(pay, 'context', 0, 0, tiled=True)]
    ppermute x0 -> x9, starting transfers between devices: none -> 12.3 us  [the longest x6 6.42 us: along_row(): lax.ppermute(block, 'context', [(SIDE * y + x, SIDE * y + (x + shift) % S...]
    unnamed x40 -> x24, local copies, waits for them, and re-layouts: 11.1 us -> 3.04 us
    ppermute x0 -> x9, waiting for transfers between devices: none -> 7.83 us  [the longest x6 7.82 us: along_row(): lax.ppermute(block, 'context', [(SIDE * y + x, SIDE * y + (x + shift) % S...]
    all_to_all x1 -> x0, starting transfers between devices: 5.58 us -> none  [on_device(): back = lax.all_to_all(answer, 'context', 0, 0, tiled=True)]
    ppermute x1, waiting for transfers between devices: 5.02 us -> 1.96 us  [on_device(): after = lax.ppermute(rim, 'context', [(i, i - 1) for i in range(1, RANKS)])]
    ppermute x1, waiting for transfers between devices: 2.16 us -> 0.01 us  [on_device(): lax.ppermute(edge, 'context', [(i, i + 1) for i in range(RANKS - 1)])]
    slice x5 -> x0, local copies, waits for them, and re-layouts: 2.12 us -> none  [the longest x3 2.11 us: on_device(): v[TOKENS - RIM:]]
  transfers between devices with their start and end apart: 3 -> 11, of which waited for: 2 -> 5; matrix products, arithmetic and copies ran while one was open for 0% -> 0% of each run, Pallas kernels for 15% -> 32%
where the time goes in v2:
time: 57.1 us; the launch traced here: 56.1 us
  Pallas kernels  24.4 us (43%)
  starting transfers between devices  17.9 us (31%)
  waiting for transfers between devices  9.79 us (17%)
  local copies, waits for them, and re-layouts  3.04 us (5%)
  between operations  1.03 us (2%)
    pallas_call x10, Pallas kernels, call(): pl.pallas_call(kernel, out_shape=shapes, in_specs=[w for _, w in ins], ou...  24.4 us
    ppermute x6, waiting for transfers between devices, along_row(): lax.ppermute(block, 'context', [(SIDE * y + x, SIDE * y + (x + shift) % S...  7.82 us
    ppermute x6, starting transfers between devices, along_row(): lax.ppermute(block, 'context', [(SIDE * y + x, SIDE * y + (x + shift) % S...  6.42 us
    ppermute x3, starting transfers between devices, along_column(): lax.ppermute(block, 'context', [(SIDE * y + x, SIDE * ((y + shift) % SIDE...  5.9 us
    ppermute x1, starting transfers between devices, on_device(): lax.ppermute(edge, 'context', [(i, i + 1) for i in range(RANKS - 1)])  3.4 us
    unnamed x24, local copies, waits for them, and re-layouts  3.04 us
    ppermute x1, starting transfers between devices, on_device(): after = lax.ppermute(rim, 'context', [(i, i - 1) for i in range(1, RANKS)])  2.16 us
    ppermute x1, waiting for transfers between devices, on_device(): after = lax.ppermute(rim, 'context', [(i, i - 1) for i in range(1, RANKS)])  1.96 us
  transfers between devices with their start and end apart: 11, of which 5 were waited for; matrix products, arithmetic and copies ran while one was open for 0% of the time, Pallas kernels for 32%

profile of v2, /device:TPU:38, one launch (start us, length us, event | category | flops | bytes accessed | tf_op | source)
XLA Modules:
  0.0 56.1 jit_solution(8417099143971847779)
XLA Ops:
  0.7 1.5 %shard_map.146 = bf16[3,1280]{1,0:T(4,128)(2,1)} custom-call(bf16[256,1024]{1,0:T(8,128)(2,1)} %xs.5, bf16[256,128]{1,0:T(8,128)(2,1)} %bs.5, bf16[256,128]{1,0:T(8,128)(2,1)} %cs.5), custom_call_target="tpu_custom_call" | custom-call | bytes 663040 | tf_op jit(solution)/shard_map/pallas_call | solution.py:633
  2.2 3.4 %collective-permute-start = (bf16[3,1280]{1,0:T(4,128)(2,1)}, bf16[3,1280]{1,0:T(4,128)(2,1)S(1)}, u32[]{:S(2)}, u32[]{:S(2)}) collective-permute-start(bf16[3,1280]{1,0:T(4,128)(2,1)} %shard_map.146), channel_id=1, source_target_pairs={{0,1},{1,2},{2,3},{3,4},{4,5},{5,6},{6,7},{7,8},{8,9},{9,10},{10,1... | collective-permute-start | bytes 23048 | tf_op jit(solution)/shard_map/ppermute | solution.py:670
  6.2 1.0 %copy-done.6 = bf16[256,1024]{1,0:T(8,128)(2,1)S(1)} copy-done((bf16[256,1024]{1,0:T(8,128)(2,1)S(1)}, bf16[256,1024]{1,0:T(8,128)(2,1)}, u32[]{:S(2)}) %copy-start.6) | copy-done | bytes 524312
  7.3 0.7 %copy-done.8 = f32[4,1024]{1,0:T(4,128)S(1)} copy-done((f32[4,1024]{1,0:T(4,128)S(1)}, f32[4,1024]{1,0:T(4,128)}, u32[]{:S(2)}) %copy-start.8) | copy-done | bytes 16408
  8.0 2.5 %shard_map.147 = (f32[2,128,1024]{2,1,0:T(8,128)S(1)}, f32[16,1280]{1,0:T(8,128)S(1)}, f32[16,1024]{1,0:T(8,128)S(1)}, f32[16,1024]{1,0:T(8,128)S(1)}, f32[4,128...) custom-call(bf16[256,1024]{1,0:T(8,128)(2,1)S(1)} %copy-done, ...), custom_call_target="tpu_custom_call" | custom-call | flops 2000000000 | bytes 2654336 | tf_op jit(solution)/shard_map/pallas_call | solution.py:633
  10.5 0.9 %shard_map.148 = (bf16[4,144,128]{2,1,0:T(8,128)(2,1)S(1)}, bf16[4,144,128]{2,1,0:T(8,128)(2,1)S(1)}, bf16[4,144,128]{2,1,0:T(8,128)(2,1)S(1)}, bf16[4,144,128]{2,1,0:T(8,128)(2,1)S(1)}) custom-call(bf16[3,1280]{1,0:T(4,128)(2,1)S(1)} %collective-permute-done.before, f32[2,128,1024]{2,1,0:T(8,128)S(1)} %get-tuple-element.54.sg, ...), custom_call_target="tpu_custom_call" | custom-call | bytes 1945088 | tf_op jit(solution)/shard_map/pallas_call | solution.py:633
  12.0 2.1 %collective-permute-start.2 = (bf16[4,144,128]{2,1,0:T(8,128)(2,1)S(1)}, bf16[4,144,128]{2,1,0:T(8,128)(2,1)S(1)}, u32[]{:S(2)}, u32[]{:S(2)}) collective-permute-start(bf16[4,144,128]{2,1,0:T(8,128)(2,1)S(1)} %get-tuple-element.62), channel_id=1, source_target_pairs={{0,2},{1,3},{2,0},{3,1},{4,6},{5,7},{6,4},{7,5},{8,10},{9,11},{10,... | collective-permute-start | bytes 442376 | tf_op jit(solution)/shard_map/ppermute | solution.py:645
  15.0 5.6 %shard_map.149 = (f32[256,512]{1,0:T(8,128)S(1)}, f32[256,512]{1,0:T(8,128)S(1)}, f32[256,512]{1,0:T(8,128)S(1)}, bf16[2,256,512]{2,1,0:T(8,128)(2,1)S(1)}, bf16...) custom-call(bf16[256,1024]{1,0:T(8,128)(2,1)S(1)} %copy-done, ...), custom_call_target="tpu_custom_call" | custom-call | flops 4000000000 | bytes 4828736 | tf_op jit(solution)/shard_map/pallas_call | solution.py:633
  20.7 1.0 %collective-permute-done.3.refs_3_ = bf16[4,144,128]{2,1,0:T(8,128)(2,1)S(1)} collective-permute-done((bf16[4,144,128]{2,1,0:T(8,128)(2,1)S(1)}, bf16[4,144,128]{2,1,0:T(8,128)(2,1)S(1)}, u32[]{:S(2)}, u32[]{:S(2)}) %collective-permute-start.3) | collective-permute-done | bytes 147488 | tf_op jit(solution)/shard_map/ppermute | solution.py:645
  22.3 1.7 %collective-permute-start.4 = (bf16[4,80,128]{2,1,0:T(8,128)(2,1)S(1)}, bf16[4,80,128]{2,1,0:T(8,128)(2,1)S(1)}, u32[]{:S(2)}, u32[]{:S(2)}) collective-permute-start(bf16[4,80,128]{2,1,0:T(8,128)(2,1)S(1)} %get-tuple-element.67), channel_id=1, source_target_pairs={{0,4},{1,5},{2,6},{3,7},{4,8},{5,9},{6,10},{7,11},{8,12},{9,13},{1... | collective-permute-start | bytes 245768 | tf_op jit(solution)/shard_map/ppermute | solution.py:651
  23.9 2.9 %collective-permute-start.5 = (bf16[4,80,128]{2,1,0:T(8,128)(2,1)S(1)}, bf16[4,80,128]{2,1,0:T(8,128)(2,1)S(1)}, u32[]{:S(2)}, u32[]{:S(2)}) collective-permute-start(bf16[4,80,128]{2,1,0:T(8,128)(2,1)S(1)} %get-tuple-element.68), channel_id=1, source_target_pairs={{0,8},{1,9},{2,10},{3,11},{4,12},{5,13},{6,14},{7,15},{8,0},{9,1},... | collective-permute-start | bytes 245768 | tf_op jit(solution)/shard_map/ppermute | solution.py:651
  26.8 1.3 %collective-permute-start.6 = (bf16[4,80,128]{2,1,0:T(8,128)(2,1)S(1)}, bf16[4,80,128]{2,1,0:T(8,128)(2,1)S(1)}, u32[]{:S(2)}, u32[]{:S(2)}) collective-permute-start(bf16[4,80,128]{2,1,0:T(8,128)(2,1)S(1)} %get-tuple-element.69), channel_id=1, source_target_pairs={{0,12},{1,13},{2,14},{3,15},{4,0},{5,1},{6,2},{7,3},{8,4},{9,5},{1... | collective-permute-start | bytes 245768 | tf_op jit(solution)/shard_map/ppermute | solution.py:651
  28.2 6.3 %shard_map.151 = (f32[256,512]{1,0:T(8,128)S(1)}, f32[256,512]{1,0:T(8,128)S(1)}, f32[256,512]{1,0:T(8,128)S(1)}, bf16[2,256,512]{2,1,0:T(8,128)(2,1)S(1)}, bf16...) custom-call(bf16[256,1024]{1,0:T(8,128)(2,1)S(1)} %copy-done, ...), custom_call_target="tpu_custom_call" | custom-call | flops 4000000000 | bytes 4746816 | tf_op jit(solution)/shard_map/pallas_call | solution.py:633
  34.4 0.8 %shard_map.152 = (bf16[4,144,128]{2,1,0:T(8,128)(2,1)S(1)}, bf16[4,144,128]{2,1,0:T(8,128)(2,1)S(1)}, bf16[4,144,128]{2,1,0:T(8,128)(2,1)S(1)}, bf16[4,144,128]{2,1,0:T(8,128)(2,1)S(1)}) custom-call(bf16[4,80,128]{2,1,0:T(8,128)(2,1)S(1)} %collective-permute-done.4.refs_0_, bf16[4,80,128]{2,1,0:T(8,128)(2,1)S(1)} %collective-permute-done.5.refs_1_, ...), custom_call_target="tpu_custom_call" | custom-call | bytes 1982464 | tf_op jit(solution)/shard_map/pallas_call | solution.py:633
  35.2 2.1 %collective-permute-start.7 = (bf16[4,144,128]{2,1,0:T(8,128)(2,1)S(1)}, bf16[4,144,128]{2,1,0:T(8,128)(2,1)S(1)}, u32[]{:S(2)}, u32[]{:S(2)}) collective-permute-start(bf16[4,144,128]{2,1,0:T(8,128)(2,1)S(1)} %get-tuple-element.75), channel_id=1, source_target_pairs={{0,1},{1,2},{2,3},{3,0},{4,5},{5,6},{6,7},{7,4},{8,9},{9,10},{10,1... | collective-permute-start | bytes 442376 | tf_op jit(solution)/shard_map/ppermute | solution.py:645
  37.3 0.7 %collective-permute-start.8 = (bf16[4,144,128]{2,1,0:T(8,128)(2,1)S(1)}, bf16[4,144,128]{2,1,0:T(8,128)(2,1)S(1)}, u32[]{:S(2)}, u32[]{:S(2)}) collective-permute-start(bf16[4,144,128]{2,1,0:T(8,128)(2,1)S(1)} %get-tuple-element.76), channel_id=1, source_target_pairs={{0,2},{1,3},{2,0},{3,1},{4,6},{5,7},{6,4},{7,5},{8,10},{9,11},{10,... | collective-permute-start | bytes 442376 | tf_op jit(solution)/shard_map/ppermute | solution.py:645
  38.7 2.1 %collective-permute-done.7.refs_1_ = bf16[4,144,128]{2,1,0:T(8,128)(2,1)S(1)} collective-permute-done((bf16[4,144,128]{2,1,0:T(8,128)(2,1)S(1)}, bf16[4,144,128]{2,1,0:T(8,128)(2,1)S(1)}, u32[]{:S(2)}, u32[]{:S(2)}) %collective-permute-start.7) | collective-permute-done | bytes 147488 | tf_op jit(solution)/shard_map/ppermute | solution.py:645
  40.8 3.2 %collective-permute-done.8.refs_2_ = bf16[4,144,128]{2,1,0:T(8,128)(2,1)S(1)} collective-permute-done((bf16[4,144,128]{2,1,0:T(8,128)(2,1)S(1)}, bf16[4,144,128]{2,1,0:T(8,128)(2,1)S(1)}, u32[]{:S(2)}, u32[]{:S(2)}) %collective-permute-start.8) | collective-permute-done | bytes 147488 | tf_op jit(solution)/shard_map/ppermute | solution.py:645
  44.0 1.5 %collective-permute-done.9.refs_3_ = bf16[4,144,128]{2,1,0:T(8,128)(2,1)S(1)} collective-permute-done((bf16[4,144,128]{2,1,0:T(8,128)(2,1)S(1)}, bf16[4,144,128]{2,1,0:T(8,128)(2,1)S(1)}, u32[]{:S(2)}, u32[]{:S(2)}) %collective-permute-start.9) | collective-permute-done | bytes 147488 | tf_op jit(solution)/shard_map/ppermute | solution.py:645
  45.5 1.0 %shard_map.153 = (bf16[256,1024]{1,0:T(8,128)(2,1)S(1)}, bf16[256,1024]{1,0:T(8,128)(2,1)S(1)}, f32[3,1280]{1,0:T(4,128)S(1)}) custom-call(bf16[4,144,128]{2,1,0:T(8,128)(2,1)S(1)} %get-tuple-element.74.refs_0_, bf16[4,144,128]{2,1,0:T(8,128)(2,1)S(1)} %collective-permute-done.7.refs_1_, bf16[4,144,128]{2,1,0:T(8,128)(2,1)S(1)} %collective-permute-done.8.refs_2_, ...), custom_call_target="tpu_custom_call" | custom-call | bytes 6962176 | tf_op jit(solution)/shard_map/pallas_call | solution.py:633
  46.5 2.2 %collective-permute-start.10 = (f32[3,1280]{1,0:T(4,128)S(1)}, f32[3,1280]{1,0:T(4,128)S(1)}, u32[]{:S(2)}, u32[]{:S(2)}) collective-permute-start(f32[3,1280]{1,0:T(4,128)S(1)} %get-tuple-element.98), channel_id=1, source_target_pairs={{1,0},{2,1},{3,2},{4,3},{5,4},{6,5},{7,6},{8,7},{9,8},{10,9},{11,1... | collective-permute-start | bytes 46088 | tf_op jit(solution)/shard_map/ppermute | solution.py:721
  48.7 3.7 %shard_map.154 = (f32[256,1024]{1,0:T(8,128)}, f32[256,1024]{1,0:T(8,128)S(1)}, f32[256,256]{1,0:T(8,128)S(1)}, f32[16,256]{1,0:T(8,128)}) custom-call(bf16[256,1024]{1,0:T(8,128)(2,1)S(1)} %get-tuple-element.90.e_cat, bf16[256,1024]{1,0:T(8,128)(2,1)S(1)} %get-tuple-element.91.f_cat, bf16[256,128]{1,0:T(8,128)(2,1)S(1)} %get-tuple-element.92.columns, ...), custom_call_target="tpu_custom_call" | custom-call | flops 2000000000 | bytes 9887872 | tf_op jit(solution)/shard_map/pallas_call | solution.py:633
  52.4 2.0 %collective-permute-done.10.after = f32[3,1280]{1,0:T(4,128)S(1)} collective-permute-done((f32[3,1280]{1,0:T(4,128)S(1)}, f32[3,1280]{1,0:T(4,128)S(1)}, u32[]{:S(2)}, u32[]{:S(2)}) %collective-permute-start.10) | collective-permute-done | bytes 15392 | tf_op jit(solution)/shard_map/ppermute | solution.py:721
  54.3 1.6 %shard_map.155 = (f32[256,1024]{1,0:T(8,128)}, f32[256,128]{1,0:T(8,128)}, f32[256,128]{1,0:T(8,128)}) custom-call(f32[256,1024]{1,0:T(8,128)S(1)} %get-tuple-element.96.dpre, f32[256,256]{1,0:T(8,128)S(1)} %get-tuple-element.97.dpre_bc, f32[3,1280]{1,0:T(4,128)S(1)} %collective-permute-done.10.after, f32[4,1280]{1,0:T(4,128)S(1)} %get-tuple-element.58.taps), custom_call_target="tpu_custom_call" | custom-call | bytes 2657280 | tf_op jit(solution)/shard_map/pallas_call | solution.py:633
  (32 shorter events, 3.3 us)
Async XLA Ops:
  0.6 5.0 %copy-start.2 = (bf16[256,128]{1,0:T(8,128)(2,1)S(1)}, bf16[256,128]{1,0:T(8,128)(2,1)}, u32[]{:S(2)}) copy-start(bf16[256,128]{1,0:T(8,128)(2,1)} %cs.5) | copy-start | bytes 196612
  0.6 5.0 %copy-start.1 = (bf16[256,128]{1,0:T(8,128)(2,1)S(1)}, bf16[256,128]{1,0:T(8,128)(2,1)}, u32[]{:S(2)}) copy-start(bf16[256,128]{1,0:T(8,128)(2,1)} %bs.5) | copy-start | bytes 196612
  0.7 5.0 %copy-start = (bf16[256,1024]{1,0:T(8,128)(2,1)S(1)}, bf16[256,1024]{1,0:T(8,128)(2,1)}, u32[]{:S(2)}) copy-start(bf16[256,1024]{1,0:T(8,128)(2,1)} %xs.5) | copy-start | bytes 1572868
  0.7 5.0 %copy-start.3 = (bf16[16,256]{1,0:T(8,128)(2,1)S(1)}, bf16[16,256]{1,0:T(8,128)(2,1)}, u32[]{:S(2)}) copy-start(bf16[16,256]{1,0:T(8,128)(2,1)} %dts.3) | copy-start | bytes 24580
  0.7 5.0 %copy-start.10 = (f32[4,128]{1,0:T(4,128)S(1)}, f32[4,128]{1,0:T(4,128)}, u32[]{:S(2)}) copy-start(f32[4,128]{1,0:T(4,128)} %taps_c.1) | copy-start | bytes 6148
  2.1 3.5 %copy-start.9 = (f32[4,128]{1,0:T(4,128)S(1)}, f32[4,128]{1,0:T(4,128)}, u32[]{:S(2)}) copy-start(f32[4,128]{1,0:T(4,128)} %taps_b.1) | copy-start | bytes 6148
  2.2 8.4 %collective-permute-start = (bf16[3,1280]{1,0:T(4,128)(2,1)}, bf16[3,1280]{1,0:T(4,128)(2,1)S(1)}, u32[]{:S(2)}, u32[]{:S(2)}) collective-permute-start(bf16[3,1280]{1,0:T(4,128)(2,1)} %shard_map.146), channel_id=1, source_target_pairs={{0,1},{1,2},{2,3},{3,4},{4,5},{5,6},{6,7},{7,8},{8,9},{9,10},{10,1... | collective-permute-start | bytes 23048 | tf_op jit(solution)/shard_map/ppermute | solution.py:670
  5.6 0.7 %copy-start.4 = (f32[16]{0:T(128)S(1)}, f32[16]{0:T(128)}, u32[]{:S(2)}) copy-start(f32[16]{0:T(128)} %param.15) | copy-start | bytes 196
  5.6 0.7 %copy-start.5 = (f32[16]{0:T(128)S(1)}, f32[16]{0:T(128)}, u32[]{:S(2)}) copy-start(f32[16]{0:T(128)} %param.16) | copy-start | bytes 196
  6.2 1.0 %copy-start.6 = (bf16[256,1024]{1,0:T(8,128)(2,1)S(1)}, bf16[256,1024]{1,0:T(8,128)(2,1)}, u32[]{:S(2)}) copy-start(bf16[256,1024]{1,0:T(8,128)(2,1)} %gs.5) | copy-start | bytes 1572868
  7.3 0.7 %copy-start.8 = (f32[4,1024]{1,0:T(4,128)S(1)}, f32[4,1024]{1,0:T(4,128)}, u32[]{:S(2)}) copy-start(f32[4,1024]{1,0:T(4,128)} %taps_x.1) | copy-start | bytes 49156
  10.5 3.8 %copy-start.7 = (bf16[256,1024]{1,0:T(8,128)(2,1)S(1)}, bf16[256,1024]{1,0:T(8,128)(2,1)}, u32[]{:S(2)}) copy-start(bf16[256,1024]{1,0:T(8,128)(2,1)} %gs.5) | copy-start | bytes 1572868
  11.5 9.2 %collective-permute-start.1 = (bf16[4,144,128]{2,1,0:T(8,128)(2,1)S(1)}, bf16[4,144,128]{2,1,0:T(8,128)(2,1)S(1)}, u32[]{:S(2)}, u32[]{:S(2)}) collective-permute-start(bf16[4,144,128]{2,1,0:T(8,128)(2,1)S(1)} %get-tuple-element.61), channel_id=1, source_target_pairs={{0,1},{1,2},{2,3},{3,0},{4,5},{5,6},{6,7},{7,4},{8,9},{9,10},{10,1... | collective-permute-start | bytes 442376 | tf_op jit(solution)/shard_map/ppermute | solution.py:645
  12.0 8.7 %collective-permute-start.2 = (bf16[4,144,128]{2,1,0:T(8,128)(2,1)S(1)}, bf16[4,144,128]{2,1,0:T(8,128)(2,1)S(1)}, u32[]{:S(2)}, u32[]{:S(2)}) collective-permute-start(bf16[4,144,128]{2,1,0:T(8,128)(2,1)S(1)} %get-tuple-element.62), channel_id=1, source_target_pairs={{0,2},{1,3},{2,0},{3,1},{4,6},{5,7},{6,4},{7,5},{8,10},{9,11},{10,... | collective-permute-start | bytes 442376 | tf_op jit(solution)/shard_map/ppermute | solution.py:645
  14.1 7.6 %collective-permute-start.3 = (bf16[4,144,128]{2,1,0:T(8,128)(2,1)S(1)}, bf16[4,144,128]{2,1,0:T(8,128)(2,1)S(1)}, u32[]{:S(2)}, u32[]{:S(2)}) collective-permute-start(bf16[4,144,128]{2,1,0:T(8,128)(2,1)S(1)} %get-tuple-element.63), channel_id=1, source_target_pairs={{0,3},{1,0},{2,1},{3,2},{4,7},{5,4},{6,5},{7,6},{8,11},{9,8},{10,9... | collective-permute-start | bytes 442376 | tf_op jit(solution)/shard_map/ppermute | solution.py:645
  14.4 0.7 %copy-start.11 = (f32[16]{0:T(128)S(1)}, f32[16]{0:T(128)}, u32[]{:S(2)}) copy-start(f32[16]{0:T(128)} %param.17) | copy-start | bytes 196
  22.3 12.2 %collective-permute-start.4 = (bf16[4,80,128]{2,1,0:T(8,128)(2,1)S(1)}, bf16[4,80,128]{2,1,0:T(8,128)(2,1)S(1)}, u32[]{:S(2)}, u32[]{:S(2)}) collective-permute-start(bf16[4,80,128]{2,1,0:T(8,128)(2,1)S(1)} %get-tuple-element.67), channel_id=1, source_target_pairs={{0,4},{1,5},{2,6},{3,7},{4,8},{5,9},{6,10},{7,11},{8,12},{9,13},{1... | collective-permute-start | bytes 245768 | tf_op jit(solution)/shard_map/ppermute | solution.py:651
  23.9 10.5 %collective-permute-start.5 = (bf16[4,80,128]{2,1,0:T(8,128)(2,1)S(1)}, bf16[4,80,128]{2,1,0:T(8,128)(2,1)S(1)}, u32[]{:S(2)}, u32[]{:S(2)}) collective-permute-start(bf16[4,80,128]{2,1,0:T(8,128)(2,1)S(1)} %get-tuple-element.68), channel_id=1, source_target_pairs={{0,8},{1,9},{2,10},{3,11},{4,12},{5,13},{6,14},{7,15},{8,0},{9,1},... | collective-permute-start | bytes 245768 | tf_op jit(solution)/shard_map/ppermute | solution.py:651
  26.8 7.6 %collective-permute-start.6 = (bf16[4,80,128]{2,1,0:T(8,128)(2,1)S(1)}, bf16[4,80,128]{2,1,0:T(8,128)(2,1)S(1)}, u32[]{:S(2)}, u32[]{:S(2)}) collective-permute-start(bf16[4,80,128]{2,1,0:T(8,128)(2,1)S(1)} %get-tuple-element.69), channel_id=1, source_target_pairs={{0,12},{1,13},{2,14},{3,15},{4,0},{5,1},{6,2},{7,3},{8,4},{9,5},{1... | collective-permute-start | bytes 245768 | tf_op jit(solution)/shard_map/ppermute | solution.py:651
  35.2 5.6 %collective-permute-start.7 = (bf16[4,144,128]{2,1,0:T(8,128)(2,1)S(1)}, bf16[4,144,128]{2,1,0:T(8,128)(2,1)S(1)}, u32[]{:S(2)}, u32[]{:S(2)}) collective-permute-start(bf16[4,144,128]{2,1,0:T(8,128)(2,1)S(1)} %get-tuple-element.75), channel_id=1, source_target_pairs={{0,1},{1,2},{2,3},{3,0},{4,5},{5,6},{6,7},{7,4},{8,9},{9,10},{10,1... | collective-permute-start | bytes 442376 | tf_op jit(solution)/shard_map/ppermute | solution.py:645
  37.3 6.8 %collective-permute-start.8 = (bf16[4,144,128]{2,1,0:T(8,128)(2,1)S(1)}, bf16[4,144,128]{2,1,0:T(8,128)(2,1)S(1)}, u32[]{:S(2)}, u32[]{:S(2)}) collective-permute-start(bf16[4,144,128]{2,1,0:T(8,128)(2,1)S(1)} %get-tuple-element.76), channel_id=1, source_target_pairs={{0,2},{1,3},{2,0},{3,1},{4,6},{5,7},{6,4},{7,5},{8,10},{9,11},{10,... | collective-permute-start | bytes 442376 | tf_op jit(solution)/shard_map/ppermute | solution.py:645
  38.0 7.5 %collective-permute-start.9 = (bf16[4,144,128]{2,1,0:T(8,128)(2,1)S(1)}, bf16[4,144,128]{2,1,0:T(8,128)(2,1)S(1)}, u32[]{:S(2)}, u32[]{:S(2)}) collective-permute-start(bf16[4,144,128]{2,1,0:T(8,128)(2,1)S(1)} %get-tuple-element.77), channel_id=1, source_target_pairs={{0,3},{1,0},{2,1},{3,2},{4,7},{5,4},{6,5},{7,6},{8,11},{9,8},{10,9... | collective-permute-start | bytes 442376 | tf_op jit(solution)/shard_map/ppermute | solution.py:645
  46.5 7.8 %collective-permute-start.10 = (f32[3,1280]{1,0:T(4,128)S(1)}, f32[3,1280]{1,0:T(4,128)S(1)}, u32[]{:S(2)}, u32[]{:S(2)}) collective-permute-start(f32[3,1280]{1,0:T(4,128)S(1)} %get-tuple-element.98), channel_id=1, source_target_pairs={{1,0},{2,1},{3,2},{4,3},{5,4},{6,5},{7,6},{8,7},{9,8},{10,9},{11,1... | collective-permute-start | bytes 46088 | tf_op jit(solution)/shard_map/ppermute | solution.py:721

commit v3 on v2

--- a/solution.py
+++ b/solution.py
@@ -344,11 +344,12 @@
         back[...] = code_scr[lax.rem(x + shift, SIDE)]
 
 
-def block_kernel(
-    first_pair, xs, gs, bs, cs, before, taps, cums, steps, after_this, skip,
-    ys, dxs, slopes, xws, ges, bcs, slopes_bc, dbcs, sums,
-    rows_scr, ds_scr, off_scr, diag_scr, cols_scr, pick_scr, sc_scr, row_scr, acc_scr,
-):
+def block_setup(bs, cs, taps, cums, steps, rows_scr, shared):
+    bcs, slopes_bc, sc_scr, off_scr, cols_scr, pick_scr, row_scr, diag_scr, ds, acc, dg = shared
+
+    def rows(parts, s):
+        return tuple(p[s * SUB : s * SUB + SUB] for p in parts)
+
     cum, step = cums[...], steps[...]
     shifted = cum - jnp.log(step)
     for head in range(HEADS):
@@ -367,9 +368,6 @@
     same = r % 2 == l // HEAD_DIM
     for n in range(5):
         pick_scr[:, 512 + 128 * n : 640 + 128 * n] = onehot(((r - 96) // 32 == n) & (r >= 96) & same)
-    pair_of = (iota((TOKENS, 256), 1) % HEADS) // 2
-    column = iota((256, 128), 1) - (iota((256, 128), 0) // HEAD_DIM) % 2
-    rows_scr[8 - RIM : 8, :] = before[...].astype(f32)
     for n, (raw, lanes) in enumerate(((bs, B_LANES), (cs, C_LANES))):
         rows_scr[8:, lanes] = raw[...].astype(f32)
         act, slope = slope_of(conv_rows(rows_scr, taps[:, lanes], lanes))
@@ -379,21 +377,26 @@
     r, l = iota((SUB, SUB), 0), iota((SUB, SUB), 1)
     b2, c2 = split2(b), split2(c)
 
-    def rows(parts, s):
-        return tuple(p[s * SUB : s * SUB + SUB] for p in parts)
-
     for s in range(2):
         sc_scr[s] = jnp.where(r > l, dot3(rows(c2, s), rows(b2, s), NT), 0.0)
         sc_scr[2 + s] = jnp.where(l > r, dot3(rows(b2, s), rows(c2, s), NT), 0.0)
     off_scr[0] = jnp.concatenate(split2(dot3(rows(c2, 1), rows(b2, 0), NT)), axis=1)
     off_scr[1] = jnp.concatenate(split2(dot3(rows(b2, 0), rows(c2, 1), NT)), axis=1)
-    ds_scr[...] = jnp.zeros_like(ds_scr)
-    acc_scr[...] = jnp.zeros_like(acc_scr)
+    ds[...] = jnp.zeros_like(ds)
+    acc[...] = jnp.zeros_like(acc)
     diag = jnp.broadcast_to(jnp.sum(b * c, axis=1, keepdims=True), (TOKENS, 128))
-    diag_scr[0] = diag
-    diag_scr[1] = jnp.zeros((TOKENS, 128), f32)
+    diag_scr[...] = diag
+    dg[...] = jnp.zeros_like(dg)
+
+
+def block_pairs(first_pair, count, xs, gs, taps, skip, outs, rows_scr, shared):
+    ys, dxs, slopes, xws, ges = outs
+    _, _, sc_scr, off_scr, cols_scr, pick_scr, row_scr, diag_scr, ds, acc, dg = shared
+    r, l = iota((SUB, SUB), 0), iota((SUB, SUB), 1)
     low = low_half((SUB, 128))
     zero = jnp.zeros((SUB, 128), bf16)
+    pair_of = (iota((TOKENS, 256), 1) % HEADS) // 2
+    column = iota((256, 128), 1) - (iota((256, 128), 0) // HEAD_DIM) % 2
 
     def twice(hi, lo):
         return jnp.concatenate([jnp.concatenate([hi, lo], axis=1), jnp.concatenate([hi, zero], axis=1)], axis=0)
@@ -442,63 +445,104 @@
             g1 = jnp.where(low, 0.0, gf_s).astype(bf16)
             g01 = jnp.concatenate([g0, g1], axis=0)
             dm = dot(jnp.concatenate([g01, g01], axis=1), jnp.concatenate([xh_s, xl_s], axis=1), NT)
-            ds_scr[s] += dm[:SUB] * decays[0] + dm[SUB:] * decays[1]
+            ds[s] += dm[:SUB] * decays[0] + dm[SUB:] * decays[1]
             y_parts.append(jnp.where(low, y2[:SUB], y2[SUB:]))
             dx_parts.append(jnp.where(low, dx2[:SUB], dx2[SUB:]))
         xwh, xwl = split2(x[:SUB] * outer_x[:SUB])
         geh, gel = split2(gf[SUB:] * inner_x[SUB:])
         y_parts[1] += inner_x[SUB:] * fold(dot(off_scr[0], twice(xwh, xwl)))
         dx_parts[0] += outer_x[:SUB] * fold(dot(off_scr[1], twice(geh, gel)))
-        ds_scr[2] += dot(jnp.concatenate([geh, gel], axis=1), jnp.concatenate([xwh, xwh], axis=1), NT) + dot(geh, xwl, NT)
+        ds[2] += dot(jnp.concatenate([geh, gel], axis=1), jnp.concatenate([xwh, xwh], axis=1), NT) + dot(geh, xwl, NT)
         y = jnp.concatenate(y_parts, axis=0)
         dx = jnp.concatenate(dx_parts, axis=0)
         xg = x * gf
         xdx = x * dx
-        total = acc_scr[...]
+        total = acc[...]
         for n, v in enumerate((gf * y - xdx, xdx, xg)):
             hot = onehot(column == n * HEADS + head)
             total += dot(jnp.concatenate(split2(v), axis=1), hot)
-        acc_scr[...] = total
-        diag_scr[1] += step_x * xg
-        direct = jnp.where(low_half((TOKENS, 128)), skip[0, head], skip[0, head + 1]) + diag_scr[0] * step_x
+        acc[...] = total
+        dg[...] += step_x * xg
+        direct = jnp.where(low_half((TOKENS, 128)), skip[:, head : head + 1], skip[:, head + 1 : head + 2]) + diag_scr[...] * step_x
         ys[:, local] = y + direct * x
         dxs[:, local] = dx + direct * gf
 
-    for pair in range(first_pair, first_pair + PAIRS // 2):
+    for pair in range(first_pair, first_pair + count):
         pair_step(pair)
-    d_diag = jnp.sum(diag_scr[1], axis=1, keepdims=True)
+
+
+def block_finish(steps, dbcs, sums, shared):
+    bcs, _, _, _, _, _, _, diag_scr, ds, acc, dg = shared
+    step = steps[...]
+    b, c = bcs[:, :STATE], bcs[:, STATE:]
+    b2, c2 = split2(b), split2(c)
+    r, l = iota((SUB, SUB), 0), iota((SUB, SUB), 1)
+
+    def rows(parts, s):
+        return tuple(p[s * SUB : s * SUB + SUB] for p in parts)
+
+    d_diag = jnp.sum(dg[...], axis=1, keepdims=True)
     db = d_diag * c
     dc = d_diag * b
     for s in range(2):
-        ds = jnp.where(r > l, ds_scr[s], 0.0)
-        d2 = split2(ds)
-        t2 = split2(ds.T)
+        d = jnp.where(r > l, ds[s], 0.0)
+        d2 = split2(d)
+        t2 = split2(d.T)
         at = slice(s * SUB, s * SUB + SUB)
         dc_s = dc[at] + dot3(d2, rows(b2, s))
         db_s = db[at] + dot3(t2, rows(c2, s))
         if s == 0:
-            db_s += dot3(split2(ds_scr[2].T), rows(c2, 1))
+            db_s += dot3(split2(ds[2].T), rows(c2, 1))
         else:
-            dc_s += dot3(split2(ds_scr[2]), rows(b2, 0))
+            dc_s += dot3(split2(ds[2]), rows(b2, 0))
         dbcs[at, :STATE] = db_s
         dbcs[at, STATE:] = dc_s
-    turned = acc_scr[...].T
+    turned = acc[...].T
     sums[0] = turned[0:HEADS]
-    sums[1] = turned[HEADS : 2 * HEADS] / step + diag_scr[0].T[0:1] * turned[2 * HEADS : 3 * HEADS]
+    sums[1] = turned[HEADS : 2 * HEADS] / step + diag_scr[...].T[0:1] * turned[2 * HEADS : 3 * HEADS]
+
+
+def block_kernel(first_pair, count, *refs):
+    (xs, gs, bs, cs, before, taps, cums, steps, skip, _), refs = refs[:10], refs[10:]
+    rows_scr, refs = refs[-1], refs[:-1]
+    rows_scr[8 - RIM : 8, :] = before[...].astype(f32)
+    if first_pair == 0:
+        outs, shared = refs[:5], refs[5:]
+        block_setup(bs, cs, taps, cums, steps, rows_scr, shared)
+    else:
+        (*kept, ds_in, acc_in, dg_in), refs = refs[:11], refs[11:]
+        outs, (ds, acc, dg) = refs[:5], refs[-3:]
+        ds[...] = ds_in[...]
+        acc[...] = acc_in[...]
+        dg[...] = dg_in[...]
+        shared = (*kept, ds, acc, dg)
+    block_pairs(first_pair, count, xs, gs, taps, skip, outs, rows_scr, shared)
+    if first_pair + count == PAIRS:
+        block_finish(steps, refs[5], refs[6], shared)
 
 
 def wide_product(a2, cat, lanes):
     return dot(jnp.concatenate([a2[0], a2[0]], axis=1), cat[:, lanes]) + dot(a2[1], cat[:STATE, lanes])
 
 
-def both_halves(n):
-    per = PARTS // 2
-    return n // per, pl.ds((n % per) * PART, PART)
+GROUP_PAIRS = (3, 2, 3)
+
+
+def columns_of(refs, n, *lead):
+    pieces = []
+    for pair in range(2 * n, 2 * n + 2):
+        group = 0
+        while pair >= GROUP_PAIRS[group]:
+            pair -= GROUP_PAIRS[group]
+            group += 1
+        pieces.append(refs[group][(*lead, slice(pair * 128, pair * 128 + 128))])
+    return jnp.concatenate(pieces, axis=1)
 
 
 def rim_kernel(*refs):
     backs, refs = refs[:SIDE], refs[SIDE:]
-    bc, dx0, dx1, slope0, slope1, slope_bc, dbc0, dbc1, xw0, xw1, ge0, ge1, end16, e_cat, f_cat, rim = refs
+    (bc, slope_bc, dbc, end16), refs = refs[:4], refs[4:]
+    dxs, slopes, xws, ges, (e_cat, f_cat, rim) = refs[:3], refs[3:6], refs[6:9], refs[9:12], refs[12:]
     x, _ = place()
     for shift, back in enumerate(backs):
         q = lax.rem(x - shift + SIDE, SIDE)
@@ -517,49 +561,47 @@
             cat[STATE:, quarter(q)] = lo
     b2 = split2(bc[0:16, :STATE])
     for n in range(PARTS):
-        side, lanes = both_halves(n)
-        dx, slope = ((dx0, slope0), (dx1, slope1))[side]
-        d = (dx[0:16, lanes] + end16[:, part(n)] * wide_product(b2, f_cat, part(n))) * slope[0:16, lanes]
+        top = slice(0, 16)
+        d = columns_of(dxs, n, top) + end16[:, part(n)] * wide_product(b2, f_cat, part(n))
+        d = d * columns_of(slopes, n, top)
         rim[:, n * PART : n * PART + PART] = d[:RIM]
-    for n, (v, cat) in enumerate((((xw0, xw1), f_cat), ((ge0, ge1), e_cat))):
-        hi, lo = (jnp.concatenate([v[0][m, 0:16, :], v[1][m, 0:16, :]], axis=1) for m in range(2))
+    for n, (v, cat) in enumerate(((xws, f_cat), (ges, e_cat))):
+        hi, lo = (jnp.concatenate([w[m, 0:16, :] for w in v], axis=1) for m in range(2))
         both = dot(hi, cat[...], NT)
         d = both[:, :STATE] + both[:, STATE:] + dot(lo, cat[:STATE], NT)
         cut = slice(n * STATE, n * STATE + STATE)
-        d = (dbc0[0:16, cut] + dbc1[0:16, cut] + d) * slope_bc[0:16, cut]
+        d = (dbc[0:16, cut] + d) * slope_bc[0:16, cut]
         rim[:, WIDTH + n * STATE : WIDTH + n * STATE + STATE] = d[:RIM]
 
 
-def main_kernel(
-    e_cat, f_cat, columns, bc, y0, y1, dx0, dx1, slope0, slope1, ge0, ge1, xw0, xw1, dbc0, dbc1, slope_bc,
-    sums0, sums1, cums, steps, dts, bias, rate,
-    y_out, dpre, dpre_bc, dt_out,
-    ys, gdt, out_sems,
-):
+def main_kernel(*refs):
+    (e_cat, f_cat, columns, bc, dbc, slope_bc, sums, cums, steps, dts, bias, rate), refs = refs[:12], refs[12:]
+    groups, (y_out, dpre, dpre_bc, dt_out, ys, gdt, out_sems) = refs[:15], refs[15:]
     b2, c2 = split2(bc[:, :STATE]), split2(bc[:, STATE:])
     grads = [[jnp.zeros((TOKENS, PART), f32), jnp.zeros((TOKENS, STATE), f32)] for _ in range(2)]
     total = jnp.zeros((TOKENS, 128), f32)
     both = jnp.zeros((8, 128), f32)
+    whole = slice(None)
     out = []
     for n in range(PARTS):
         lanes = part(n)
         heads = n * PART // HEAD_DIM
-        side, own = both_halves(n)
-        y_in, dx, slope, ge, xw = ((y0, dx0, slope0, ge0, xw0), (y1, dx1, slope1, ge1, xw1))[side]
+        y_in, dx, slope = (columns_of(groups[k::5], n, whole) for k in range(3))
+        xw, ge = ([columns_of(groups[k::5], n, m, whole) for m in range(2)] for k in (3, 4))
         start_x = dot(columns[...], spread_matrix(2, 128, 0, heads, HEAD_DIM, PART))
         end_x = dot(columns[...], spread_matrix(2, 128, 1, heads, HEAD_DIM, PART))
         ce = wide_product(c2, e_cat, lanes)
         bf = wide_product(b2, f_cat, lanes)
-        ys[:, lanes] = y_in[:, own] + start_x * ce
+        ys[:, lanes] = y_in + start_x * ce
         copy = pltpu.make_async_copy(ys.at[:, lanes], y_out.at[:, lanes], out_sems.at[n])
         copy.start()
         out.append(copy)
-        dpre[:, lanes] = (dx[:, own] + end_x * bf) * slope[:, own]
+        dpre[:, lanes] = (dx + end_x * bf) * slope
         for grad, v, cat in zip(grads, (xw, ge), (f_cat, e_cat)):
-            grad[0] += dot(v[0, :, own], cat[:, lanes], NT)
-            grad[1] += dot(v[1, :, own], cat[:STATE, lanes], NT)
+            grad[0] += dot(v[0], cat[:, lanes], NT)
+            grad[1] += dot(v[1], cat[:STATE, lanes], NT)
         for v, product, offset in ((xw, bf, 0), (ge, ce, HEADS)):
-            hi, lo = split2((v[0, :, own].astype(f32) + v[1, :, own].astype(f32)) * product)
+            hi, lo = split2((v[0].astype(f32) + v[1].astype(f32)) * product)
             hot = sum_matrix(PART, offset + heads)
             total += dot(hi, hot) + dot(lo, hot)
         e = e_cat[:STATE, lanes].astype(f32) + e_cat[STATE:, lanes].astype(f32)
@@ -569,7 +611,7 @@
         both += dot(hi, hot) + dot(lo, hot)
     for n, grad in enumerate(grads):
         cut = slice(n * STATE, n * STATE + STATE)
-        d = dbc0[:, cut] + dbc1[:, cut] + grad[0][:, :STATE] + grad[0][:, STATE:] + grad[1]
+        d = dbc[:, cut] + grad[0][:, :STATE] + grad[0][:, STATE:] + grad[1]
         dpre_bc[:, cut] = d * slope_bc[:, cut]
     turned = total.T
     later, kept = turned[0:HEADS], turned[HEADS : 2 * HEADS]
@@ -583,10 +625,8 @@
 
     cum, step = cums[...], steps[...]
     ends = jnp.exp(cum[:, SUB - 1 : SUB] + cum[:, TOKENS - 1 : TOKENS])
-    local = sums0[0] + sums1[0]
-    direct = sums0[1] + sums1[1]
-    d_decay = summed(local + kept, suffix) + summed(later, prefix) + ends * to_column(both[0:1, 0:HEADS])
-    d_step = direct + later / step - jnp.exp(to_column(rate[...])) * d_decay
+    d_decay = summed(sums[0] + kept, suffix) + summed(later, prefix) + ends * to_column(both[0:1, 0:HEADS])
+    d_step = sums[1] + later / step - jnp.exp(to_column(rate[...])) * d_decay
     pre = dts[...].astype(f32) + to_column(bias[...])
     gdt[...] = d_step / (1.0 + jnp.exp(-pre))
     out.append(pltpu.make_async_copy(gdt, dt_out, out_sems.at[PARTS]))
@@ -623,7 +663,6 @@
 
 
 VMEM = pl.BlockSpec(memory_space=pltpu.VMEM)
-SMEM = pl.BlockSpec(memory_space=pltpu.SMEM)
 HBM = pl.BlockSpec(memory_space=pltpu.HBM)
 
 
@@ -665,7 +704,7 @@
 
     (edge,) = call(
         edge_kernel, [(a, HBM) for a in (x_raw, b_raw, c_raw)], [((RIM, ALL), bf16, VMEM)], [((16, ALL), bf16)], [3],
-        mib=60,
+        mib=60, flops=2_000_000_000,
     )
     before = lax.ppermute(edge, "context", [(i, i + 1) for i in range(RANKS - 1)])
     sg, pre16, end16, ge16, taps, total, cum, step, columns = call(
@@ -682,47 +721,61 @@
         send_kernel, near(before, sg, pre16, end16, ge16, taps, total), [message] * SIDE, [(rim16, f32), (rim16, f32)]
     )
 
-    def block(first_pair, after_this):
-        half = (TOKENS, WIDTH // 2)
+    def block(group, after_this, shared):
+        first_pair, count = sum(GROUP_PAIRS[:group]), GROUP_PAIRS[group]
+        own = (TOKENS, count * 128)
+        outs = [(own, f32, VMEM)] * 3 + [((2,) + own, bf16, VMEM)] * 2
+        square = (TOKENS, 128)
+        carried = [((3, SUB, SUB), f32, VMEM), (square, f32, VMEM), (square, f32, VMEM)]
+        if group == 0:
+            outs += [
+                (bc, f32, VMEM), (bc, f32, VMEM), ((4, SUB, SUB), f32, VMEM), ((2, SUB, 2 * SUB), bf16, VMEM),
+                ((TOKENS, 256), f32, VMEM), ((256, 1152), bf16, VMEM), ((2 * HEADS, 8, TOKENS), f32, VMEM),
+                (square, f32, VMEM),
+            ]
+        if group == len(GROUP_PAIRS) - 1:
+            outs += [(bc, f32, VMEM), ((2,) + slim, f32, VMEM)]
         return call(
-            functools.partial(block_kernel, first_pair),
-            near(x_raw, grad_y, b_raw, c_raw, before, taps, cum, step, after_this) + [(skip_gain, SMEM)],
-            [(half, f32, VMEM)] * 3 + [((2,) + half, bf16, VMEM)] * 2 + [(bc, f32, VMEM)] * 3
-            + [((2,) + slim, f32, VMEM)],
-            [((TOKENS + 8, ALL), f32), ((3, SUB, SUB), f32), ((2, SUB, 2 * SUB), bf16), ((2, TOKENS, 128), f32),
-             ((TOKENS, 256), f32), ((256, 1152), bf16), ((4, SUB, SUB), f32), ((2 * HEADS, 8, TOKENS), f32),
-             ((TOKENS, 128), f32)],
+            functools.partial(block_kernel, first_pair, count),
+            near(x_raw, grad_y, b_raw, c_raw, before, taps, cum, step, skip_gain, after_this, *shared),
+            outs + carried,
+            [((TOKENS + 8, ALL), f32)],
             flops=4_000_000_000,
         )
 
     got = [pays[0]] + [along_row(pays[shift], shift) for shift in (1, 2, 3)]
-    y0, dx0, slope0, xw0, ge0, bcs, slope_bc, dbc0, sums0 = block(0, pays[0])
+    done = block(0, pays[0], ())
+    group0, shared = done[:5], done[5:]
     *sends, s_all, g_all, d_all = call(
         row_kernel,
-        near(*got, sums0),
+        near(*got, shared[-1]),
         [((QUARTER, ROWMSG, 128), bf16, VMEM)] * (SIDE - 1)
         + [((SIDE, QUARTER, HEAD_DIM, 128), f32, VMEM)] * 2 + [((SIDE, QUARTER, 8, 128), f32, VMEM)],
     )
     rows = [along_column(sends[shift - 1], shift) for shift in (1, 2, 3)]
-    y1, dx1, slope1, xw1, ge1, _, _, dbc1, sums1 = block(PAIRS // 2, d_all)
+    done = block(1, d_all, shared)
+    group1, sums_so_far = done[:5], done[5:]
     answers = call(
         column_kernel,
-        near(*rows, s_all, g_all, d_all, sums1),
+        near(*rows, s_all, g_all, d_all, sums_so_far[-1]),
         [message] * SIDE,
         [((SIDE, QUARTER, HEAD_DIM, 128), f32), ((SIDE, QUARTER, 8, 128), f32), ((SIDE, QUARTER, CHUNK, 128), bf16)],
     )
     backs = [answers[0]] + [along_row(answers[shift], shift) for shift in (1, 2, 3)]
+    done = block(2, answers[0], [*shared[:8], *sums_so_far])
+    group2, (dbc, sums) = done[:5], done[5:7]
+    bcs, slope_bc = shared[:2]
+    groups = (group0, group1, group2)
     cat = ((2 * STATE, WIDTH), bf16)
     e_cat, f_cat, rim = call(
         rim_kernel,
-        near(*backs, bcs, dx0, dx1, slope0, slope1, slope_bc, dbc0, dbc1, xw0, xw1, ge0, ge1, end16),
+        near(*backs, bcs, slope_bc, dbc, end16, *[g[n] for n in (1, 2, 3, 4) for g in groups]),
         [(*cat, VMEM), (*cat, VMEM), ((RIM, ALL), f32, VMEM)],
     )
     after = lax.ppermute(rim, "context", [(i, i - 1) for i in range(1, RANKS)])
     y_out, dpre, dpre_bc, grad_dt = call(
         main_kernel,
-        near(e_cat, f_cat, columns, bcs, y0, y1, dx0, dx1, slope0, slope1, ge0, ge1, xw0, xw1, dbc0, dbc1, slope_bc,
-             sums0, sums1, cum, step, dt_raw, dt_bias, a_log),
+        near(e_cat, f_cat, columns, bcs, dbc, slope_bc, sums, cum, step, dt_raw, dt_bias, a_log, *[a for g in groups for a in g]),
         [(wide, f32, HBM), (wide, f32, VMEM), (bc, f32, VMEM), (slim, f32, HBM)],
         [(wide, f32), (slim, f32)],
         [PARTS + 1],

time: 57.1 us -> 51 us (0.89)
  waiting for transfers between devices: 9.79 us -> 6.76 us
  local copies, waits for them, and re-layouts: 3.04 us -> 1.27 us
  Pallas kernels: 24.4 us -> 22.8 us
    ppermute x6, waiting for transfers between devices: 7.82 us -> 4.3 us  [along_row(): lax.ppermute(block, 'context', [(SIDE * y + x, SIDE * y + (x + shift) % S...]
    unnamed x24 -> x22, local copies, waits for them, and re-layouts: 3.04 us -> 1.27 us
    pallas_call x10 -> x11, Pallas kernels: 24.4 us -> 22.8 us  [call(): pl.pallas_call(kernel, out_shape=shapes, in_specs=[w for _, w in ins], ou...]
    ppermute x3, waiting for transfers between devices: 0.01 us -> 0.78 us  [along_column(): lax.ppermute(block, 'context', [(SIDE * y + x, SIDE * ((y + shift) % SIDE...]
  transfers between devices with their start and end apart: 11 -> 11, of which waited for: 5 -> 5; matrix products, arithmetic and copies ran while one was open for 0% -> 0% of each run, Pallas kernels for 32% -> 33%
where the time goes in v3:
time: 51 us; the launch traced here: 50.3 us
  Pallas kernels  22.8 us (45%)
  starting transfers between devices  18.4 us (36%)
  waiting for transfers between devices  6.76 us (13%)
  local copies, waits for them, and re-layouts  1.27 us (2%)
  between operations  1.06 us (2%)
    pallas_call x11, Pallas kernels, call(): pl.pallas_call(kernel, out_shape=shapes, in_specs=[w for _, w in ins], ou...  22.8 us
    ppermute x3, starting transfers between devices, along_column(): lax.ppermute(block, 'context', [(SIDE * y + x, SIDE * ((y + shift) % SIDE...  6.32 us
    ppermute x6, starting transfers between devices, along_row(): lax.ppermute(block, 'context', [(SIDE * y + x, SIDE * y + (x + shift) % S...  6.11 us
    ppermute x6, waiting for transfers between devices, along_row(): lax.ppermute(block, 'context', [(SIDE * y + x, SIDE * y + (x + shift) % S...  4.3 us
    ppermute x1, starting transfers between devices, on_device(): lax.ppermute(edge, 'context', [(i, i + 1) for i in range(RANKS - 1)])  3.4 us
    ppermute x1, starting transfers between devices, on_device(): after = lax.ppermute(rim, 'context', [(i, i - 1) for i in range(1, RANKS)])  2.53 us
    ppermute x1, waiting for transfers between devices, on_device(): after = lax.ppermute(rim, 'context', [(i, i - 1) for i in range(1, RANKS)])  1.67 us
    unnamed x22, local copies, waits for them, and re-layouts  1.27 us
  transfers between devices with their start and end apart: 11, of which 5 were waited for; matrix products, arithmetic and copies ran while one was open for 0% of the time, Pallas kernels for 33%

profile of v3, /device:TPU:38, one launch (start us, length us, event | category | flops | bytes accessed | tf_op | source)
XLA Modules:
  0.0 50.3 jit_solution(1913526191929486366)
XLA Ops:
  0.7 1.5 %shard_map.146 = bf16[3,1280]{1,0:T(4,128)(2,1)} custom-call(bf16[256,1024]{1,0:T(8,128)(2,1)} %refs_0_.5, bf16[256,128]{1,0:T(8,128)(2,1)} %refs_2_.5, bf16[256,128]{1,0:T(8,128)(2,1)} %refs_3_.5), custom_call_target="tpu_custom_call" | custom-call | flops 2000000000 | bytes 663040 | tf_op jit(solution)/shard_map/pallas_call | solution.py:672
  2.2 3.4 %collective-permute-start = (bf16[3,1280]{1,0:T(4,128)(2,1)}, bf16[3,1280]{1,0:T(4,128)(2,1)S(1)}, u32[]{:S(2)}, u32[]{:S(2)}) collective-permute-start(bf16[3,1280]{1,0:T(4,128)(2,1)} %shard_map.146), channel_id=1, source_target_pairs={{0,1},{1,2},{2,3},{3,4},{4,5},{5,6},{6,7},{7,8},{8,9},{9,10},{10,1... | collective-permute-start | bytes 23048 | tf_op jit(solution)/shard_map/ppermute | solution.py:709
  6.3 2.5 %shard_map.147 = (f32[2,128,1024]{2,1,0:T(8,128)S(1)}, f32[16,1280]{1,0:T(8,128)S(1)}, f32[16,1024]{1,0:T(8,128)S(1)}, f32[16,1024]{1,0:T(8,128)S(1)}, f32[4,128...) custom-call(bf16[256,1024]{1,0:T(8,128)(2,1)S(1)} %copy-done, ...), custom_call_target="tpu_custom_call" | custom-call | flops 2000000000 | bytes 2654336 | tf_op jit(solution)/shard_map/pallas_call | solution.py:672
  8.8 0.9 %shard_map.148 = (bf16[4,144,128]{2,1,0:T(8,128)(2,1)S(1)}, bf16[4,144,128]{2,1,0:T(8,128)(2,1)S(1)}, bf16[4,144,128]{2,1,0:T(8,128)(2,1)S(1)}, bf16[4,144,128]{2,1,0:T(8,128)(2,1)S(1)}) custom-call(bf16[3,1280]{1,0:T(4,128)(2,1)S(1)} %collective-permute-done.before.refs_4_, f32[2,128,1024]{2,1,0:T(8,128)S(1)} %get-tuple-element.69.sg, ...), custom_call_target="tpu_custom_call" | custom-call | bytes 1945088 | tf_op jit(solution)/shard_map/pallas_call | solution.py:672
  10.3 2.1 %collective-permute-start.2 = (bf16[4,144,128]{2,1,0:T(8,128)(2,1)S(1)}, bf16[4,144,128]{2,1,0:T(8,128)(2,1)S(1)}, u32[]{:S(2)}, u32[]{:S(2)}) collective-permute-start(bf16[4,144,128]{2,1,0:T(8,128)(2,1)S(1)} %get-tuple-element.77), channel_id=1, source_target_pairs={{0,2},{1,3},{2,0},{3,1},{4,6},{5,7},{6,4},{7,5},{8,10},{9,11},{10,... | collective-permute-start | bytes 442376 | tf_op jit(solution)/shard_map/ppermute | solution.py:684
  12.6 0.7 %copy-done.8 = f32[16]{0:T(128)S(1)} copy-done((f32[16]{0:T(128)S(1)}, f32[16]{0:T(128)}, u32[]{:S(2)}) %copy-start.8) | copy-done | bytes 88
  13.3 3.9 %shard_map.149 = (f32[256,384]{1,0:T(8,128)S(1)}, f32[256,384]{1,0:T(8,128)S(1)}, f32[256,384]{1,0:T(8,128)S(1)}, bf16[2,256,384]{2,1,0:T(8,128)(2,1)S(1)}, bf16...) custom-call(bf16[256,1024]{1,0:T(8,128)(2,1)S(1)} %copy-done, ...), custom_call_target="tpu_custom_call" | custom-call | flops 4000000000 | bytes 5975616 | tf_op jit(solution)/shard_map/pallas_call | solution.py:672
  17.2 1.1 %collective-permute-done.2.refs_2_ = bf16[4,144,128]{2,1,0:T(8,128)(2,1)S(1)} collective-permute-done((bf16[4,144,128]{2,1,0:T(8,128)(2,1)S(1)}, bf16[4,144,128]{2,1,0:T(8,128)(2,1)S(1)}, u32[]{:S(2)}, u32[]{:S(2)}) %collective-permute-start.2) | collective-permute-done | bytes 147488 | tf_op jit(solution)/shard_map/ppermute | solution.py:684
  18.3 1.6 %collective-permute-done.3.refs_3_ = bf16[4,144,128]{2,1,0:T(8,128)(2,1)S(1)} collective-permute-done((bf16[4,144,128]{2,1,0:T(8,128)(2,1)S(1)}, bf16[4,144,128]{2,1,0:T(8,128)(2,1)S(1)}, u32[]{:S(2)}, u32[]{:S(2)}) %collective-permute-start.3) | collective-permute-done | bytes 147488 | tf_op jit(solution)/shard_map/ppermute | solution.py:684
  20.5 2.1 %collective-permute-start.4 = (bf16[4,80,128]{2,1,0:T(8,128)(2,1)S(1)}, bf16[4,80,128]{2,1,0:T(8,128)(2,1)S(1)}, u32[]{:S(2)}, u32[]{:S(2)}) collective-permute-start(bf16[4,80,128]{2,1,0:T(8,128)(2,1)S(1)} %get-tuple-element.82), channel_id=1, source_target_pairs={{0,4},{1,5},{2,6},{3,7},{4,8},{5,9},{6,10},{7,11},{8,12},{9,13},{1... | collective-permute-start | bytes 245768 | tf_op jit(solution)/shard_map/ppermute | solution.py:690
  22.6 2.9 %collective-permute-start.5 = (bf16[4,80,128]{2,1,0:T(8,128)(2,1)S(1)}, bf16[4,80,128]{2,1,0:T(8,128)(2,1)S(1)}, u32[]{:S(2)}, u32[]{:S(2)}) collective-permute-start(bf16[4,80,128]{2,1,0:T(8,128)(2,1)S(1)} %get-tuple-element.83), channel_id=1, source_target_pairs={{0,8},{1,9},{2,10},{3,11},{4,12},{5,13},{6,14},{7,15},{8,0},{9,1},... | collective-permute-start | bytes 245768 | tf_op jit(solution)/shard_map/ppermute | solution.py:690
  25.5 1.3 %collective-permute-start.6 = (bf16[4,80,128]{2,1,0:T(8,128)(2,1)S(1)}, bf16[4,80,128]{2,1,0:T(8,128)(2,1)S(1)}, u32[]{:S(2)}, u32[]{:S(2)}) collective-permute-start(bf16[4,80,128]{2,1,0:T(8,128)(2,1)S(1)} %get-tuple-element.84), channel_id=1, source_target_pairs={{0,12},{1,13},{2,14},{3,15},{4,0},{5,1},{6,2},{7,3},{8,4},{9,5},{1... | collective-permute-start | bytes 245768 | tf_op jit(solution)/shard_map/ppermute | solution.py:690
  26.8 2.3 %shard_map.151 = (f32[256,256]{1,0:T(8,128)S(1)}, f32[256,256]{1,0:T(8,128)S(1)}, f32[256,256]{1,0:T(8,128)S(1)}, bf16[2,256,256]{2,1,0:T(8,128)(2,1)S(1)}, bf16...) custom-call(bf16[256,1024]{1,0:T(8,128)(2,1)S(1)} %copy-done, ...), custom_call_target="tpu_custom_call" | custom-call | flops 4000000000 | bytes 5697088 | tf_op jit(solution)/shard_map/pallas_call | solution.py:672
  29.1 0.8 %collective-permute-done.6.refs_2_ = bf16[4,80,128]{2,1,0:T(8,128)(2,1)S(1)} collective-permute-done((bf16[4,80,128]{2,1,0:T(8,128)(2,1)S(1)}, bf16[4,80,128]{2,1,0:T(8,128)(2,1)S(1)}, u32[]{:S(2)}, u32[]{:S(2)}) %collective-permute-start.6) | collective-permute-done | bytes 81952 | tf_op jit(solution)/shard_map/ppermute | solution.py:690
  29.9 0.8 %shard_map.152 = (bf16[4,144,128]{2,1,0:T(8,128)(2,1)S(1)}, bf16[4,144,128]{2,1,0:T(8,128)(2,1)S(1)}, bf16[4,144,128]{2,1,0:T(8,128)(2,1)S(1)}, bf16[4,144,128]{2,1,0:T(8,128)(2,1)S(1)}) custom-call(bf16[4,80,128]{2,1,0:T(8,128)(2,1)S(1)} %collective-permute-done.4.refs_0_, bf16[4,80,128]{2,1,0:T(8,128)(2,1)S(1)} %collective-permute-done.5.refs_1_, ...), custom_call_target="tpu_custom_call" | custom-call | bytes 2080768 | tf_op jit(solution)/shard_map/pallas_call | solution.py:672
  31.3 1.7 %collective-permute-start.8 = (bf16[4,144,128]{2,1,0:T(8,128)(2,1)S(1)}, bf16[4,144,128]{2,1,0:T(8,128)(2,1)S(1)}, u32[]{:S(2)}, u32[]{:S(2)}) collective-permute-start(bf16[4,144,128]{2,1,0:T(8,128)(2,1)S(1)} %get-tuple-element.101), channel_id=1, source_target_pairs={{0,2},{1,3},{2,0},{3,1},{4,6},{5,7},{6,4},{7,5},{8,10},{9,11},{10,... | collective-permute-start | bytes 442376 | tf_op jit(solution)/shard_map/ppermute | solution.py:684
  33.0 0.9 %collective-permute-start.9 = (bf16[4,144,128]{2,1,0:T(8,128)(2,1)S(1)}, bf16[4,144,128]{2,1,0:T(8,128)(2,1)S(1)}, u32[]{:S(2)}, u32[]{:S(2)}) collective-permute-start(bf16[4,144,128]{2,1,0:T(8,128)(2,1)S(1)} %get-tuple-element.102), channel_id=1, source_target_pairs={{0,3},{1,0},{2,1},{3,2},{4,7},{5,4},{6,5},{7,6},{8,11},{9,8},{10,9... | collective-permute-start | bytes 442376 | tf_op jit(solution)/shard_map/ppermute | solution.py:684
  33.9 4.2 %shard_map.153 = (f32[256,384]{1,0:T(8,128)S(1)}, f32[256,384]{1,0:T(8,128)S(1)}, f32[256,384]{1,0:T(8,128)S(1)}, bf16[2,256,384]{2,1,0:T(8,128)(2,1)S(1)}, bf16...) custom-call(bf16[256,1024]{1,0:T(8,128)(2,1)S(1)} %copy-done, ...), custom_call_target="tpu_custom_call" | custom-call | flops 4000000000 | bytes 6729280 | tf_op jit(solution)/shard_map/pallas_call | solution.py:672
  38.1 1.5 %collective-permute-done.9.refs_3_ = bf16[4,144,128]{2,1,0:T(8,128)(2,1)S(1)} collective-permute-done((bf16[4,144,128]{2,1,0:T(8,128)(2,1)S(1)}, bf16[4,144,128]{2,1,0:T(8,128)(2,1)S(1)}, u32[]{:S(2)}, u32[]{:S(2)}) %collective-permute-start.9) | collective-permute-done | bytes 147488 | tf_op jit(solution)/shard_map/ppermute | solution.py:684
  39.6 1.0 %shard_map.154 = (bf16[256,1024]{1,0:T(8,128)(2,1)S(1)}, bf16[256,1024]{1,0:T(8,128)(2,1)S(1)}, f32[3,1280]{1,0:T(4,128)S(1)}) custom-call(bf16[4,144,128]{2,1,0:T(8,128)(2,1)S(1)} %get-tuple-element.99.refs_9_.refs_0_, bf16[4,144,128]{2,1,0:T(8,128)(2,1)S(1)} %collective-permute-done.7.refs_1_, bf16[4,144,128]{2,1,0:T(8,128)(2,1)S(1)} %collective-permute-done.8.refs_2_, ...), custom_call_target="tpu_custom_call" | custom-call | bytes 6700032 | tf_op jit(solution)/shard_map/pallas_call | solution.py:672
  40.6 2.5 %collective-permute-start.10 = (f32[3,1280]{1,0:T(4,128)S(1)}, f32[3,1280]{1,0:T(4,128)S(1)}, u32[]{:S(2)}, u32[]{:S(2)}) collective-permute-start(f32[3,1280]{1,0:T(4,128)S(1)} %get-tuple-element.128), channel_id=1, source_target_pairs={{1,0},{2,1},{3,2},{4,3},{5,4},{6,5},{7,6},{8,7},{9,8},{10,9},{11,1... | collective-permute-start | bytes 46088 | tf_op jit(solution)/shard_map/ppermute | solution.py:775
  43.2 3.6 %shard_map.155 = (f32[256,1024]{1,0:T(8,128)}, f32[256,1024]{1,0:T(8,128)S(1)}, f32[256,256]{1,0:T(8,128)S(1)}, f32[16,256]{1,0:T(8,128)}) custom-call(bf16[256,1024]{1,0:T(8,128)(2,1)S(1)} %get-tuple-element.118.refs_0_, bf16[256,1024]{1,0:T(8,128)(2,1)S(1)} %get-tuple-element.119.refs_1_, bf16[256,128]{1,0:T(8,128)(2,1)S(1)} %get-tuple-element.120.refs_2_, ...), custom_call_target="tpu_custom_call" | custom-call | flops 2000000000 | bytes 9592960 | tf_op jit(solution)/shard_map/pallas_call | solution.py:672
  46.8 1.7 %collective-permute-done.10.after = f32[3,1280]{1,0:T(4,128)S(1)} collective-permute-done((f32[3,1280]{1,0:T(4,128)S(1)}, f32[3,1280]{1,0:T(4,128)S(1)}, u32[]{:S(2)}, u32[]{:S(2)}) %collective-permute-start.10) | collective-permute-done | bytes 15392 | tf_op jit(solution)/shard_map/ppermute | solution.py:775
  48.4 1.6 %shard_map.156 = (f32[256,1024]{1,0:T(8,128)}, f32[256,128]{1,0:T(8,128)}, f32[256,128]{1,0:T(8,128)}) custom-call(f32[256,1024]{1,0:T(8,128)S(1)} %get-tuple-element.126.dpre, f32[256,256]{1,0:T(8,128)S(1)} %get-tuple-element.127.dpre_bc, f32[3,1280]{1,0:T(4,128)S(1)} %collective-permute-done.10.after, f32[4,1280]{1,0:T(4,128)S(1)} %get-tuple-element.73.taps.refs_5_), custom_call_target="tpu_custom_call" | custom-call | bytes 2657280 | tf_op jit(solution)/shard_map/pallas_call | solution.py:672
  (31 shorter events, 2.6 us)
Async XLA Ops:
  0.6 5.0 %copy-start.3 = (bf16[256,128]{1,0:T(8,128)(2,1)S(1)}, bf16[256,128]{1,0:T(8,128)(2,1)}, u32[]{:S(2)}) copy-start(bf16[256,128]{1,0:T(8,128)(2,1)} %refs_3_.5) | copy-start | bytes 196612
  0.6 5.0 %copy-start.2 = (bf16[256,128]{1,0:T(8,128)(2,1)S(1)}, bf16[256,128]{1,0:T(8,128)(2,1)}, u32[]{:S(2)}) copy-start(bf16[256,128]{1,0:T(8,128)(2,1)} %refs_2_.5) | copy-start | bytes 196612
  0.7 5.0 %copy-start = (bf16[256,1024]{1,0:T(8,128)(2,1)S(1)}, bf16[256,1024]{1,0:T(8,128)(2,1)}, u32[]{:S(2)}) copy-start(bf16[256,1024]{1,0:T(8,128)(2,1)} %refs_0_.5) | copy-start | bytes 1572868
  0.7 5.0 %copy-start.1 = (bf16[256,1024]{1,0:T(8,128)(2,1)S(1)}, bf16[256,1024]{1,0:T(8,128)(2,1)}, u32[]{:S(2)}) copy-start(bf16[256,1024]{1,0:T(8,128)(2,1)} %refs_1_.5) | copy-start | bytes 1572868
  0.7 5.0 %copy-start.5 = (bf16[16,256]{1,0:T(8,128)(2,1)S(1)}, bf16[16,256]{1,0:T(8,128)(2,1)}, u32[]{:S(2)}) copy-start(bf16[16,256]{1,0:T(8,128)(2,1)} %refs_9_.1) | copy-start | bytes 24580
  0.7 5.0 %copy-start.4 = (f32[4,1024]{1,0:T(4,128)S(1)}, f32[4,1024]{1,0:T(4,128)}, u32[]{:S(2)}) copy-start(f32[4,1024]{1,0:T(4,128)} %taps_x.1) | copy-start | bytes 49156
  0.7 5.0 %copy-start.7 = (f32[4,128]{1,0:T(4,128)S(1)}, f32[4,128]{1,0:T(4,128)}, u32[]{:S(2)}) copy-start(f32[4,128]{1,0:T(4,128)} %taps_c.1) | copy-start | bytes 6148
  2.2 3.5 %copy-start.6 = (f32[4,128]{1,0:T(4,128)S(1)}, f32[4,128]{1,0:T(4,128)}, u32[]{:S(2)}) copy-start(f32[4,128]{1,0:T(4,128)} %taps_b.1) | copy-start | bytes 6148
  2.2 6.6 %collective-permute-start = (bf16[3,1280]{1,0:T(4,128)(2,1)}, bf16[3,1280]{1,0:T(4,128)(2,1)S(1)}, u32[]{:S(2)}, u32[]{:S(2)}) collective-permute-start(bf16[3,1280]{1,0:T(4,128)(2,1)} %shard_map.146), channel_id=1, source_target_pairs={{0,1},{1,2},{2,3},{3,4},{4,5},{5,6},{6,7},{7,8},{8,9},{9,10},{10,1... | collective-permute-start | bytes 23048 | tf_op jit(solution)/shard_map/ppermute | solution.py:709
  5.6 0.7 %copy-start.9 = (f32[16]{0:T(128)S(1)}, f32[16]{0:T(128)}, u32[]{:S(2)}) copy-start(f32[16]{0:T(128)} %param.15) | copy-start | bytes 196
  5.6 0.7 %copy-start.10 = (f32[16]{0:T(128)S(1)}, f32[16]{0:T(128)}, u32[]{:S(2)}) copy-start(f32[16]{0:T(128)} %param.16) | copy-start | bytes 196
  9.7 7.5 %collective-permute-start.1 = (bf16[4,144,128]{2,1,0:T(8,128)(2,1)S(1)}, bf16[4,144,128]{2,1,0:T(8,128)(2,1)S(1)}, u32[]{:S(2)}, u32[]{:S(2)}) collective-permute-start(bf16[4,144,128]{2,1,0:T(8,128)(2,1)S(1)} %get-tuple-element.76), channel_id=1, source_target_pairs={{0,1},{1,2},{2,3},{3,0},{4,5},{5,6},{6,7},{7,4},{8,9},{9,10},{10,1... | collective-permute-start | bytes 442376 | tf_op jit(solution)/shard_map/ppermute | solution.py:684
  10.3 8.0 %collective-permute-start.2 = (bf16[4,144,128]{2,1,0:T(8,128)(2,1)S(1)}, bf16[4,144,128]{2,1,0:T(8,128)(2,1)S(1)}, u32[]{:S(2)}, u32[]{:S(2)}) collective-permute-start(bf16[4,144,128]{2,1,0:T(8,128)(2,1)S(1)} %get-tuple-element.77), channel_id=1, source_target_pairs={{0,2},{1,3},{2,0},{3,1},{4,6},{5,7},{6,4},{7,5},{8,10},{9,11},{10,... | collective-permute-start | bytes 442376 | tf_op jit(solution)/shard_map/ppermute | solution.py:684
  12.4 7.6 %collective-permute-start.3 = (bf16[4,144,128]{2,1,0:T(8,128)(2,1)S(1)}, bf16[4,144,128]{2,1,0:T(8,128)(2,1)S(1)}, u32[]{:S(2)}, u32[]{:S(2)}) collective-permute-start(bf16[4,144,128]{2,1,0:T(8,128)(2,1)S(1)} %get-tuple-element.78), channel_id=1, source_target_pairs={{0,3},{1,0},{2,1},{3,2},{4,7},{5,4},{6,5},{7,6},{8,11},{9,8},{10,9... | collective-permute-start | bytes 442376 | tf_op jit(solution)/shard_map/ppermute | solution.py:684
  12.6 0.7 %copy-start.8 = (f32[16]{0:T(128)S(1)}, f32[16]{0:T(128)}, u32[]{:S(2)}) copy-start(f32[16]{0:T(128)} %param.17) | copy-start | bytes 196
  20.5 8.6 %collective-permute-start.4 = (bf16[4,80,128]{2,1,0:T(8,128)(2,1)S(1)}, bf16[4,80,128]{2,1,0:T(8,128)(2,1)S(1)}, u32[]{:S(2)}, u32[]{:S(2)}) collective-permute-start(bf16[4,80,128]{2,1,0:T(8,128)(2,1)S(1)} %get-tuple-element.82), channel_id=1, source_target_pairs={{0,4},{1,5},{2,6},{3,7},{4,8},{5,9},{6,10},{7,11},{8,12},{9,13},{1... | collective-permute-start | bytes 245768 | tf_op jit(solution)/shard_map/ppermute | solution.py:690
  22.6 6.6 %collective-permute-start.5 = (bf16[4,80,128]{2,1,0:T(8,128)(2,1)S(1)}, bf16[4,80,128]{2,1,0:T(8,128)(2,1)S(1)}, u32[]{:S(2)}, u32[]{:S(2)}) collective-permute-start(bf16[4,80,128]{2,1,0:T(8,128)(2,1)S(1)} %get-tuple-element.83), channel_id=1, source_target_pairs={{0,8},{1,9},{2,10},{3,11},{4,12},{5,13},{6,14},{7,15},{8,0},{9,1},... | collective-permute-start | bytes 245768 | tf_op jit(solution)/shard_map/ppermute | solution.py:690
  25.5 4.4 %collective-permute-start.6 = (bf16[4,80,128]{2,1,0:T(8,128)(2,1)S(1)}, bf16[4,80,128]{2,1,0:T(8,128)(2,1)S(1)}, u32[]{:S(2)}, u32[]{:S(2)}) collective-permute-start(bf16[4,80,128]{2,1,0:T(8,128)(2,1)S(1)} %get-tuple-element.84), channel_id=1, source_target_pairs={{0,12},{1,13},{2,14},{3,15},{4,0},{5,1},{6,2},{7,3},{8,4},{9,5},{1... | collective-permute-start | bytes 245768 | tf_op jit(solution)/shard_map/ppermute | solution.py:690
  30.7 7.4 %collective-permute-start.7 = (bf16[4,144,128]{2,1,0:T(8,128)(2,1)S(1)}, bf16[4,144,128]{2,1,0:T(8,128)(2,1)S(1)}, u32[]{:S(2)}, u32[]{:S(2)}) collective-permute-start(bf16[4,144,128]{2,1,0:T(8,128)(2,1)S(1)} %get-tuple-element.100), channel_id=1, source_target_pairs={{0,1},{1,2},{2,3},{3,0},{4,5},{5,6},{6,7},{7,4},{8,9},{9,10},{10,1... | collective-permute-start | bytes 442376 | tf_op jit(solution)/shard_map/ppermute | solution.py:684
  31.3 6.8 %collective-permute-start.8 = (bf16[4,144,128]{2,1,0:T(8,128)(2,1)S(1)}, bf16[4,144,128]{2,1,0:T(8,128)(2,1)S(1)}, u32[]{:S(2)}, u32[]{:S(2)}) collective-permute-start(bf16[4,144,128]{2,1,0:T(8,128)(2,1)S(1)} %get-tuple-element.101), channel_id=1, source_target_pairs={{0,2},{1,3},{2,0},{3,1},{4,6},{5,7},{6,4},{7,5},{8,10},{9,11},{10,... | collective-permute-start | bytes 442376 | tf_op jit(solution)/shard_map/ppermute | solution.py:684
  33.0 6.6 %collective-permute-start.9 = (bf16[4,144,128]{2,1,0:T(8,128)(2,1)S(1)}, bf16[4,144,128]{2,1,0:T(8,128)(2,1)S(1)}, u32[]{:S(2)}, u32[]{:S(2)}) collective-permute-start(bf16[4,144,128]{2,1,0:T(8,128)(2,1)S(1)} %get-tuple-element.102), channel_id=1, source_target_pairs={{0,3},{1,0},{2,1},{3,2},{4,7},{5,4},{6,5},{7,6},{8,11},{9,8},{10,9... | collective-permute-start | bytes 442376 | tf_op jit(solution)/shard_map/ppermute | solution.py:684
  40.6 7.8 %collective-permute-start.10 = (f32[3,1280]{1,0:T(4,128)S(1)}, f32[3,1280]{1,0:T(4,128)S(1)}, u32[]{:S(2)}, u32[]{:S(2)}) collective-permute-start(f32[3,1280]{1,0:T(4,128)S(1)} %get-tuple-element.128), channel_id=1, source_target_pairs={{1,0},{2,1},{3,2},{4,3},{5,4},{6,5},{7,6},{8,7},{9,8},{10,9},{11,1... | collective-permute-start | bytes 46088 | tf_op jit(solution)/shard_map/ppermute | solution.py:775

commit v4 on v3

--- a/solution.py
+++ b/solution.py
@@ -175,7 +175,7 @@
 C_LANES = pl.ds(WIDTH + STATE, STATE)
 
 
-def edge_kernel(x_raw, b_raw, c_raw, edge, scr, sems):
+def edge_kernel(x_raw, b_raw, c_raw, dt_bias, a_log, skip, edge, params, scr, rows_scr, sems):
     rows = pl.ds(TOKENS - 16, 16)
     wait(
         begin(
@@ -183,32 +183,32 @@
                 (x_raw.at[rows, :], scr.at[:, pl.ds(0, WIDTH)]),
                 (b_raw.at[rows, :], scr.at[:, B_LANES]),
                 (c_raw.at[rows, :], scr.at[:, C_LANES]),
+                (dt_bias, rows_scr.at[0]),
+                (a_log, rows_scr.at[1]),
+                (skip, rows_scr.at[2]),
             ],
             sems,
         )
     )
     edge[...] = scr[...].astype(f32)[16 - RIM :].astype(bf16)
+    for n in range(3):
+        params[n] = jnp.broadcast_to(rows_scr[n], (8, HEADS))
 
 
 def first_kernel(
-    xs, gs, bs, cs, dts, bias, rate, taps_x, taps_b, taps_c,
+    xs, gs, bs, cs, dts, params, taps_x, taps_b, taps_c,
     sg, pre16, end16, ge16, taps_out, total_out, cum_out, step_out, columns_out,
     rows_scr,
 ):
-    pre = dts[...].astype(f32) + to_column(bias[...])
+    pre = dts[...].astype(f32) + to_column(params[0][0:1])
     step = jnp.maximum(pre, 0.0) + jnp.log1p(jnp.exp(-jnp.abs(pre)))
-    log_decay = -jnp.exp(to_column(rate[...])) * step
+    log_decay = -jnp.exp(to_column(params[1][0:1])) * step
     r, c = iota((TOKENS, TOKENS), 0), iota((TOKENS, TOKENS), 1)
     upto = onehot((r <= c) & (r // SUB == c // SUB))
     parts = split3(log_decay)
     cum = dot(parts[2], upto) + dot(parts[1], upto) + dot(parts[0], upto)
-    cum_out[...] = cum
-    step_out[...] = step
     _, _, from_start, to_end, total = decay_terms(cum, step)
-    for head in range(HEADS):
-        total_out[head] = jnp.broadcast_to(total[head : head + 1], (8, 128))
     columns = stack_columns([from_start, to_end])
-    columns_out[...] = columns
     taps_out[:, 0:WIDTH] = taps_x[...]
     taps_out[:, WIDTH : WIDTH + STATE] = taps_b[...]
     taps_out[:, WIDTH + STATE :] = taps_c[...]
@@ -235,6 +235,11 @@
         ge16[:, lanes] = ge[:16]
         sg[0, :, lanes] = dot3(bt, split2(xw))
         sg[1, :, lanes] = dot3(ct, split2(ge))
+    cum_out[...] = cum
+    step_out[...] = step
+    columns_out[...] = columns
+    for head in range(HEADS):
+        total_out[head] = jnp.broadcast_to(total[head : head + 1], (8, 128))
 
 
 def quarter(q):
@@ -463,7 +468,7 @@
             total += dot(jnp.concatenate(split2(v), axis=1), hot)
         acc[...] = total
         dg[...] += step_x * xg
-        direct = jnp.where(low_half((TOKENS, 128)), skip[:, head : head + 1], skip[:, head + 1 : head + 2]) + diag_scr[...] * step_x
+        direct = jnp.where(low_half((TOKENS, 128)), skip[2][0:1, head : head + 1], skip[2][0:1, head + 1 : head + 2]) + diag_scr[...] * step_x
         ys[:, local] = y + direct * x
         dxs[:, local] = dx + direct * gf
 
@@ -525,7 +530,7 @@
     return dot(jnp.concatenate([a2[0], a2[0]], axis=1), cat[:, lanes]) + dot(a2[1], cat[:STATE, lanes])
 
 
-GROUP_PAIRS = (3, 2, 3)
+GROUP_PAIRS = (4, 2, 2)
 
 
 def columns_of(refs, n, *lead):
@@ -575,7 +580,7 @@
 
 
 def main_kernel(*refs):
-    (e_cat, f_cat, columns, bc, dbc, slope_bc, sums, cums, steps, dts, bias, rate), refs = refs[:12], refs[12:]
+    (e_cat, f_cat, columns, bc, dbc, slope_bc, sums, cums, steps, dts, params), refs = refs[:11], refs[11:]
     groups, (y_out, dpre, dpre_bc, dt_out, ys, gdt, out_sems) = refs[:15], refs[15:]
     b2, c2 = split2(bc[:, :STATE]), split2(bc[:, STATE:])
     grads = [[jnp.zeros((TOKENS, PART), f32), jnp.zeros((TOKENS, STATE), f32)] for _ in range(2)]
@@ -626,8 +631,8 @@
     cum, step = cums[...], steps[...]
     ends = jnp.exp(cum[:, SUB - 1 : SUB] + cum[:, TOKENS - 1 : TOKENS])
     d_decay = summed(sums[0] + kept, suffix) + summed(later, prefix) + ends * to_column(both[0:1, 0:HEADS])
-    d_step = sums[1] + later / step - jnp.exp(to_column(rate[...])) * d_decay
-    pre = dts[...].astype(f32) + to_column(bias[...])
+    d_step = sums[1] + later / step - jnp.exp(to_column(params[1][0:1])) * d_decay
+    pre = dts[...].astype(f32) + to_column(params[0][0:1])
     gdt[...] = d_step / (1.0 + jnp.exp(-pre))
     out.append(pltpu.make_async_copy(gdt, dt_out, out_sems.at[PARTS]))
     out[-1].start()
@@ -702,14 +707,19 @@
     def near(*arrays):
         return [(a, VMEM) for a in arrays]
 
-    (edge,) = call(
-        edge_kernel, [(a, HBM) for a in (x_raw, b_raw, c_raw)], [((RIM, ALL), bf16, VMEM)], [((16, ALL), bf16)], [3],
-        mib=60, flops=2_000_000_000,
+    edge, params = call(
+        edge_kernel,
+        [(a, HBM) for a in (x_raw, b_raw, c_raw, dt_bias, a_log, skip_gain)],
+        [((RIM, ALL), bf16, VMEM), ((3, 8, HEADS), f32, VMEM)],
+        [((16, ALL), bf16), ((3, 1, HEADS), f32)],
+        [6],
+        flops=2_000_000_000,
+        mib=60,
     )
     before = lax.ppermute(edge, "context", [(i, i + 1) for i in range(RANKS - 1)])
     sg, pre16, end16, ge16, taps, total, cum, step, columns = call(
         first_kernel,
-        near(x_raw, grad_y, b_raw, c_raw, dt_raw, dt_bias, a_log, conv_x, conv_b, conv_c),
+        near(x_raw, grad_y, b_raw, c_raw, dt_raw, params, conv_x, conv_b, conv_c),
         [((2, STATE, WIDTH), f32, VMEM), ((16, ALL), f32, VMEM), (rim16, f32, VMEM), (rim16, f32, VMEM),
          ((4, ALL), f32, VMEM), ((HEADS, 8, 128), f32, VMEM), (slim, f32, VMEM), (slim, f32, VMEM),
          ((TOKENS, 128), bf16, VMEM)],
@@ -737,7 +747,7 @@
             outs += [(bc, f32, VMEM), ((2,) + slim, f32, VMEM)]
         return call(
             functools.partial(block_kernel, first_pair, count),
-            near(x_raw, grad_y, b_raw, c_raw, before, taps, cum, step, skip_gain, after_this, *shared),
+            near(x_raw, grad_y, b_raw, c_raw, before, taps, cum, step, params, after_this, *shared),
             outs + carried,
             [((TOKENS + 8, ALL), f32)],
             flops=4_000_000_000,
@@ -775,7 +785,7 @@
     after = lax.ppermute(rim, "context", [(i, i - 1) for i in range(1, RANKS)])
     y_out, dpre, dpre_bc, grad_dt = call(
         main_kernel,
-        near(e_cat, f_cat, columns, bcs, dbc, slope_bc, sums, cum, step, dt_raw, dt_bias, a_log, *[a for g in groups for a in g]),
+        near(e_cat, f_cat, columns, bcs, dbc, slope_bc, sums, cum, step, dt_raw, params, *[a for g in groups for a in g]),
         [(wide, f32, HBM), (wide, f32, VMEM), (bc, f32, VMEM), (slim, f32, HBM)],
         [(wide, f32), (slim, f32)],
         [PARTS + 1],

time: 51 us -> 51.2 us (level)
  local copies, waits for them, and re-layouts: 1.27 us -> 0.74 us
    ppermute x6, waiting for transfers between devices: 4.3 us -> 5.07 us  [along_row(): lax.ppermute(block, 'context', [(SIDE * y + x, SIDE * y + (x + shift) % S...]
    unnamed x22 -> x20, local copies, waits for them, and re-layouts: 1.27 us -> 0.74 us
  transfers between devices with their start and end apart: 11 -> 11, of which waited for: 5 -> 6; matrix products, arithmetic and copies ran while one was open for 0% -> 0% of each run, Pallas kernels for 33% -> 33%
where the time goes in v4:
time: 51.2 us; the launch traced here: 50.2 us
  Pallas kernels  22.7 us (44%)
  starting transfers between devices  18.6 us (36%)
  waiting for transfers between devices  7.09 us (14%)
  between operations  1.06 us (2%)
  local copies, waits for them, and re-layouts  0.74 us (1%)
    pallas_call x11, Pallas kernels, call(): pl.pallas_call(kernel, out_shape=shapes, in_specs=[w for _, w in ins], ou...  22.7 us
    ppermute x3, starting transfers between devices, along_column(): lax.ppermute(block, 'context', [(SIDE * y + x, SIDE * ((y + shift) % SIDE...  6.2 us
    ppermute x6, starting transfers between devices, along_row(): lax.ppermute(block, 'context', [(SIDE * y + x, SIDE * y + (x + shift) % S...  6.15 us
    ppermute x6, waiting for transfers between devices, along_row(): lax.ppermute(block, 'context', [(SIDE * y + x, SIDE * y + (x + shift) % S...  5.07 us
    ppermute x1, starting transfers between devices, on_device(): lax.ppermute(edge, 'context', [(i, i + 1) for i in range(RANKS - 1)])  3.4 us
    ppermute x1, starting transfers between devices, on_device(): after = lax.ppermute(rim, 'context', [(i, i - 1) for i in range(1, RANKS)])  2.85 us
    ppermute x1, waiting for transfers between devices, on_device(): after = lax.ppermute(rim, 'context', [(i, i - 1) for i in range(1, RANKS)])  1.25 us
  transfers between devices with their start and end apart: 11, of which 6 were waited for; matrix products, arithmetic and copies ran while one was open for 0% of the time, Pallas kernels for 33%

profile of v4, /device:TPU:38, one launch (start us, length us, event | category | flops | bytes accessed | tf_op | source)
XLA Modules:
  0.0 50.2 jit_solution(6707895377947908116)
XLA Ops:
  0.7 1.5 %shard_map.146 = (bf16[3,1280]{1,0:T(4,128)(2,1)}, f32[3,8,16]{2,1,0:T(8,128)}) custom-call(bf16[256,1024]{1,0:T(8,128)(2,1)} %refs_0_.5, bf16[256,128]{1,0:T(8,128)(2,1)} %refs_2_.5, bf16[256,128]{1,0:T(8,128)(2,1)} %refs_3_.5, f32[1,16]{1,0:T(1,128)} %bitcast.3, f32[1,16]{1,0:T(1,128)} %bitcast.4, f32[1,16]{1,0:T(1,128)} %bitcast.5), custom_call_target="tpu_custom_call" | custom-call | flops 2000000000 | bytes 664768 | tf_op jit(solution)/shard_map/pallas_call | solution.py:677
  2.2 3.4 %collective-permute-start = (bf16[3,1280]{1,0:T(4,128)(2,1)}, bf16[3,1280]{1,0:T(4,128)(2,1)S(1)}, u32[]{:S(2)}, u32[]{:S(2)}) collective-permute-start(bf16[3,1280]{1,0:T(4,128)(2,1)} %get-tuple-element.71), channel_id=1, source_target_pairs={{0,1},{1,2},{2,3},{3,4},{4,5},{5,6},{6,7},{7,8},{8,9},{9,10},{10,1... | collective-permute-start | bytes 23048 | tf_op jit(solution)/shard_map/ppermute | solution.py:719
  6.4 2.5 %shard_map.147 = (f32[2,128,1024]{2,1,0:T(8,128)S(1)}, f32[16,1280]{1,0:T(8,128)S(1)}, f32[16,1024]{1,0:T(8,128)S(1)}, f32[16,1024]{1,0:T(8,128)S(1)}, f32[4,128...) custom-call(bf16[256,1024]{1,0:T(8,128)(2,1)S(1)} %copy-done, ...), custom_call_target="tpu_custom_call" | custom-call | flops 2000000000 | bytes 2655744 | tf_op jit(solution)/shard_map/pallas_call | solution.py:677
  9.0 0.9 %shard_map.148 = (bf16[4,144,128]{2,1,0:T(8,128)(2,1)S(1)}, bf16[4,144,128]{2,1,0:T(8,128)(2,1)S(1)}, bf16[4,144,128]{2,1,0:T(8,128)(2,1)S(1)}, bf16[4,144,128]{2,1,0:T(8,128)(2,1)S(1)}) custom-call(bf16[3,1280]{1,0:T(4,128)(2,1)S(1)} %collective-permute-done.before.refs_4_, f32[2,128,1024]{2,1,0:T(8,128)S(1)} %get-tuple-element.73.sg, ...), custom_call_target="tpu_custom_call" | custom-call | bytes 1945088 | tf_op jit(solution)/shard_map/pallas_call | solution.py:677
  10.4 2.1 %collective-permute-start.2 = (bf16[4,144,128]{2,1,0:T(8,128)(2,1)S(1)}, bf16[4,144,128]{2,1,0:T(8,128)(2,1)S(1)}, u32[]{:S(2)}, u32[]{:S(2)}) collective-permute-start(bf16[4,144,128]{2,1,0:T(8,128)(2,1)S(1)} %get-tuple-element.81), channel_id=1, source_target_pairs={{0,2},{1,3},{2,0},{3,1},{4,6},{5,7},{6,4},{7,5},{8,10},{9,11},{10,... | collective-permute-start | bytes 442376 | tf_op jit(solution)/shard_map/ppermute | solution.py:689
  12.8 4.9 %shard_map.149 = (f32[256,512]{1,0:T(8,128)S(1)}, f32[256,512]{1,0:T(8,128)S(1)}, f32[256,512]{1,0:T(8,128)S(1)}, bf16[2,256,512]{2,1,0:T(8,128)(2,1)S(1)}, bf16...) custom-call(bf16[256,1024]{1,0:T(8,128)(2,1)S(1)} %copy-done, ...), custom_call_target="tpu_custom_call" | custom-call | flops 4000000000 | bytes 6632448 | tf_op jit(solution)/shard_map/pallas_call | solution.py:677
  17.7 0.8 %collective-permute-done.2.refs_2_ = bf16[4,144,128]{2,1,0:T(8,128)(2,1)S(1)} collective-permute-done((bf16[4,144,128]{2,1,0:T(8,128)(2,1)S(1)}, bf16[4,144,128]{2,1,0:T(8,128)(2,1)S(1)}, u32[]{:S(2)}, u32[]{:S(2)}) %collective-permute-start.2) | collective-permute-done | bytes 147488 | tf_op jit(solution)/shard_map/ppermute | solution.py:689
  18.5 1.6 %collective-permute-done.3.refs_3_ = bf16[4,144,128]{2,1,0:T(8,128)(2,1)S(1)} collective-permute-done((bf16[4,144,128]{2,1,0:T(8,128)(2,1)S(1)}, bf16[4,144,128]{2,1,0:T(8,128)(2,1)S(1)}, u32[]{:S(2)}, u32[]{:S(2)}) %collective-permute-start.3) | collective-permute-done | bytes 147488 | tf_op jit(solution)/shard_map/ppermute | solution.py:689
  20.7 2.0 %collective-permute-start.4 = (bf16[4,80,128]{2,1,0:T(8,128)(2,1)S(1)}, bf16[4,80,128]{2,1,0:T(8,128)(2,1)S(1)}, u32[]{:S(2)}, u32[]{:S(2)}) collective-permute-start(bf16[4,80,128]{2,1,0:T(8,128)(2,1)S(1)} %get-tuple-element.86), channel_id=1, source_target_pairs={{0,4},{1,5},{2,6},{3,7},{4,8},{5,9},{6,10},{7,11},{8,12},{9,13},{1... | collective-permute-start | bytes 245768 | tf_op jit(solution)/shard_map/ppermute | solution.py:695
  22.6 2.9 %collective-permute-start.5 = (bf16[4,80,128]{2,1,0:T(8,128)(2,1)S(1)}, bf16[4,80,128]{2,1,0:T(8,128)(2,1)S(1)}, u32[]{:S(2)}, u32[]{:S(2)}) collective-permute-start(bf16[4,80,128]{2,1,0:T(8,128)(2,1)S(1)} %get-tuple-element.87), channel_id=1, source_target_pairs={{0,8},{1,9},{2,10},{3,11},{4,12},{5,13},{6,14},{7,15},{8,0},{9,1},... | collective-permute-start | bytes 245768 | tf_op jit(solution)/shard_map/ppermute | solution.py:695
  25.5 1.3 %collective-permute-start.6 = (bf16[4,80,128]{2,1,0:T(8,128)(2,1)S(1)}, bf16[4,80,128]{2,1,0:T(8,128)(2,1)S(1)}, u32[]{:S(2)}, u32[]{:S(2)}) collective-permute-start(bf16[4,80,128]{2,1,0:T(8,128)(2,1)S(1)} %get-tuple-element.88), channel_id=1, source_target_pairs={{0,12},{1,13},{2,14},{3,15},{4,0},{5,1},{6,2},{7,3},{8,4},{9,5},{1... | collective-permute-start | bytes 245768 | tf_op jit(solution)/shard_map/ppermute | solution.py:695
  26.9 2.3 %shard_map.151 = (f32[256,256]{1,0:T(8,128)S(1)}, f32[256,256]{1,0:T(8,128)S(1)}, f32[256,256]{1,0:T(8,128)S(1)}, bf16[2,256,256]{2,1,0:T(8,128)(2,1)S(1)}, bf16...) custom-call(bf16[256,1024]{1,0:T(8,128)(2,1)S(1)} %copy-done, ...), custom_call_target="tpu_custom_call" | custom-call | flops 4000000000 | bytes 5698560 | tf_op jit(solution)/shard_map/pallas_call | solution.py:677
  29.2 0.8 %collective-permute-done.6.refs_2_ = bf16[4,80,128]{2,1,0:T(8,128)(2,1)S(1)} collective-permute-done((bf16[4,80,128]{2,1,0:T(8,128)(2,1)S(1)}, bf16[4,80,128]{2,1,0:T(8,128)(2,1)S(1)}, u32[]{:S(2)}, u32[]{:S(2)}) %collective-permute-start.6) | collective-permute-done | bytes 81952 | tf_op jit(solution)/shard_map/ppermute | solution.py:695
  30.0 0.8 %shard_map.152 = (bf16[4,144,128]{2,1,0:T(8,128)(2,1)S(1)}, bf16[4,144,128]{2,1,0:T(8,128)(2,1)S(1)}, bf16[4,144,128]{2,1,0:T(8,128)(2,1)S(1)}, bf16[4,144,128]{2,1,0:T(8,128)(2,1)S(1)}) custom-call(bf16[4,80,128]{2,1,0:T(8,128)(2,1)S(1)} %collective-permute-done.4.refs_0_, bf16[4,80,128]{2,1,0:T(8,128)(2,1)S(1)} %collective-permute-done.5.refs_1_, ...), custom_call_target="tpu_custom_call" | custom-call | bytes 2080768 | tf_op jit(solution)/shard_map/pallas_call | solution.py:677
  31.4 1.9 %collective-permute-start.8 = (bf16[4,144,128]{2,1,0:T(8,128)(2,1)S(1)}, bf16[4,144,128]{2,1,0:T(8,128)(2,1)S(1)}, u32[]{:S(2)}, u32[]{:S(2)}) collective-permute-start(bf16[4,144,128]{2,1,0:T(8,128)(2,1)S(1)} %get-tuple-element.105), channel_id=1, source_target_pairs={{0,2},{1,3},{2,0},{3,1},{4,6},{5,7},{6,4},{7,5},{8,10},{9,11},{10,... | collective-permute-start | bytes 442376 | tf_op jit(solution)/shard_map/ppermute | solution.py:689
  33.2 0.7 %collective-permute-start.9 = (bf16[4,144,128]{2,1,0:T(8,128)(2,1)S(1)}, bf16[4,144,128]{2,1,0:T(8,128)(2,1)S(1)}, u32[]{:S(2)}, u32[]{:S(2)}) collective-permute-start(bf16[4,144,128]{2,1,0:T(8,128)(2,1)S(1)} %get-tuple-element.106), channel_id=1, source_target_pairs={{0,3},{1,0},{2,1},{3,2},{4,7},{5,4},{6,5},{7,6},{8,11},{9,8},{10,9... | collective-permute-start | bytes 442376 | tf_op jit(solution)/shard_map/ppermute | solution.py:689
  34.0 3.0 %shard_map.153 = (f32[256,256]{1,0:T(8,128)S(1)}, f32[256,256]{1,0:T(8,128)S(1)}, f32[256,256]{1,0:T(8,128)S(1)}, bf16[2,256,256]{2,1,0:T(8,128)(2,1)S(1)}, bf16...) custom-call(bf16[256,1024]{1,0:T(8,128)(2,1)S(1)} %copy-done, ...), custom_call_target="tpu_custom_call" | custom-call | flops 4000000000 | bytes 6075392 | tf_op jit(solution)/shard_map/pallas_call | solution.py:677
  36.9 1.1 %collective-permute-done.8.refs_2_ = bf16[4,144,128]{2,1,0:T(8,128)(2,1)S(1)} collective-permute-done((bf16[4,144,128]{2,1,0:T(8,128)(2,1)S(1)}, bf16[4,144,128]{2,1,0:T(8,128)(2,1)S(1)}, u32[]{:S(2)}, u32[]{:S(2)}) %collective-permute-start.8) | collective-permute-done | bytes 147488 | tf_op jit(solution)/shard_map/ppermute | solution.py:689
  38.0 1.6 %collective-permute-done.9.refs_3_ = bf16[4,144,128]{2,1,0:T(8,128)(2,1)S(1)} collective-permute-done((bf16[4,144,128]{2,1,0:T(8,128)(2,1)S(1)}, bf16[4,144,128]{2,1,0:T(8,128)(2,1)S(1)}, u32[]{:S(2)}, u32[]{:S(2)}) %collective-permute-start.9) | collective-permute-done | bytes 147488 | tf_op jit(solution)/shard_map/ppermute | solution.py:689
  39.6 1.0 %shard_map.154 = (bf16[256,1024]{1,0:T(8,128)(2,1)S(1)}, bf16[256,1024]{1,0:T(8,128)(2,1)S(1)}, f32[3,1280]{1,0:T(4,128)S(1)}) custom-call(bf16[4,144,128]{2,1,0:T(8,128)(2,1)S(1)} %get-tuple-element.103.refs_9_.refs_0_, bf16[4,144,128]{2,1,0:T(8,128)(2,1)S(1)} %collective-permute-done.7.refs_1_, bf16[4,144,128]{2,1,0:T(8,128)(2,1)S(1)} %collective-permute-done.8.refs_2_, ...), custom_call_target="tpu_custom_call" | custom-call | bytes 6700032 | tf_op jit(solution)/shard_map/pallas_call | solution.py:677
  40.6 2.8 %collective-permute-start.10 = (f32[3,1280]{1,0:T(4,128)S(1)}, f32[3,1280]{1,0:T(4,128)S(1)}, u32[]{:S(2)}, u32[]{:S(2)}) collective-permute-start(f32[3,1280]{1,0:T(4,128)S(1)} %get-tuple-element.132), channel_id=1, source_target_pairs={{1,0},{2,1},{3,2},{4,3},{5,4},{6,5},{7,6},{8,7},{9,8},{10,9},{11,1... | collective-permute-start | bytes 46088 | tf_op jit(solution)/shard_map/ppermute | solution.py:785
  43.4 3.7 %shard_map.155 = (f32[256,1024]{1,0:T(8,128)}, f32[256,1024]{1,0:T(8,128)S(1)}, f32[256,256]{1,0:T(8,128)S(1)}, f32[16,256]{1,0:T(8,128)}) custom-call(bf16[256,1024]{1,0:T(8,128)(2,1)S(1)} %get-tuple-element.122.refs_0_, bf16[256,1024]{1,0:T(8,128)(2,1)S(1)} %get-tuple-element.123.refs_1_, bf16[256,128]{1,0:T(8,128)(2,1)S(1)} %get-tuple-element.124.refs_2_, ...), custom_call_target="tpu_custom_call" | custom-call | flops 2000000000 | bytes 9594368 | tf_op jit(solution)/shard_map/pallas_call | solution.py:677
  47.1 1.2 %collective-permute-done.10.after = f32[3,1280]{1,0:T(4,128)S(1)} collective-permute-done((f32[3,1280]{1,0:T(4,128)S(1)}, f32[3,1280]{1,0:T(4,128)S(1)}, u32[]{:S(2)}, u32[]{:S(2)}) %collective-permute-start.10) | collective-permute-done | bytes 15392 | tf_op jit(solution)/shard_map/ppermute | solution.py:785
  48.4 1.7 %shard_map.156 = (f32[256,1024]{1,0:T(8,128)}, f32[256,128]{1,0:T(8,128)}, f32[256,128]{1,0:T(8,128)}) custom-call(f32[256,1024]{1,0:T(8,128)S(1)} %get-tuple-element.130.dpre, f32[256,256]{1,0:T(8,128)S(1)} %get-tuple-element.131.dpre_bc, f32[3,1280]{1,0:T(4,128)S(1)} %collective-permute-done.10.after, f32[4,1280]{1,0:T(4,128)S(1)} %get-tuple-element.77.taps.refs_5_), custom_call_target="tpu_custom_call" | custom-call | bytes 2657280 | tf_op jit(solution)/shard_map/pallas_call | solution.py:677
  (29 shorter events, 2.7 us)
Async XLA Ops:
  0.6 5.0 %copy-start = (bf16[256,1024]{1,0:T(8,128)(2,1)S(1)}, bf16[256,1024]{1,0:T(8,128)(2,1)}, u32[]{:S(2)}) copy-start(bf16[256,1024]{1,0:T(8,128)(2,1)} %refs_0_.5) | copy-start | bytes 1572868
  0.6 5.0 %copy-start.1 = (bf16[256,1024]{1,0:T(8,128)(2,1)S(1)}, bf16[256,1024]{1,0:T(8,128)(2,1)}, u32[]{:S(2)}) copy-start(bf16[256,1024]{1,0:T(8,128)(2,1)} %refs_1_.5) | copy-start | bytes 1572868
  0.7 5.0 %copy-start.2 = (bf16[256,128]{1,0:T(8,128)(2,1)S(1)}, bf16[256,128]{1,0:T(8,128)(2,1)}, u32[]{:S(2)}) copy-start(bf16[256,128]{1,0:T(8,128)(2,1)} %refs_2_.5) | copy-start | bytes 196612
  0.7 5.0 %copy-start.3 = (bf16[256,128]{1,0:T(8,128)(2,1)S(1)}, bf16[256,128]{1,0:T(8,128)(2,1)}, u32[]{:S(2)}) copy-start(bf16[256,128]{1,0:T(8,128)(2,1)} %refs_3_.5) | copy-start | bytes 196612
  0.7 5.0 %copy-start.4 = (f32[4,1024]{1,0:T(4,128)S(1)}, f32[4,1024]{1,0:T(4,128)}, u32[]{:S(2)}) copy-start(f32[4,1024]{1,0:T(4,128)} %taps_x.1) | copy-start | bytes 49156
  0.7 5.0 %copy-start.5 = (bf16[16,256]{1,0:T(8,128)(2,1)S(1)}, bf16[16,256]{1,0:T(8,128)(2,1)}, u32[]{:S(2)}) copy-start(bf16[16,256]{1,0:T(8,128)(2,1)} %refs_9_.1) | copy-start | bytes 24580
  0.7 5.0 %copy-start.7 = (f32[4,128]{1,0:T(4,128)S(1)}, f32[4,128]{1,0:T(4,128)}, u32[]{:S(2)}) copy-start(f32[4,128]{1,0:T(4,128)} %taps_c.1) | copy-start | bytes 6148
  2.2 3.5 %copy-start.6 = (f32[4,128]{1,0:T(4,128)S(1)}, f32[4,128]{1,0:T(4,128)}, u32[]{:S(2)}) copy-start(f32[4,128]{1,0:T(4,128)} %taps_b.1) | copy-start | bytes 6148
  2.2 6.7 %collective-permute-start = (bf16[3,1280]{1,0:T(4,128)(2,1)}, bf16[3,1280]{1,0:T(4,128)(2,1)S(1)}, u32[]{:S(2)}, u32[]{:S(2)}) collective-permute-start(bf16[3,1280]{1,0:T(4,128)(2,1)} %get-tuple-element.71), channel_id=1, source_target_pairs={{0,1},{1,2},{2,3},{3,4},{4,5},{5,6},{6,7},{7,8},{8,9},{9,10},{10,1... | collective-permute-start | bytes 23048 | tf_op jit(solution)/shard_map/ppermute | solution.py:719
  5.7 0.7 %copy-start.8 = (f32[3,8,16]{2,1,0:T(8,128)S(1)}, f32[3,8,16]{2,1,0:T(8,128)}, u32[]{:S(2)}) copy-start(f32[3,8,16]{2,1,0:T(8,128)} %get-tuple-element.72.params.refs_8_.refs_10_) | copy-start | bytes 4612
  9.9 7.8 %collective-permute-start.1 = (bf16[4,144,128]{2,1,0:T(8,128)(2,1)S(1)}, bf16[4,144,128]{2,1,0:T(8,128)(2,1)S(1)}, u32[]{:S(2)}, u32[]{:S(2)}) collective-permute-start(bf16[4,144,128]{2,1,0:T(8,128)(2,1)S(1)} %get-tuple-element.80), channel_id=1, source_target_pairs={{0,1},{1,2},{2,3},{3,0},{4,5},{5,6},{6,7},{7,4},{8,9},{9,10},{10,1... | collective-permute-start | bytes 442376 | tf_op jit(solution)/shard_map/ppermute | solution.py:689
  10.4 8.1 %collective-permute-start.2 = (bf16[4,144,128]{2,1,0:T(8,128)(2,1)S(1)}, bf16[4,144,128]{2,1,0:T(8,128)(2,1)S(1)}, u32[]{:S(2)}, u32[]{:S(2)}) collective-permute-start(bf16[4,144,128]{2,1,0:T(8,128)(2,1)S(1)} %get-tuple-element.81), channel_id=1, source_target_pairs={{0,2},{1,3},{2,0},{3,1},{4,6},{5,7},{6,4},{7,5},{8,10},{9,11},{10,... | collective-permute-start | bytes 442376 | tf_op jit(solution)/shard_map/ppermute | solution.py:689
  12.5 7.6 %collective-permute-start.3 = (bf16[4,144,128]{2,1,0:T(8,128)(2,1)S(1)}, bf16[4,144,128]{2,1,0:T(8,128)(2,1)S(1)}, u32[]{:S(2)}, u32[]{:S(2)}) collective-permute-start(bf16[4,144,128]{2,1,0:T(8,128)(2,1)S(1)} %get-tuple-element.82), channel_id=1, source_target_pairs={{0,3},{1,0},{2,1},{3,2},{4,7},{5,4},{6,5},{7,6},{8,11},{9,8},{10,9... | collective-permute-start | bytes 442376 | tf_op jit(solution)/shard_map/ppermute | solution.py:689
  20.6 6.2 %copy-start.9 = (f32[3,8,16]{2,1,0:T(8,128)S(1)}, f32[3,8,16]{2,1,0:T(8,128)}, u32[]{:S(2)}) copy-start(f32[3,8,16]{2,1,0:T(8,128)} %get-tuple-element.72.params.refs_8_.refs_10_) | copy-start | bytes 4612
  20.7 8.5 %collective-permute-start.4 = (bf16[4,80,128]{2,1,0:T(8,128)(2,1)S(1)}, bf16[4,80,128]{2,1,0:T(8,128)(2,1)S(1)}, u32[]{:S(2)}, u32[]{:S(2)}) collective-permute-start(bf16[4,80,128]{2,1,0:T(8,128)(2,1)S(1)} %get-tuple-element.86), channel_id=1, source_target_pairs={{0,4},{1,5},{2,6},{3,7},{4,8},{5,9},{6,10},{7,11},{8,12},{9,13},{1... | collective-permute-start | bytes 245768 | tf_op jit(solution)/shard_map/ppermute | solution.py:695
  22.6 6.6 %collective-permute-start.5 = (bf16[4,80,128]{2,1,0:T(8,128)(2,1)S(1)}, bf16[4,80,128]{2,1,0:T(8,128)(2,1)S(1)}, u32[]{:S(2)}, u32[]{:S(2)}) collective-permute-start(bf16[4,80,128]{2,1,0:T(8,128)(2,1)S(1)} %get-tuple-element.87), channel_id=1, source_target_pairs={{0,8},{1,9},{2,10},{3,11},{4,12},{5,13},{6,14},{7,15},{8,0},{9,1},... | collective-permute-start | bytes 245768 | tf_op jit(solution)/shard_map/ppermute | solution.py:695
  25.5 4.4 %collective-permute-start.6 = (bf16[4,80,128]{2,1,0:T(8,128)(2,1)S(1)}, bf16[4,80,128]{2,1,0:T(8,128)(2,1)S(1)}, u32[]{:S(2)}, u32[]{:S(2)}) collective-permute-start(bf16[4,80,128]{2,1,0:T(8,128)(2,1)S(1)} %get-tuple-element.88), channel_id=1, source_target_pairs={{0,12},{1,13},{2,14},{3,15},{4,0},{5,1},{6,2},{7,3},{8,4},{9,5},{1... | collective-permute-start | bytes 245768 | tf_op jit(solution)/shard_map/ppermute | solution.py:695
  30.7 6.2 %collective-permute-start.7 = (bf16[4,144,128]{2,1,0:T(8,128)(2,1)S(1)}, bf16[4,144,128]{2,1,0:T(8,128)(2,1)S(1)}, u32[]{:S(2)}, u32[]{:S(2)}) collective-permute-start(bf16[4,144,128]{2,1,0:T(8,128)(2,1)S(1)} %get-tuple-element.104), channel_id=1, source_target_pairs={{0,1},{1,2},{2,3},{3,0},{4,5},{5,6},{6,7},{7,4},{8,9},{9,10},{10,1... | collective-permute-start | bytes 442376 | tf_op jit(solution)/shard_map/ppermute | solution.py:689
  31.4 6.6 %collective-permute-start.8 = (bf16[4,144,128]{2,1,0:T(8,128)(2,1)S(1)}, bf16[4,144,128]{2,1,0:T(8,128)(2,1)S(1)}, u32[]{:S(2)}, u32[]{:S(2)}) collective-permute-start(bf16[4,144,128]{2,1,0:T(8,128)(2,1)S(1)} %get-tuple-element.105), channel_id=1, source_target_pairs={{0,2},{1,3},{2,0},{3,1},{4,6},{5,7},{6,4},{7,5},{8,10},{9,11},{10,... | collective-permute-start | bytes 442376 | tf_op jit(solution)/shard_map/ppermute | solution.py:689
  33.2 6.4 %collective-permute-start.9 = (bf16[4,144,128]{2,1,0:T(8,128)(2,1)S(1)}, bf16[4,144,128]{2,1,0:T(8,128)(2,1)S(1)}, u32[]{:S(2)}, u32[]{:S(2)}) collective-permute-start(bf16[4,144,128]{2,1,0:T(8,128)(2,1)S(1)} %get-tuple-element.106), channel_id=1, source_target_pairs={{0,3},{1,0},{2,1},{3,2},{4,7},{5,4},{6,5},{7,6},{8,11},{9,8},{10,9... | collective-permute-start | bytes 442376 | tf_op jit(solution)/shard_map/ppermute | solution.py:689
  40.6 7.8 %collective-permute-start.10 = (f32[3,1280]{1,0:T(4,128)S(1)}, f32[3,1280]{1,0:T(4,128)S(1)}, u32[]{:S(2)}, u32[]{:S(2)}) collective-permute-start(f32[3,1280]{1,0:T(4,128)S(1)} %get-tuple-element.132), channel_id=1, source_target_pairs={{1,0},{2,1},{3,2},{4,3},{5,4},{6,5},{7,6},{8,7},{9,8},{10,9},{11,1... | collective-permute-start | bytes 46088 | tf_op jit(solution)/shard_map/ppermute | solution.py:785
